TPU v7x, 32 devices: a whole 2x2x4 slice. The times are simulated.
32 devices in a mesh: groups: 2 (over y), row: 4 (over z), col: 2 (over x), layer: 2 (over core).
Axes of the slice: x: 2, y: 2, z: 4, core: 2. Of those that a mesh axis runs over, the one named last changes fastest.
Arguments:
- a_tiles: bfloat16 [8, 2, 2, 8, 8, 128, 128], P(('groups', 'row'), 'col', None, None, 'layer'), parts along dimension 0, may hold values from -6 to 6
- a_offsets: int32 [8, 2, 2, 8, 8], P(('groups', 'row'), 'col', None, None, 'layer'), parts along dimension 0, may hold values from -2 to 2
- atom_owner: int32 [128], P(('groups', 'row', 'col')), parts along dimension 0, may hold values from 0 to 1, as said below
- b_tiles: bfloat16 [128, 12, 128, 128], P(('groups', 'row', 'col'), 'layer'), parts along dimension 0, may hold values from -0.5 to 0.5
- b_offsets: int32 [128, 12], P('groups'), parts along dimension 0, may hold values from -2 to 2
- c_offsets: int32 [128, 8], P(('groups', 'row', 'col')), parts along dimension 0, may hold values from -4 to 4
- block_sizes: int32 [128], P('groups'), parts along dimension 0, may hold values from 64 to 128
Outputs:
- c_tiles: bfloat16 [128, 8, 128, 128], P(('groups', 'row', 'col'), 'layer'), parts along dimension 0
There are 2 independent parts, one for each index of `groups`. A program takes and returns all parts, laid end to end along the dimension named above; each array names one. Nothing has to cross between parts.
Inputs may be any that keep to these rules, and one draw needn't show every extreme that they name: `atom_owner`: in the atoms of one device (aligned blocks of 8 atoms) no owner holds more than 8 atoms, and some owner holds exactly 8.
All inputs are finite; a program needn't handle non-finite values.
Results may differ from a plain program's by a relative error of at most 0.001.
Values may be sent and summed in bfloat16 or wider, within the bound.
No kernel may reach another device: no remote copies, remote signals or barrier semaphores. Data moves between devices by JAX's collectives and lax.ppermute only.
A program may use at most 64 MiB of HBM per device.

v0:
```python
import jax
import jax.numpy as jnp
from jax import lax
from jax.sharding import PartitionSpec as P

BAND = 2


def with_halo(cells, sides, width):
    for axis, dim in sides:
        count = lax.axis_size(axis)
        head = lax.slice_in_dim(cells, 0, width, axis=dim)
        tail = lax.slice_in_dim(cells, cells.shape[dim] - width, cells.shape[dim], axis=dim)
        cells = jnp.concatenate(
            [
                lax.ppermute(tail, axis, [(i, (i + 1) % count) for i in range(count)]),
                cells,
                lax.ppermute(head, axis, [((i + 1) % count, i) for i in range(count)]),
            ],
            axis=dim,
        )
    return cells


def local(a_tiles, a_offsets, atom_owner, b_tiles, b_offsets, c_offsets, block_sizes):
    band_width = BAND
    window_rows = 2 * band_width + 1
    cycle_size = lax.axis_size("row") * lax.axis_size("col")
    atom_count = atom_owner.shape[0]
    blocks_total = atom_count * cycle_size
    tile_width = a_tiles.shape[-1]
    bucket_size = a_tiles.shape[3]
    start_atom = (lax.axis_index("row") * lax.axis_size("col") + lax.axis_index("col")) * atom_count
    received, shifts = (
        lax.all_to_all(a_tiles, "col", split_axis=2, concat_axis=1, tiled=True),
        lax.all_to_all(a_offsets, "col", split_axis=2, concat_axis=1, tiled=True),
    )
    half_slots = a_tiles.shape[4]
    received = received.reshape(-1, half_slots, tile_width, tile_width)
    shifts = shifts.reshape(-1, half_slots)
    incoming = received.shape[0]
    places = jnp.arange(atom_count, dtype=jnp.int32)
    same_owner = atom_owner[:, None] == atom_owner[None, :]
    earlier = places[None, :] < places[:, None]
    owner_rank = jnp.sum(same_owner & earlier, axis=1)
    source = atom_owner * bucket_size + owner_rank
    selector = (source[:, None] == jnp.arange(incoming, dtype=jnp.int32)[None, :]).astype(
        jnp.bfloat16
    )
    a_rows = jnp.einsum(
        "pq,qsab->psab", selector, received, preferred_element_type=jnp.float32
    ).astype(jnp.bfloat16)
    a_shift = jnp.take(shifts, source, axis=0)
    b_local = lax.all_gather(b_tiles, "layer", axis=1, tiled=True)
    banded = with_halo(b_local, ((("row", "col"), 0),), band_width)
    band_rows = (
        start_atom - band_width + jnp.arange(atom_count + 2 * band_width, dtype=jnp.int32)
    ) % blocks_total
    band_cols = (band_rows[:, None] + jnp.take(b_offsets, band_rows, axis=0)) % blocks_total
    row_iota = lax.broadcasted_iota(jnp.int32, (tile_width, tile_width), 0)
    col_iota = lax.broadcasted_iota(jnp.int32, (tile_width, tile_width), 1)
    outer_sizes = jnp.take(block_sizes, band_cols)
    masked_b = jnp.where(col_iota < outer_sizes[:, :, None, None], banded, jnp.zeros_like(banded))
    own_atoms = start_atom + places
    contracted = (own_atoms[:, None] + a_shift) % blocks_total
    band_slot = places[:, None] + band_width + a_shift
    row_sizes = jnp.take(block_sizes, own_atoms)
    inner_sizes = jnp.take(block_sizes, contracted)
    keep_a = (row_iota < row_sizes[:, None, None, None]) & (
        col_iota < inner_sizes[:, :, None, None]
    )
    masked_a = jnp.where(keep_a, a_rows, jnp.zeros_like(a_rows))
    c_cols = (own_atoms[:, None] + c_offsets) % blocks_total
    window_iota = jnp.arange(window_rows, dtype=jnp.int32)

    def per_atom(items):
        tiles_row, shift_row, slots_row, wanted, place = items
        window = lax.dynamic_slice_in_dim(masked_b, place, window_rows, 0)
        pick = (shift_row[:, None] + band_width == window_iota[None, :]).astype(jnp.bfloat16)
        picked = jnp.einsum(
            "tw,wubc->tubc", pick, window, preferred_element_type=jnp.float32
        ).astype(jnp.bfloat16)
        reached = jnp.take(band_cols, slots_row, axis=0)
        matches = (wanted[:, None, None] == reached[None]).astype(jnp.float32)
        products = jnp.einsum(
            "tab,tubc->tuac", tiles_row, picked, preferred_element_type=jnp.float32
        )
        return jnp.einsum("stu,tuac->sac", matches, products, precision=lax.Precision.HIGHEST)

    partial_tiles = lax.map(per_atom, (masked_a, a_shift, band_slot, c_cols, places))
    summed = lax.psum_scatter(partial_tiles, "layer", scatter_dimension=1, tiled=True)
    return summed.astype(jnp.bfloat16)


def solution(mesh):
    placed = (
        P(("groups", "row"), "col", None, None, "layer", None, None),
        P(("groups", "row"), "col", None, None, "layer"),
        P(("groups", "row", "col")),
        P(("groups", "row", "col"), "layer", None, None),
        P("groups", None),
        P(("groups", "row", "col"), None),
        P("groups"),
    )
    return jax.shard_map(
        local,
        mesh=mesh,
        in_specs=placed,
        out_specs=P(("groups", "row", "col"), "layer", None, None),
        check_vma=False,
    )
```

profile of v0, /device:TPU:0, one launch (start us, length us, event | category | flops | bytes accessed | tf_op | source)
XLA Modules:
  0.0 243.9 jit_solution(7517590144286635658)
XLA Ops:
  6.5 2.8 %copy.64 = bf16[8,6,128,128]{3,2,0,1:T(8,128)(2,1)} copy(bf16[8,6,128,128]{3,2,1,0:T(8,128)(2,1)} %param.12) | data formatting | bytes 3145728 | tf_op args[3]
  9.3 4.2 %all-to-all-start = ((s32[1,1,2,8,4]{3,4,1,0,2:T(4,128)}), s32[1,1,2,8,4]{3,4,1,0,2:T(4,128)S(1)}, u32[]{:S(2)}, u32[]{:S(2)}) async-start(s32[1,1,2,8,4]{3,4,1,0,2:T(4,128)} %bitcast), calls=%async_computation | async-start | bytes 8192 | tf_op jit(solution)/shard_map/all_to_all | solution.py:36
  18.7 4.9 %all-to-all-start.1 = ((bf16[1,1,2,8,4,128,128]{6,5,4,3,1,0,2:T(8,128)(2,1)}), bf16[1,1,2,8,4,128,128]{6,5,4,3,1,0,2:T(8,128)(2,1)}, u32[]{:S(2)}, u32[]{:S(2)}) async-start(bf16[1,1,2,8,4,128,128]{6,5,4,3,1,0,2:T(8,128)(2,1)} %bitcast.8), calls=%async_computation.1 | async-start | bytes 4194304 | tf_op jit(solution)/shard_map/all_to_all | solution.py:35
  24.5 2.7 %fusion.48 = (bf16[2,12,128,128]{3,2,0,1:T(8,128)(2,1)}, bf16[2,12,128,128]{3,2,0,1:T(8,128)(2,1)}) fusion(bf16[8,12,128,128]{3,2,0,1:T(8,128)(2,1)} %all-gather.2.cloned.1.call-done), kind=kLoop, calls=%fused_computation.112 | loop fusion | bytes 3145728 | tf_op jit(solution)/shard_map/slice | solution.py:13
  27.3 2.0 collective-permute-start
  29.3 3.6 %collective-permute-start.1 = (bf16[2,12,128,128]{3,2,0,1:T(8,128)(2,1)}, bf16[2,12,128,128]{3,2,0,1:T(8,128)(2,1)}, u32[]{:S(2)}, u32[]{:S(2)}) collective-permute-start(bf16[2,12,128,128]{3,2,0,1:T(8,128)(2,1)} %get-tuple-element.148), channel_id=1, source_target_pairs={{2,0},{4,2},{6,4},{8,6},{10,8},{12,10},{14,12},{0,14},{3,1},{5,3},... | collective-permute-start | bytes 2359304 | tf_op jit(solution)/shard_map/ppermute | solution.py:18
  33.9 32.9 %all-to-all-done.1 = bf16[1,1,2,8,4,128,128]{6,5,4,3,1,0,2:T(8,128)(2,1)} async-done(((bf16[1,1,2,8,4,128,128]{6,5,4,3,1,0,2:T(8,128)(2,1)}), bf16[1,1,2,8,4,128,128]{6,5,4,3,1,0,2:T(8,128)(2,1)}, u32[]{:S(2)}, u32[]{:S(2)}) %all-to-all-start.1) | async-done | bytes 2097184 | tf_op jit(solution)/shard_map/all_to_all | solution.py:35
  66.8 3.0 %fusion.27 = bf16[8,4,128,128]{3,0,2,1:T(8,128)(2,1)S(1)} fusion(bf16[1,1,2,8,4,128,128]{6,5,4,3,1,0,2:T(8,128)(2,1)} %all-to-all-done.1, s32[8,4]{0,1:T(4,128)S(1)} %copy.67, pred[8,128,128]{2,0,1:T(8,128)(4,1)S(1)} %iota_compare_fusion.3, s32[8]{0:T(128)S(1)} %get-tuple-element.146), kind=kOutput, calls=%fused_computation.45 | convolution fusion | flops 18874496 | bytes 3276960 | tf_op jit(solution)/shard_map/pq,qsab->psab/dot_general | solution.py:50
  71.0 9.1 %collective-permute-done = bf16[2,12,128,128]{3,2,0,1:T(8,128)(2,1)} collective-permute-done((bf16[2,12,128,128]{3,2,0,1:T(8,128)(2,1)}, bf16[2,12,128,128]{3,2,0,1:T(8,128)(2,1)}, u32[]{:S(2)}, u32[]{:S(2)}) %collective-permute-start) | collective-permute-done | bytes 786464 | tf_op jit(solution)/shard_map/ppermute | solution.py:16
  80.1 2.7 %collective-permute-done.1 = bf16[2,12,128,128]{3,2,0,1:T(8,128)(2,1)} collective-permute-done((bf16[2,12,128,128]{3,2,0,1:T(8,128)(2,1)}, bf16[2,12,128,128]{3,2,0,1:T(8,128)(2,1)}, u32[]{:S(2)}, u32[]{:S(2)}) %collective-permute-start.1) | collective-permute-done | bytes 786464 | tf_op jit(solution)/shard_map/ppermute | solution.py:18
  82.8 4.4 %fusion.22 = bf16[12,12,128,128]{3,2,0,1:T(8,128)(2,1)} fusion(bf16[2,12,128,128]{3,2,0,1:T(8,128)(2,1)} %collective-permute-done.1, bf16[8,12,128,128]{3,2,0,1:T(8,128)(2,1)S(1)} %copy-done.1, bf16[2,12,128,128]{3,2,0,1:T(8,128)(2,1)} %collective-permute-done, s32[12,12]{0,1:T(8,128)S(1)} %copy.63), kind=kLoop, calls=%fused_computation.38 | loop fusion | flops 18874368 | bytes 9437760 | tf_op jit(solution)/shard_map/jit(_where)/select_n | solution.py:63
  87.2 133.8 %while.11 = (s32[]{:T(128)}, f32[8,8,128,128]{3,2,1,0:T(8,128)}, s32[8,8]{1,0:T(8,128)S(1)}, s32[8,4]{1,0:T(8,128)S(1)}, s32[12,12]{1,0:T(8,128)S(1)}, /*index=5...) while((s32[]{:T(128)}, f32[8,8,128,128]{3,2,1,0:T(8,128)}, ...), condition=%wide.region_2.3_spmd.clone, body=%wide.region_1.2_spmd.clone.sunk | while | flops 285476352 | bytes 23337312 | solution.py:90
  89.7 1.7 constant_dynamic-slice_fusion.5
  94.6 3.4 %copy.106 = f32[4,12,128,128]{3,1,0,2:T(8,128)} copy(f32[4,12,128,128]{2,3,1,0:T(8,128)S(1)} %convolution_bitcast_fusion.4) | data formatting | bytes 6291456 | tf_op jit(solution)/shard_map/while/body/eval_jaxpr/tab,tubc->tuac/transpose | solution.py:85
  98.7 4.4 %convolution_bitcast_fusion.5 = f32[1,8,128,128]{3,1,2,0:T(8,128)S(1)} fusion(f32[4,12,128,128]{3,1,0,2:T(8,128)} %copy.106, s32[4,12]{1,0:T(4,128)S(1)} %broadcast_select_fusion.4, s32[8]{0:T(128)S(1)} %fusion.69), kind=kOutput, calls=%fused_computation.12.clone.1 | convolution fusion | flops 75497856 | bytes 3670240 | tf_op jit(solution)/shard_map/while/body/eval_jaxpr/stu,tuac->sac/dot_general | solution.py:88
  106.4 1.7 constant_dynamic-slice_fusion.5
  111.3 3.4 %copy.106 = f32[4,12,128,128]{3,1,0,2:T(8,128)} copy(f32[4,12,128,128]{2,3,1,0:T(8,128)S(1)} %convolution_bitcast_fusion.4) | data formatting | bytes 6291456 | tf_op jit(solution)/shard_map/while/body/eval_jaxpr/tab,tubc->tuac/transpose | solution.py:85
  115.4 4.4 %convolution_bitcast_fusion.5 = f32[1,8,128,128]{3,1,2,0:T(8,128)S(1)} fusion(f32[4,12,128,128]{3,1,0,2:T(8,128)} %copy.106, s32[4,12]{1,0:T(4,128)S(1)} %broadcast_select_fusion.4, s32[8]{0:T(128)S(1)} %fusion.69), kind=kOutput, calls=%fused_computation.12.clone.1 | convolution fusion | flops 75497856 | bytes 3670240 | tf_op jit(solution)/shard_map/while/body/eval_jaxpr/stu,tuac->sac/dot_general | solution.py:88
  128.0 3.4 %copy.106 = f32[4,12,128,128]{3,1,0,2:T(8,128)} copy(f32[4,12,128,128]{2,3,1,0:T(8,128)S(1)} %convolution_bitcast_fusion.4) | data formatting | bytes 6291456 | tf_op jit(solution)/shard_map/while/body/eval_jaxpr/tab,tubc->tuac/transpose | solution.py:85
  132.2 4.4 %convolution_bitcast_fusion.5 = f32[1,8,128,128]{3,1,2,0:T(8,128)S(1)} fusion(f32[4,12,128,128]{3,1,0,2:T(8,128)} %copy.106, s32[4,12]{1,0:T(4,128)S(1)} %broadcast_select_fusion.4, s32[8]{0:T(128)S(1)} %fusion.69), kind=kOutput, calls=%fused_computation.12.clone.1 | convolution fusion | flops 75497856 | bytes 3670240 | tf_op jit(solution)/shard_map/while/body/eval_jaxpr/stu,tuac->sac/dot_general | solution.py:88
  144.8 3.4 %copy.106 = f32[4,12,128,128]{3,1,0,2:T(8,128)} copy(f32[4,12,128,128]{2,3,1,0:T(8,128)S(1)} %convolution_bitcast_fusion.4) | data formatting | bytes 6291456 | tf_op jit(solution)/shard_map/while/body/eval_jaxpr/tab,tubc->tuac/transpose | solution.py:85
  148.9 4.4 %convolution_bitcast_fusion.5 = f32[1,8,128,128]{3,1,2,0:T(8,128)S(1)} fusion(f32[4,12,128,128]{3,1,0,2:T(8,128)} %copy.106, s32[4,12]{1,0:T(4,128)S(1)} %broadcast_select_fusion.4, s32[8]{0:T(128)S(1)} %fusion.69), kind=kOutput, calls=%fused_computation.12.clone.1 | convolution fusion | flops 75497856 | bytes 3670240 | tf_op jit(solution)/shard_map/while/body/eval_jaxpr/stu,tuac->sac/dot_general | solution.py:88
  161.5 3.4 %copy.106 = f32[4,12,128,128]{3,1,0,2:T(8,128)} copy(f32[4,12,128,128]{2,3,1,0:T(8,128)S(1)} %convolution_bitcast_fusion.4) | data formatting | bytes 6291456 | tf_op jit(solution)/shard_map/while/body/eval_jaxpr/tab,tubc->tuac/transpose | solution.py:85
  165.6 4.4 %convolution_bitcast_fusion.5 = f32[1,8,128,128]{3,1,2,0:T(8,128)S(1)} fusion(f32[4,12,128,128]{3,1,0,2:T(8,128)} %copy.106, s32[4,12]{1,0:T(4,128)S(1)} %broadcast_select_fusion.4, s32[8]{0:T(128)S(1)} %fusion.69), kind=kOutput, calls=%fused_computation.12.clone.1 | convolution fusion | flops 75497856 | bytes 3670240 | tf_op jit(solution)/shard_map/while/body/eval_jaxpr/stu,tuac->sac/dot_general | solution.py:88
  178.2 3.4 %copy.106 = f32[4,12,128,128]{3,1,0,2:T(8,128)} copy(f32[4,12,128,128]{2,3,1,0:T(8,128)S(1)} %convolution_bitcast_fusion.4) | data formatting | bytes 6291456 | tf_op jit(solution)/shard_map/while/body/eval_jaxpr/tab,tubc->tuac/transpose | solution.py:85
  182.3 4.4 %convolution_bitcast_fusion.5 = f32[1,8,128,128]{3,1,2,0:T(8,128)S(1)} fusion(f32[4,12,128,128]{3,1,0,2:T(8,128)} %copy.106, s32[4,12]{1,0:T(4,128)S(1)} %broadcast_select_fusion.4, s32[8]{0:T(128)S(1)} %fusion.69), kind=kOutput, calls=%fused_computation.12.clone.1 | convolution fusion | flops 75497856 | bytes 3670240 | tf_op jit(solution)/shard_map/while/body/eval_jaxpr/stu,tuac->sac/dot_general | solution.py:88
  194.9 3.4 %copy.106 = f32[4,12,128,128]{3,1,0,2:T(8,128)} copy(f32[4,12,128,128]{2,3,1,0:T(8,128)S(1)} %convolution_bitcast_fusion.4) | data formatting | bytes 6291456 | tf_op jit(solution)/shard_map/while/body/eval_jaxpr/tab,tubc->tuac/transpose | solution.py:85
  199.0 4.4 %convolution_bitcast_fusion.5 = f32[1,8,128,128]{3,1,2,0:T(8,128)S(1)} fusion(f32[4,12,128,128]{3,1,0,2:T(8,128)} %copy.106, s32[4,12]{1,0:T(4,128)S(1)} %broadcast_select_fusion.4, s32[8]{0:T(128)S(1)} %fusion.69), kind=kOutput, calls=%fused_computation.12.clone.1 | convolution fusion | flops 75497856 | bytes 3670240 | tf_op jit(solution)/shard_map/while/body/eval_jaxpr/stu,tuac->sac/dot_general | solution.py:88
  206.8 1.7 constant_dynamic-slice_fusion.5
  211.7 3.4 %copy.106 = f32[4,12,128,128]{3,1,0,2:T(8,128)} copy(f32[4,12,128,128]{2,3,1,0:T(8,128)S(1)} %convolution_bitcast_fusion.4) | data formatting | bytes 6291456 | tf_op jit(solution)/shard_map/while/body/eval_jaxpr/tab,tubc->tuac/transpose | solution.py:85
  215.8 4.4 %convolution_bitcast_fusion.5 = f32[1,8,128,128]{3,1,2,0:T(8,128)S(1)} fusion(f32[4,12,128,128]{3,1,0,2:T(8,128)} %copy.106, s32[4,12]{1,0:T(4,128)S(1)} %broadcast_select_fusion.4, s32[8]{0:T(128)S(1)} %fusion.69), kind=kOutput, calls=%fused_computation.12.clone.1 | convolution fusion | flops 75497856 | bytes 3670240 | tf_op jit(solution)/shard_map/while/body/eval_jaxpr/stu,tuac->sac/dot_general | solution.py:88
  221.1 14.9 %all-reduce.2 = bf16[8,8,128,128]{3,2,1,0:T(8,128)(2,1)S(1)} all-reduce(f32[8,8,128,128]{3,2,1,0:T(8,128)} %get-tuple-element.57), channel_id=2, replica_groups=mesh['groups'=2,'row'=4,'col'=2,'layer'=2] {'layer'}, use_global_device_ids=true, to_apply=%region_3.4.clone | all-reduce | flops 1048576 | bytes 6291456
  (151 shorter events, 59.8 us)
Async XLA Ops:
  6.5 7.9 %copy-start = (s32[64]{0:T(128)S(1)}, s32[64]{0:T(128)}, u32[]{:S(2)}) copy-start(s32[64]{0:T(128)} %param.15) | copy-start | bytes 772
  6.5 7.0 %copy-start.2 = (s32[64,12]{0,1:T(8,128)S(1)}, s32[64,12]{0,1:T(8,128)}, u32[]{:S(2)}) copy-start(s32[64,12]{0,1:T(8,128)} %param.13) | copy-start | bytes 9220
  6.5 18.0 %all-gather.2.cloned.1.call-start = ((), (), s32[]{:S(2)}) async-start(), calls=%async_computation.2 | async-start | bytes 4718592 | tf_op jit(solution)/shard_map/all_gather | solution.py:54
  9.3 9.4 %all-to-all-start = ((s32[1,1,2,8,4]{3,4,1,0,2:T(4,128)}), s32[1,1,2,8,4]{3,4,1,0,2:T(4,128)S(1)}, u32[]{:S(2)}, u32[]{:S(2)}) async-start(s32[1,1,2,8,4]{3,4,1,0,2:T(4,128)} %bitcast), calls=%async_computation | async-start | bytes 8192 | tf_op jit(solution)/shard_map/all_to_all | solution.py:36
  14.5 2.5 %copy-start.5 = (u32[32]{0:T(128)S(1)}, u32[32]{0:T(128)}, u32[]{:S(2)}) copy-start(u32[32]{0:T(128)} %constant.173) | copy-start | bytes 388
  14.5 3.1 %copy-start.4 = (s32[8]{0:T(128)S(1)}, s32[8]{0:T(128)}, u32[]{:S(2)}) copy-start(s32[8]{0:T(128)} %param.11) | copy-start | bytes 100
  14.5 3.3 %copy-start.3 = (s32[8,8]{1,0:T(8,128)S(1)}, s32[8,8]{1,0:T(8,128)}, u32[]{:S(2)}) copy-start(s32[8,8]{1,0:T(8,128)} %param.14) | copy-start | bytes 772
  18.7 48.1 %all-to-all-start.1 = ((bf16[1,1,2,8,4,128,128]{6,5,4,3,1,0,2:T(8,128)(2,1)}), bf16[1,1,2,8,4,128,128]{6,5,4,3,1,0,2:T(8,128)(2,1)}, u32[]{:S(2)}, u32[]{:S(2)}) async-start(bf16[1,1,2,8,4,128,128]{6,5,4,3,1,0,2:T(8,128)(2,1)} %bitcast.8), calls=%async_computation.1 | async-start | bytes 4194304 | tf_op jit(solution)/shard_map/all_to_all | solution.py:35
  27.3 52.9 %collective-permute-start = (bf16[2,12,128,128]{3,2,0,1:T(8,128)(2,1)}, bf16[2,12,128,128]{3,2,0,1:T(8,128)(2,1)}, u32[]{:S(2)}, u32[]{:S(2)}) collective-permute-start(bf16[2,12,128,128]{3,2,0,1:T(8,128)(2,1)} %get-tuple-element.147), channel_id=1, source_target_pairs={{0,2},{2,4},{4,6},{6,8},{8,10},{10,12},{12,14},{14,0},{1,3},{3,5},... | collective-permute-start | bytes 2359304 | tf_op jit(solution)/shard_map/ppermute | solution.py:16
  29.3 53.6 %collective-permute-start.1 = (bf16[2,12,128,128]{3,2,0,1:T(8,128)(2,1)}, bf16[2,12,128,128]{3,2,0,1:T(8,128)(2,1)}, u32[]{:S(2)}, u32[]{:S(2)}) collective-permute-start(bf16[2,12,128,128]{3,2,0,1:T(8,128)(2,1)} %get-tuple-element.148), channel_id=1, source_target_pairs={{2,0},{4,2},{6,4},{8,6},{10,8},{12,10},{14,12},{0,14},{3,1},{5,3},... | collective-permute-start | bytes 2359304 | tf_op jit(solution)/shard_map/ppermute | solution.py:18
  33.9 49.0 %copy-start.1 = (bf16[8,12,128,128]{3,2,0,1:T(8,128)(2,1)S(1)}, bf16[8,12,128,128]{3,2,0,1:T(8,128)(2,1)}, u32[]{:S(2)}) copy-start(bf16[8,12,128,128]{3,2,0,1:T(8,128)(2,1)} %all-gather.2.cloned.1.call-done) | copy-start | bytes 9437188
Sparse Core Ops, SparseCore 0:
  9.4 14.8 all-gather.1
where the time goes:
time: 245 us; the launch traced here: 244 us
  local copies, waits for them, and re-layouts  70.6 us (29%)
  matrix products  63.4 us (26%)
  waiting for transfers between devices  44.8 us (18%)
  loops' own time  15.2 us (6%)
  blocking collectives  14.9 us (6%)
  starting transfers between devices  14.7 us (6%)
  between operations  14.2 us (6%)
  other arithmetic  6.13 us (3%)
    dot_general x8, matrix products, per_atom(): jnp.einsum('stu,tuac->sac', matches, products, precision=lax.Precision.HI...  35 us
    all_to_all x1, waiting for transfers between devices, local(): lax.all_to_all(a_tiles, 'col', split_axis=2, concat_axis=1, tiled=True)  32.9 us
    transpose x8, local copies, waits for them, and re-layouts, per_atom(): jnp.einsum('tab,tubc->tuac', tiles_row, picked, preferred_element_type=jn...  27.4 us
    another operation x1, loops' own time, local(): lax.map(per_atom, (masked_a, a_shift, band_slot, c_cols, places))  15.2 us
    unnamed x1, blocking collectives  14.9 us
    dynamic_slice x8, local copies, waits for them, and re-layouts, per_atom(): window = lax.dynamic_slice_in_dim(masked_b, place, window_rows, 0)  13.5 us
    dot_general x8, matrix products, per_atom(): jnp.einsum('tab,tubc->tuac', tiles_row, picked, preferred_element_type=jn...  13 us
    dot_general x8, matrix products, per_atom(): jnp.einsum('tw,wubc->tubc', pick, window, preferred_element_type=jnp.floa...  12.4 us
  transfers between devices with their start and end apart: 5, of which 3 were waited for; matrix products, arithmetic and copies ran while one was open for 5% of the time, Pallas kernels for 0%

commit v1 on v0

v1 whole, which is shorter than its diff:
```python
import functools

import jax
import jax.numpy as jnp
from jax import lax
from jax.experimental import pallas as pl
from jax.experimental.pallas import tpu as pltpu
from jax.sharding import PartitionSpec as P

BAND = 2
WIDTH = 2 * BAND + 1
SMEM = pl.BlockSpec(memory_space=pltpu.SMEM)
VMEM = pl.BlockSpec(memory_space=pltpu.VMEM)
HBM = pl.BlockSpec(memory_space=pl.ANY)


def band_kernel(pos, b_offsets, sizes, b_own, b_peer, table, tail, head, total):
    atoms, half, tile, _ = b_own.shape
    blocks = sizes.shape[0]
    start, layer = pos[0], pos[1]
    row_iota = lax.broadcasted_iota(jnp.int32, (tile, tile), 0)
    col_iota = lax.broadcasted_iota(jnp.int32, (tile, tile), 1)

    def one_row(k, _):
        for w in range(WIDTH):
            total[w] = jnp.zeros((tile, tile), jnp.float32)
        for part, ref in ((layer, b_own), (1 - layer, b_peer)):
            for j in range(half):
                w = b_offsets[k, part * half + j] + BAND
                total[w] = total[w] + ref[k, j].astype(jnp.float32)
        rows = sizes[start + k]
        for w in range(WIDTH):
            cols = sizes[lax.rem(start + k + w + blocks - BAND, blocks)]
            value = jnp.where((row_iota < rows) & (col_iota < cols), total[w], 0.0)
            high = value.astype(jnp.bfloat16)
            low = (value - high.astype(jnp.float32)).astype(jnp.bfloat16)
            table[k * WIDTH + w, 0:tile] = high
            table[k * WIDTH + w, tile : 2 * tile] = low
        return 0

    lax.fori_loop(0, atoms, one_row, 0)
    tail[...] = table[pl.ds((atoms - BAND + layer) * WIDTH, WIDTH)]
    head[...] = table[pl.ds(layer * WIDTH, WIDTH)]


def band_sums(pos, b_offsets, sizes, b_own, b_peer):
    atoms, half, tile, _ = b_own.shape
    shape = lambda rows: jax.ShapeDtypeStruct((rows * WIDTH, 2 * tile, tile), jnp.bfloat16)
    return pl.pallas_call(
        band_kernel,
        out_shape=(shape(atoms), shape(1), shape(1)),
        in_specs=[SMEM, SMEM, SMEM, VMEM, VMEM],
        out_specs=(VMEM, VMEM, VMEM),
        scratch_shapes=[pltpu.VMEM((WIDTH, tile, tile), jnp.float32)],
        compiler_params=pltpu.CompilerParams(vmem_limit_bytes=24 * 2**20),
        cost_estimate=pl.CostEstimate(flops=10**7, bytes_accessed=8 * 2**20, transcendentals=0),
        name="band_sums",
    )(pos, b_offsets, sizes, b_own, b_peer)


def product_kernel(runs, n_src, n_halo, dest, aliased, atoms, *refs):
    refs = list(refs)
    pos, owner, c_offsets, sizes = refs[:4]
    del refs[:4]
    shifts = [(refs[2 * i], refs[2 * i + 1]) for i in range(n_src)]
    del refs[: 2 * n_src]
    local = refs[:2]
    del refs[:2]
    n_chunks = max(r[2] for r in runs) + 1 if n_src == 2 else 0
    chunks = [(refs[2 * i], refs[2 * i + 1]) for i in range(n_chunks)]
    del refs[: 2 * n_chunks]
    table = refs.pop(0)
    halo = refs[:n_halo]
    del refs[:n_halo]
    if aliased:
        refs.pop(0)
    out, a_v, t_v, o_v, a_sem, t_sem, o_sem = refs
    start, layer, me = pos[0], pos[1], pos[2]
    d = me if dest is None else dest
    half = shifts[0][0].shape[-1]
    slots = o_v.shape[1]
    tile = o_v.shape[2]
    mine = owner[0] == me if n_src == 2 else None
    zero_at = (atoms + 2 * BAND) * WIDTH

    first = min(r[0] for r in runs)
    last = max(r[0] + r[1] for r in runs) + 2 * BAND
    if n_halo:
        first, last = 0, atoms + 2 * BAND
    low, high = max(first, BAND), min(last, atoms + BAND)
    fills = [
        pltpu.make_async_copy(
            table.at[pl.ds((low - BAND) * WIDTH, (high - low) * WIDTH)],
            t_v.at[pl.ds(low * WIDTH, (high - low) * WIDTH)],
            t_sem.at[0],
        )
    ]
    if n_halo:
        places = (layer, 1 - layer, atoms + BAND + layer, atoms + BAND + 1 - layer)
        for i, (ref, place) in enumerate(zip(halo, places, strict=True)):
            fills.append(
                pltpu.make_async_copy(ref, t_v.at[pl.ds(place * WIDTH, WIDTH)], t_sem.at[1 + i])
            )
    base = 0
    for p0, count, chunk, at in runs:

        def fetch(n, _, p0=p0, chunk=chunk, at=at, base=base):
            def begin(src):
                for h in range(2):
                    pltpu.make_async_copy(
                        src[h], a_v.at[base + n, pl.ds(h * half, half)], a_sem.at[base + n, h]
                    ).start()

            here = (local[0].at[0, 0, d, p0 + n], local[1].at[p0 + n])
            if n_src == 2:
                pl.when(mine)(lambda: begin(here))
                pl.when(jnp.logical_not(mine))(
                    lambda: begin((chunks[chunk][0].at[at + n], chunks[chunk][1].at[at + n]))
                )
            else:
                begin(here)
            return 0

        lax.fori_loop(0, count, fetch, 0)
        base += count
    for fill in fills:
        fill.start()
    t_v[zero_at] = jnp.zeros(t_v.shape[1:], t_v.dtype)
    for fill in fills:
        fill.wait()
    row_iota = lax.broadcasted_iota(jnp.int32, (tile, slots * tile // 2), 0)
    base = 0
    for p0, count, _, _ in runs:

        def one_atom(n, _, p0=p0, base=base):
            p = p0 + n
            for h in range(2):
                pltpu.make_async_copy(
                    local[1].at[p], a_v.at[base + n, pl.ds(h * half, half)], a_sem.at[base + n, h]
                ).wait()
            reach = []
            for h in range(2):
                for t in range(half):
                    if n_src == 2:
                        shift = jnp.where(
                            mine, shifts[0][h][0, 0, d, p, t], shifts[1][h][0, 0, d, p, t]
                        )
                    else:
                        shift = shifts[0][h][0, 0, d, p, t]
                    reach.append(shift)
            wanted = [c_offsets[p, layer * slots + s] for s in range(slots)]
            size = sizes[start + p]

            def place(t, s):
                w = wanted[s] - reach[t] + BAND
                at = (p + BAND + reach[t]) * WIDTH + w
                return jnp.where((w >= 0) & (w < WIDTH), at, zero_at)

            for pair in range(slots // 2):
                total = jnp.zeros((tile, 2 * tile), jnp.float32)
                for t in range(2 * half):
                    left = a_v[base + n, t]
                    left = jnp.concatenate([left, left], axis=1)
                    right = jnp.concatenate(
                        [t_v[place(t, 2 * pair)], t_v[place(t, 2 * pair + 1)]], axis=1
                    )
                    total += jnp.dot(left, right, preferred_element_type=jnp.float32)
                total = jnp.where(row_iota < size, total, 0.0).astype(jnp.bfloat16)
                o_v[base + n, 2 * pair] = total[:, :tile]
                o_v[base + n, 2 * pair + 1] = total[:, tile:]
            pltpu.make_async_copy(o_v.at[base + n], out.at[p], o_sem.at[base + n]).start()
            return 0

        lax.fori_loop(0, count, one_atom, 0)
        base += count
    base = 0
    for p0, count, _, _ in runs:

        def finish(n, _, p0=p0, base=base):
            pltpu.make_async_copy(o_v.at[base + n], out.at[p0 + n], o_sem.at[base + n]).wait()
            return 0

        lax.fori_loop(0, count, finish, 0)
        base += count


def products(runs, scalars, shifts, local, chunks, table, halo, slots, dest, prior):
    atoms = local[1].shape[0]
    _, half, tile, _ = local[1].shape
    count = sum(r[1] for r in runs)
    operands = list(scalars) + [s for pair in shifts for s in pair] + list(local)
    operands += [c for pair in chunks for c in pair] + [table] + list(halo)
    specs = [SMEM] * (4 + 2 * len(shifts)) + [HBM] * (len(operands) - 4 - 2 * len(shifts))
    aliases = {}
    if prior is not None:
        aliases = {len(operands): 0}
        operands.append(prior)
        specs.append(HBM)
    kernel = functools.partial(
        product_kernel, runs, len(shifts), len(halo), dest, prior is not None, atoms
    )
    return pl.pallas_call(
        kernel,
        out_shape=jax.ShapeDtypeStruct((atoms, slots, tile, tile), jnp.bfloat16),
        in_specs=specs,
        out_specs=HBM,
        scratch_shapes=[
            pltpu.VMEM((count, 2 * half, tile, tile), jnp.bfloat16),
            pltpu.VMEM(((atoms + 2 * BAND) * WIDTH + 1, 2 * tile, tile), jnp.bfloat16),
            pltpu.VMEM((count, slots, tile, tile), jnp.bfloat16),
            pltpu.SemaphoreType.DMA((count, 2)),
            pltpu.SemaphoreType.DMA((5,)),
            pltpu.SemaphoreType.DMA((count,)),
        ],
        input_output_aliases=aliases,
        compiler_params=pltpu.CompilerParams(vmem_limit_bytes=24 * 2**20),
        cost_estimate=pl.CostEstimate(
            flops=count * 2 * tile**3 * 4 * half * slots,
            bytes_accessed=4 * 2**20,
            transcendentals=0,
        ),
        name="products",
    )(*operands)


def local(a_tiles, a_offsets, atom_owner, b_tiles, b_offsets, c_offsets, block_sizes):
    cols = lax.axis_size("col")
    cycle = lax.axis_size("row") * cols
    atoms = atom_owner.shape[0]
    bucket = a_tiles.shape[3]
    slots = c_offsets.shape[1] // 2
    me = lax.axis_index("col")
    layer = lax.axis_index("layer")
    start = (lax.axis_index("row") * cols + me) * atoms
    pos = jnp.stack([start, layer, me]).astype(jnp.int32)
    assert atoms * cycle > 8 * BAND and lax.axis_size("layer") == 2 and atoms >= 2 * BAND

    def across(x):
        return lax.ppermute(x, "layer", [(0, 1), (1, 0)])

    def swap(x):
        return lax.ppermute(x, "col", [(0, 1), (1, 0)])

    def onward(x):
        return lax.ppermute(x, ("row", "col"), [(i, (i + 1) % cycle) for i in range(cycle)])

    def back(x):
        return lax.ppermute(x, ("row", "col"), [((i + 1) % cycle, i) for i in range(cycle)])

    whole = cols == 2 and bucket == atoms and atoms == 8
    if whole:
        def part(p0, count):
            at = (0, 0, 1 - me, p0, 0, 0, 0)
            size = (1, 1, 1, count) + a_tiles.shape[4:]
            return lax.dynamic_slice(a_tiles, at, size).reshape((count,) + a_tiles.shape[4:])

        far = [swap(part(0, 4)), swap(part(6, 2))]
    b_peer = across(b_tiles)
    own_rows = lax.dynamic_slice_in_dim(b_offsets, start, atoms, 0)
    table, tail, head = band_sums(pos, own_rows, block_sizes, b_tiles, b_peer)
    if whole:
        rest = part(4, 2)
        tail, head, rest = lax.optimization_barrier((tail, head, rest))
    tail, head = onward(tail), back(head)
    scalars = (pos, atom_owner, c_offsets, block_sizes)
    if whole:
        far.append(swap(rest))
        shifts = [a_offsets, swap(a_offsets)]
        shifts = [(s, across(s)) for s in shifts]
        near = lax.dynamic_index_in_dim(a_tiles[0, 0], me, 0, keepdims=False)
        held = (a_tiles, across(near))
        far = [(f, across(f)) for f in far]
        halo = (tail, across(tail), head, across(head))
        call = functools.partial(
            products, scalars=scalars, shifts=shifts, local=held, table=table, slots=slots
        )
        c = call([(2, 2, 0, 2)], chunks=far[:1], halo=(), dest=None, prior=None)
        c = call(
            [(0, 2, 0, 0), (6, 2, 1, 0)], chunks=far[:2], halo=halo, dest=None, prior=c
        )
        return call([(4, 2, 0, 0)], chunks=far[2:], halo=(), dest=None, prior=c)
    received = lax.all_to_all(a_tiles, "col", split_axis=2, concat_axis=1, tiled=True)
    moved = lax.all_to_all(a_offsets, "col", split_axis=2, concat_axis=1, tiled=True)
    received = received.reshape((-1,) + received.shape[4:])
    moved = moved.reshape((-1,) + moved.shape[4:])
    places = jnp.arange(atoms, dtype=jnp.int32)
    same = atom_owner[:, None] == atom_owner[None, :]
    rank = jnp.sum(same & (places[None, :] < places[:, None]), axis=1)
    source = atom_owner * bucket + rank
    rows = jnp.take(received, source, axis=0)
    shift = jnp.take(moved, source, axis=0)[None, None, None]
    halo = (tail, across(tail), head, across(head))
    return products(
        [(0, atoms, 0, 0)],
        scalars,
        [(shift, across(shift))],
        (rows[None, None, None], across(rows)),
        [],
        table,
        halo,
        slots,
        0,
        None,
    )


def solution(mesh):
    placed = (
        P(("groups", "row"), "col", None, None, "layer", None, None),
        P(("groups", "row"), "col", None, None, "layer"),
        P(("groups", "row", "col")),
        P(("groups", "row", "col"), "layer", None, None),
        P("groups", None),
        P(("groups", "row", "col"), None),
        P("groups"),
    )
    return jax.shard_map(
        local,
        mesh=mesh,
        in_specs=placed,
        out_specs=P(("groups", "row", "col"), "layer", None, None),
        check_vma=False,
    )
```

time: 245 us -> 61.2 us (0.25)
  local copies, waits for them, and re-layouts: 70.6 us -> 6.76 us
  matrix products: 63.4 us -> 0 us
  waiting for transfers between devices: 44.8 us -> 26.5 us
  Pallas kernels: 0 us -> 15.9 us
  loops' own time: 15.2 us -> 0 us
  blocking collectives: 14.9 us -> 0 us
  between operations: 14.2 us -> 0.1 us
  other arithmetic: 6.13 us -> 0.08 us
  starting transfers between devices: 14.7 us -> 11.5 us
    dot_general x25 -> x0, matrix products: 63.4 us -> none  [the longest x8 35 us: per_atom(): jnp.einsum('stu,tuac->sac', matches, products, precision=lax.Precision.HI...]
    all_to_all x2 -> x0, waiting for transfers between devices: 32.9 us -> none  [the longest x1 32.9 us: local(): lax.all_to_all(a_tiles, 'col', split_axis=2, concat_axis=1, tiled=True)]
    transpose x8 -> x0, local copies, waits for them, and re-layouts: 27.4 us -> none  [per_atom(): jnp.einsum('tab,tubc->tuac', tiles_row, picked, preferred_element_type=jn...]
    dynamic_slice x16 -> x1, local copies, waits for them, and re-layouts: 18.2 us -> 0.07 us  [local(): own_rows = lax.dynamic_slice_in_dim(b_offsets, start, atoms, 0)]
    pallas_call x0 -> x4, Pallas kernels: none -> 15.9 us  [the longest x3 12.9 us: products(): pl.pallas_call(kernel, out_shape=jax.ShapeDtypeStruct((atoms, slots, tile...]
    another operation x1 -> x0, loops' own time: 15.2 us -> none  [local(): lax.map(per_atom, (masked_a, a_shift, band_slot, c_cols, places))]
    unnamed x1 -> x0, blocking collectives: 14.9 us -> none
    ppermute x2 -> x15, waiting for transfers between devices: 11.8 us -> 26.5 us  [the longest x4 12.1 us: swap(): return lax.ppermute(x, 'col', [(0, 1), (1, 0)])]
  transfers between devices with their start and end apart: 5 -> 15, of which waited for: 3 -> 4; matrix products, arithmetic and copies ran while one was open for 5% -> 9% of each run, Pallas kernels for 0% -> 20%
where the time goes in v1:
time: 61.2 us; the launch traced here: 60.8 us
  waiting for transfers between devices  26.5 us (43%)
  Pallas kernels  15.9 us (26%)
  starting transfers between devices  11.5 us (19%)
  local copies, waits for them, and re-layouts  6.76 us (11%)
    pallas_call x3, Pallas kernels, products(): pl.pallas_call(kernel, out_shape=jax.ShapeDtypeStruct((atoms, slots, tile...  12.9 us
    ppermute x4, waiting for transfers between devices, swap(): return lax.ppermute(x, 'col', [(0, 1), (1, 0)])  12.1 us
    ppermute x1, waiting for transfers between devices, onward(): lax.ppermute(x, ('row', 'col'), [(i, (i + 1) % cycle) for i in range(cycl...  11.9 us
    ppermute x4, starting transfers between devices, swap(): return lax.ppermute(x, 'col', [(0, 1), (1, 0)])  4.64 us
    ppermute x1, starting transfers between devices, back(): lax.ppermute(x, ('row', 'col'), [((i + 1) % cycle, i) for i in range(cycl...  3.11 us
    pallas_call x1, Pallas kernels, band_sums(): pl.pallas_call(band_kernel, out_shape=(shape(atoms), shape(1), shape(1)),...  2.98 us
    reshape x2, local copies, waits for them, and re-layouts, part(): lax.dynamic_slice(a_tiles, at, size).reshape((count,) + a_tiles.shape[4:])  2.78 us
    ppermute x1, waiting for transfers between devices, back(): lax.ppermute(x, ('row', 'col'), [((i + 1) % cycle, i) for i in range(cycl...  2.53 us
  transfers between devices with their start and end apart: 15, of which 4 were waited for; matrix products, arithmetic and copies ran while one was open for 9% of the time, Pallas kernels for 20%

profile of v1, /device:TPU:0, one launch (start us, length us, event | category | flops | bytes accessed | tf_op | source)
XLA Modules:
  0.0 60.8 jit_solution(9211029067337394307)
XLA Ops:
  0.0 0.5 collective-permute-start.4
  0.5 1.9 %dynamic-slice_bitcast_fusion.1 = bf16[4,4,128,128]{3,2,1,0:T(8,128)(2,1)} fusion(bf16[1,1,2,8,4,128,128]{6,5,4,3,2,1,0:T(8,128)(2,1)} %refs_8_.5, s32[]{:T(128)S(6)} %select_n.14), kind=kLoop, calls=%fused_computation.1 | loop fusion | bytes 1048580 | tf_op jit(solution)/shard_map/reshape | solution.py:255
  2.5 2.6 %collective-permute-start.7 = (bf16[4,4,128,128]{3,2,1,0:T(8,128)(2,1)}, bf16[4,4,128,128]{3,2,1,0:T(8,128)(2,1)}, u32[]{:S(2)}, u32[]{:S(2)}) collective-permute-start(bf16[4,4,128,128]{3,2,1,0:T(8,128)(2,1)} %dynamic-slice_bitcast_fusion.1), channel_id=1, source_target_pairs={{0,2},{2,0},{1,3},{3,1},{4,6},{6,4},{5,7},{7,5},{8,10},{10,8},{9,1... | collective-permute-start | bytes 1572872 | tf_op jit(solution)/shard_map/ppermute | solution.py:242
  5.1 2.3 %dynamic-slice_bitcast_fusion = bf16[8,4,128,128]{3,2,1,0:T(8,128)(2,1)} fusion(bf16[1,1,2,8,4,128,128]{6,5,4,3,2,1,0:T(8,128)(2,1)} %refs_8_.5, s32[]{:T(128)S(6)} %select_n.12), kind=kLoop, calls=%fused_computation | loop fusion | bytes 2097156 | tf_op jit(solution)/shard_map/jit(dynamic_index_in_dim)/squeeze | solution.py:270
  7.4 0.1 collective-permute-start.3
  7.5 0.1 copy.15.refs_4_
  7.6 0.3 collective-permute-start.1
  7.8 0.8 %dynamic-slice_bitcast_fusion.2 = (bf16[2,4,128,128]{3,2,1,0:T(8,128)(2,1)}, bf16[2,4,128,128]{3,2,1,0:T(8,128)(2,1)}) fusion(bf16[1,1,2,8,4,128,128]{6,5,4,3,2,1,0:T(8,128)(2,1)S(1)} %copy-done.1, s32[]{:T(128)S(6)} %select_n.14), kind=kLoop, calls=%fused_computation.2 | loop fusion | bytes 1048580 | tf_op jit(solution)/shard_map/reshape | solution.py:255
  8.7 1.7 %collective-permute-start.9 = (bf16[2,4,128,128]{3,2,1,0:T(8,128)(2,1)}, bf16[2,4,128,128]{3,2,1,0:T(8,128)(2,1)S(1)}, u32[]{:S(2)}, u32[]{:S(2)}) collective-permute-start(bf16[2,4,128,128]{3,2,1,0:T(8,128)(2,1)} %get-tuple-element.17), channel_id=1, source_target_pairs={{0,2},{2,0},{1,3},{3,1},{4,6},{6,4},{5,7},{7,5},{8,10},{10,8},{9,1... | collective-permute-start | bytes 786440 | tf_op jit(solution)/shard_map/ppermute | solution.py:242
  10.4 7.7 %collective-permute-done.7.refs_10_ = bf16[4,4,128,128]{3,2,1,0:T(8,128)(2,1)} collective-permute-done((bf16[4,4,128,128]{3,2,1,0:T(8,128)(2,1)}, bf16[4,4,128,128]{3,2,1,0:T(8,128)(2,1)}, u32[]{:S(2)}, u32[]{:S(2)}) %collective-permute-start.7) | collective-permute-done | bytes 524320 | tf_op jit(solution)/shard_map/ppermute | solution.py:242
  18.2 0.0 collective-permute-start.8
  18.2 0.1 constant_dynamic-slice_fusion
  18.2 0.1 pad_add_fusion.pos.refs_0_
  18.3 0.1 copy.16.b_offsets
  18.4 0.0 collective-permute-done.1.refs_6_
  18.4 0.5 collective-permute-start
  18.9 0.1 collective-permute-start.2
  19.0 1.4 %copy-done.2 = bf16[8,6,128,128]{3,2,1,0:T(8,128)(2,1)S(1)} copy-done((bf16[8,6,128,128]{3,2,1,0:T(8,128)(2,1)S(1)}, bf16[8,6,128,128]{3,2,1,0:T(8,128)(2,1)}, u32[]{:S(2)}) %copy-start.2) | copy-done | bytes 1572888
  20.4 3.0 %band_sums.1 = (bf16[40,256,128]{2,1,0:T(8,128)(2,1)S(1)}, bf16[5,256,128]{2,1,0:T(8,128)(2,1)S(1)}, bf16[5,256,128]{2,1,0:T(8,128)(2,1)S(1)}) custom-call(s32[3]{0:T(128)S(1)} %pad_add_fusion.pos.refs_0_, s32[8,12]{1,0:T(8,128)S(1)} %copy.16.b_offsets, s32[64]{0:T(128)S(1)} %copy-done.4, bf16[8,6,128,128]{3,2,1,0:T(8,128)(2,1)S(1)} %copy-done.2, ...), custom_call_target="tpu_custom_call" | custom-call | flops 10000000 | bytes 8388608 | tf_op jit(solution)/shard_map/band_sums/pallas_call | solution.py:49
  23.4 0.0 collective-permute-done.refs_5_
  23.4 2.0 %collective-permute-start.11 = (bf16[5,256,128]{2,1,0:T(8,128)(2,1)S(1)}, bf16[5,256,128]{2,1,0:T(8,128)(2,1)S(1)}, u32[]{:S(2)}, u32[]{:S(2)}) collective-permute-start(bf16[5,256,128]{2,1,0:T(8,128)(2,1)S(1)} %get-tuple-element.15), channel_id=1, source_target_pairs={{0,2},{2,4},{4,6},{6,8},{8,10},{10,12},{12,14},{14,0},{1,3},{3,5},... | collective-permute-start | bytes 983048 | tf_op jit(solution)/shard_map/ppermute | solution.py:245
  25.4 0.0 collective-permute-done.2.refs_7_
  25.4 3.1 %collective-permute-start.13 = (bf16[5,256,128]{2,1,0:T(8,128)(2,1)S(1)}, bf16[5,256,128]{2,1,0:T(8,128)(2,1)S(1)}, u32[]{:S(2)}, u32[]{:S(2)}) collective-permute-start(bf16[5,256,128]{2,1,0:T(8,128)(2,1)S(1)} %get-tuple-element.16), channel_id=1, source_target_pairs={{2,0},{4,2},{6,4},{8,6},{10,8},{12,10},{14,12},{0,14},{3,1},{5,3},... | collective-permute-start | bytes 983048 | tf_op jit(solution)/shard_map/ppermute | solution.py:248
  28.5 0.0 collective-permute-done.9.refs_12_
  28.6 11.9 %collective-permute-done.11.refs_15_ = bf16[5,256,128]{2,1,0:T(8,128)(2,1)S(1)} collective-permute-done((bf16[5,256,128]{2,1,0:T(8,128)(2,1)S(1)}, bf16[5,256,128]{2,1,0:T(8,128)(2,1)S(1)}, u32[]{:S(2)}, u32[]{:S(2)}) %collective-permute-start.11) | collective-permute-done | bytes 327712 | tf_op jit(solution)/shard_map/ppermute | solution.py:245
  40.5 2.5 %collective-permute-done.13.refs_17_ = bf16[5,256,128]{2,1,0:T(8,128)(2,1)S(1)} collective-permute-done((bf16[5,256,128]{2,1,0:T(8,128)(2,1)S(1)}, bf16[5,256,128]{2,1,0:T(8,128)(2,1)S(1)}, u32[]{:S(2)}, u32[]{:S(2)}) %collective-permute-start.13) | collective-permute-done | bytes 327712 | tf_op jit(solution)/shard_map/ppermute | solution.py:248
  43.0 0.0 collective-permute-start.14
  43.0 0.5 collective-permute-start.10
  43.5 4.3 %collective-permute-done.5.refs_10_ = bf16[2,4,128,128]{3,2,1,0:T(8,128)(2,1)S(1)} collective-permute-done((bf16[2,4,128,128]{3,2,1,0:T(8,128)(2,1)S(1)}, bf16[2,4,128,128]{3,2,1,0:T(8,128)(2,1)S(1)}, u32[]{:S(2)}, u32[]{:S(2)}) %collective-permute-start.5) | collective-permute-done | bytes 262176 | tf_op jit(solution)/shard_map/ppermute | solution.py:242
  47.9 3.8 %products.3.refs_19_ = bf16[8,4,128,128]{3,2,1,0:T(8,128)(2,1)} custom-call(s32[3]{0:T(128)S(1)} %pad_add_fusion.pos.refs_0_, s32[8]{0:T(128)S(1)} %copy-done.5, s32[8,8]{1,0:T(8,128)S(1)} %copy-done.3, s32[64]{0:T(128)S(1)} %copy-done.4, s32[1,1,2,8,4]{4,3,2,1,0:T(8,128)S(1)} %copy.15.refs_4_, s32[1,1,2,8,4]{4,3,2,1,0:T(8,128)S(1)} %collective-permute-done.refs_5_, ...), custom_call_target="tpu_custom_call" | custom-call | flops 536870912 | bytes 4194304 | tf_op jit(solution)/shard_map/products/pallas_call | solution.py:202
  51.7 5.2 %products.4.refs_13_ = bf16[8,4,128,128]{3,2,1,0:T(8,128)(2,1)} custom-call(s32[3]{0:T(128)S(1)} %pad_add_fusion.pos.refs_0_, s32[8]{0:T(128)S(1)} %copy-done.5, s32[8,8]{1,0:T(8,128)S(1)} %copy-done.3, s32[64]{0:T(128)S(1)} %copy-done.4, s32[1,1,2,8,4]{4,3,2,1,0:T(8,128)S(1)} %copy.15.refs_4_, ...), custom_call_target="tpu_custom_call", output_to_operand_aliasing={{}: (19, {})} | custom-call | flops 1073741824 | bytes 4194304 | tf_op jit(solution)/shard_map/products/pallas_call | solution.py:202
  57.0 3.9 %products.5 = bf16[8,4,128,128]{3,2,1,0:T(8,128)(2,1)} custom-call(s32[3]{0:T(128)S(1)} %pad_add_fusion.pos.refs_0_, s32[8]{0:T(128)S(1)} %copy-done.5, s32[8,8]{1,0:T(8,128)S(1)} %copy-done.3, s32[64]{0:T(128)S(1)} %copy-done.4, s32[1,1,2,8,4]{4,3,2,1,0:T(8,128)S(1)} %copy.15.refs_4_, ...), custom_call_target="tpu_custom_call", output_to_operand_aliasing={{}: (13, {})} | custom-call | flops 536870912 | bytes 4194304 | tf_op jit(solution)/shard_map/products/pallas_call | solution.py:202
  (25 shorter events, 0.1 us)
Async XLA Ops:
  0.0 18.2 %copy-start = (s32[64,12]{0,1:T(8,128)S(1)}, s32[64,12]{0,1:T(8,128)}, u32[]{:S(2)}) copy-start(s32[64,12]{0,1:T(8,128)} %param.11) | copy-start | bytes 9220
  0.0 7.8 %copy-start.1 = (bf16[1,1,2,8,4,128,128]{6,5,4,3,2,1,0:T(8,128)(2,1)S(1)}, bf16[1,1,2,8,4,128,128]{6,5,4,3,2,1,0:T(8,128)(2,1)}, u32[]{:S(2)}) copy-start(bf16[1,1,2,8,4,128,128]{6,5,4,3,2,1,0:T(8,128)(2,1)} %refs_8_.5) | copy-start | bytes 6291460
  0.0 7.5 %copy-start.7 = (s32[1,1,2,8,4]{3,4,2,1,0:T(4,128)S(1)}, s32[1,1,2,8,4]{3,4,2,1,0:T(4,128)}, u32[]{:S(2)}) copy-start(s32[1,1,2,8,4]{3,4,2,1,0:T(4,128)} %param.8) | copy-start | bytes 772
  0.0 18.9 %collective-permute-start.4 = (bf16[8,6,128,128]{3,2,1,0:T(8,128)(2,1)}, bf16[8,6,128,128]{3,2,1,0:T(8,128)(2,1)}, u32[]{:S(2)}, u32[]{:S(2)}) collective-permute-start(bf16[8,6,128,128]{3,2,1,0:T(8,128)(2,1)} %b_own.1), channel_id=1, source_target_pairs={{0,1},{1,0},{2,3},{3,2},{4,5},{5,4},{6,7},{7,6},{8,9},{9,8},{10,11... | collective-permute-start | bytes 4718600 | tf_op jit(solution)/shard_map/ppermute | solution.py:239
  0.5 18.5 %copy-start.4 = (s32[64]{0:T(128)S(1)}, s32[64]{0:T(128)}, u32[]{:S(2)}) copy-start(s32[64]{0:T(128)} %refs_3_.5) | copy-start | bytes 772
  2.5 15.7 %collective-permute-start.7 = (bf16[4,4,128,128]{3,2,1,0:T(8,128)(2,1)}, bf16[4,4,128,128]{3,2,1,0:T(8,128)(2,1)}, u32[]{:S(2)}, u32[]{:S(2)}) collective-permute-start(bf16[4,4,128,128]{3,2,1,0:T(8,128)(2,1)} %dynamic-slice_bitcast_fusion.1), channel_id=1, source_target_pairs={{0,2},{2,0},{1,3},{3,1},{4,6},{6,4},{5,7},{7,5},{8,10},{10,8},{9,1... | collective-permute-start | bytes 1572872 | tf_op jit(solution)/shard_map/ppermute | solution.py:242
  7.4 40.5 %collective-permute-start.3 = (bf16[8,4,128,128]{3,2,1,0:T(8,128)(2,1)}, bf16[8,4,128,128]{3,2,1,0:T(8,128)(2,1)S(1)}, u32[]{:S(2)}, u32[]{:S(2)}) collective-permute-start(bf16[8,4,128,128]{3,2,1,0:T(8,128)(2,1)} %dynamic-slice_bitcast_fusion), channel_id=1, source_target_pairs={{0,1},{1,0},{2,3},{3,2},{4,5},{5,4},{6,7},{7,6},{8,9},{9,8},{10,11... | collective-permute-start | bytes 3145736 | tf_op jit(solution)/shard_map/ppermute | solution.py:239
  7.5 40.3 %copy-start.3 = (s32[8,8]{1,0:T(8,128)S(1)}, s32[8,8]{1,0:T(8,128)}, u32[]{:S(2)}) copy-start(s32[8,8]{1,0:T(8,128)} %refs_2_.5) | copy-start | bytes 772
  7.5 40.3 %copy-start.5 = (s32[8]{0:T(128)S(1)}, s32[8]{0:T(128)}, u32[]{:S(2)}) copy-start(s32[8]{0:T(128)} %refs_1_.5) | copy-start | bytes 100
  7.6 10.9 %collective-permute-start.1 = (s32[1,1,2,8,4]{4,3,2,1,0:T(8,128)S(1)}, s32[1,1,2,8,4]{4,3,2,1,0:T(8,128)S(1)}, u32[]{:S(2)}, u32[]{:S(2)}) collective-permute-start(s32[1,1,2,8,4]{4,3,2,1,0:T(8,128)S(1)} %copy.15.refs_4_), channel_id=1, source_target_pairs={{0,2},{2,0},{1,3},{3,1},{4,6},{6,4},{5,7},{7,5},{8,10},{10,8},{9,1... | collective-permute-start | bytes 776 | tf_op jit(solution)/shard_map/ppermute | solution.py:242
  8.7 19.9 %collective-permute-start.9 = (bf16[2,4,128,128]{3,2,1,0:T(8,128)(2,1)}, bf16[2,4,128,128]{3,2,1,0:T(8,128)(2,1)S(1)}, u32[]{:S(2)}, u32[]{:S(2)}) collective-permute-start(bf16[2,4,128,128]{3,2,1,0:T(8,128)(2,1)} %get-tuple-element.17), channel_id=1, source_target_pairs={{0,2},{2,0},{1,3},{3,1},{4,6},{6,4},{5,7},{7,5},{8,10},{10,8},{9,1... | collective-permute-start | bytes 786440 | tf_op jit(solution)/shard_map/ppermute | solution.py:242
  18.2 24.9 %collective-permute-start.8 = (bf16[4,4,128,128]{3,2,1,0:T(8,128)(2,1)}, bf16[4,4,128,128]{3,2,1,0:T(8,128)(2,1)}, u32[]{:S(2)}, u32[]{:S(2)}) collective-permute-start(bf16[4,4,128,128]{3,2,1,0:T(8,128)(2,1)} %collective-permute-done.7.refs_10_), channel_id=1, source_target_pairs={{0,1},{1,0},{2,3},{3,2},{4,5},{5,4},{6,7},{7,6},{8,9},{9,8},{10,11... | collective-permute-start | bytes 1572872 | tf_op jit(solution)/shard_map/ppermute | solution.py:239
  18.4 5.0 %collective-permute-start = (s32[1,1,2,8,4]{4,3,2,1,0:T(8,128)S(1)}, s32[1,1,2,8,4]{4,3,2,1,0:T(8,128)S(1)}, u32[]{:S(2)}, u32[]{:S(2)}) collective-permute-start(s32[1,1,2,8,4]{4,3,2,1,0:T(8,128)S(1)} %copy.15.refs_4_), channel_id=1, source_target_pairs={{0,1},{1,0},{2,3},{3,2},{4,5},{5,4},{6,7},{7,6},{8,9},{9,8},{10,11... | collective-permute-start | bytes 776 | tf_op jit(solution)/shard_map/ppermute | solution.py:239
  18.9 6.5 %collective-permute-start.2 = (s32[1,1,2,8,4]{4,3,2,1,0:T(8,128)S(1)}, s32[1,1,2,8,4]{4,3,2,1,0:T(8,128)S(1)}, u32[]{:S(2)}, u32[]{:S(2)}) collective-permute-start(s32[1,1,2,8,4]{4,3,2,1,0:T(8,128)S(1)} %collective-permute-done.1.refs_6_), channel_id=1, source_target_pairs={{0,1},{1,0},{2,3},{3,2},{4,5},{5,4},{6,7},{7,6},{8,9},{9,8},{10,11... | collective-permute-start | bytes 776 | tf_op jit(solution)/shard_map/ppermute | solution.py:239
  19.0 1.4 %copy-start.2 = (bf16[8,6,128,128]{3,2,1,0:T(8,128)(2,1)S(1)}, bf16[8,6,128,128]{3,2,1,0:T(8,128)(2,1)}, u32[]{:S(2)}) copy-start(bf16[8,6,128,128]{3,2,1,0:T(8,128)(2,1)} %b_own.1) | copy-start | bytes 4718596
  20.4 8.1 %copy-start.6 = (bf16[2,4,128,128]{3,2,1,0:T(8,128)(2,1)S(1)}, bf16[2,4,128,128]{3,2,1,0:T(8,128)(2,1)}, u32[]{:S(2)}) copy-start(bf16[2,4,128,128]{3,2,1,0:T(8,128)(2,1)} %get-tuple-element.13) | copy-start | bytes 786436
  23.4 17.1 %collective-permute-start.11 = (bf16[5,256,128]{2,1,0:T(8,128)(2,1)S(1)}, bf16[5,256,128]{2,1,0:T(8,128)(2,1)S(1)}, u32[]{:S(2)}, u32[]{:S(2)}) collective-permute-start(bf16[5,256,128]{2,1,0:T(8,128)(2,1)S(1)} %get-tuple-element.15), channel_id=1, source_target_pairs={{0,2},{2,4},{4,6},{6,8},{8,10},{10,12},{12,14},{14,0},{1,3},{3,5},... | collective-permute-start | bytes 983048 | tf_op jit(solution)/shard_map/ppermute | solution.py:245
  25.4 17.6 %collective-permute-start.13 = (bf16[5,256,128]{2,1,0:T(8,128)(2,1)S(1)}, bf16[5,256,128]{2,1,0:T(8,128)(2,1)S(1)}, u32[]{:S(2)}, u32[]{:S(2)}) collective-permute-start(bf16[5,256,128]{2,1,0:T(8,128)(2,1)S(1)} %get-tuple-element.16), channel_id=1, source_target_pairs={{2,0},{4,2},{6,4},{8,6},{10,8},{12,10},{14,12},{0,14},{3,1},{5,3},... | collective-permute-start | bytes 983048 | tf_op jit(solution)/shard_map/ppermute | solution.py:248
  28.6 19.3 %collective-permute-start.5 = (bf16[2,4,128,128]{3,2,1,0:T(8,128)(2,1)S(1)}, bf16[2,4,128,128]{3,2,1,0:T(8,128)(2,1)S(1)}, u32[]{:S(2)}, u32[]{:S(2)}) collective-permute-start(bf16[2,4,128,128]{3,2,1,0:T(8,128)(2,1)S(1)} %copy-done.6), channel_id=1, source_target_pairs={{0,2},{2,0},{1,3},{3,1},{4,6},{6,4},{5,7},{7,5},{8,10},{10,8},{9,1... | collective-permute-start | bytes 786440 | tf_op jit(solution)/shard_map/ppermute | solution.py:242
  40.5 11.2 %collective-permute-start.12 = (bf16[5,256,128]{2,1,0:T(8,128)(2,1)S(1)}, bf16[5,256,128]{2,1,0:T(8,128)(2,1)S(1)}, u32[]{:S(2)}, u32[]{:S(2)}) collective-permute-start(bf16[5,256,128]{2,1,0:T(8,128)(2,1)S(1)} %collective-permute-done.11.refs_15_), channel_id=1, source_target_pairs={{0,1},{1,0},{2,3},{3,2},{4,5},{5,4},{6,7},{7,6},{8,9},{9,8},{10,11... | collective-permute-start | bytes 983048 | tf_op jit(solution)/shard_map/ppermute | solution.py:239
  43.0 8.7 %collective-permute-start.14 = (bf16[5,256,128]{2,1,0:T(8,128)(2,1)S(1)}, bf16[5,256,128]{2,1,0:T(8,128)(2,1)S(1)}, u32[]{:S(2)}, u32[]{:S(2)}) collective-permute-start(bf16[5,256,128]{2,1,0:T(8,128)(2,1)S(1)} %collective-permute-done.13.refs_17_), channel_id=1, source_target_pairs={{0,1},{1,0},{2,3},{3,2},{4,5},{5,4},{6,7},{7,6},{8,9},{9,8},{10,11... | collective-permute-start | bytes 983048 | tf_op jit(solution)/shard_map/ppermute | solution.py:239
  43.0 8.7 %collective-permute-start.10 = (bf16[2,4,128,128]{3,2,1,0:T(8,128)(2,1)S(1)}, bf16[2,4,128,128]{3,2,1,0:T(8,128)(2,1)S(1)}, u32[]{:S(2)}, u32[]{:S(2)}) collective-permute-start(bf16[2,4,128,128]{3,2,1,0:T(8,128)(2,1)S(1)} %collective-permute-done.9.refs_12_), channel_id=1, source_target_pairs={{0,1},{1,0},{2,3},{3,2},{4,5},{5,4},{6,7},{7,6},{8,9},{9,8},{10,11... | collective-permute-start | bytes 786440 | tf_op jit(solution)/shard_map/ppermute | solution.py:239
  47.9 9.1 %collective-permute-start.6 = (bf16[2,4,128,128]{3,2,1,0:T(8,128)(2,1)S(1)}, bf16[2,4,128,128]{3,2,1,0:T(8,128)(2,1)S(1)}, u32[]{:S(2)}, u32[]{:S(2)}) collective-permute-start(bf16[2,4,128,128]{3,2,1,0:T(8,128)(2,1)S(1)} %collective-permute-done.5.refs_10_), channel_id=1, source_target_pairs={{0,1},{1,0},{2,3},{3,2},{4,5},{5,4},{6,7},{7,6},{8,9},{9,8},{10,11... | collective-permute-start | bytes 786440 | tf_op jit(solution)/shard_map/ppermute | solution.py:239

commit v2 on v0

v2 whole, which is shorter than its diff:
```python
import functools

import jax
import jax.numpy as jnp
from jax import lax
from jax.experimental import pallas as pl
from jax.experimental.pallas import tpu as pltpu
from jax.sharding import PartitionSpec as P

BAND = 2
WIDTH = 2 * BAND + 1
SMEM = pl.BlockSpec(memory_space=pltpu.SMEM)
VMEM = pl.BlockSpec(memory_space=pltpu.VMEM)
ANY = pl.BlockSpec(memory_space=pl.ANY)


def settings(mib):
    return dict(
        compiler_params=pltpu.CompilerParams(vmem_limit_bytes=mib * 2**20),
        cost_estimate=pl.CostEstimate(flops=1, bytes_accessed=1, transcendentals=0),
    )


def cut_kernel(cuts, more, a_tiles, *refs):
    n = len(cuts)
    a_offsets = refs[0]
    outs, bounces, (in_sem, out_sem) = refs[-2 - 2 * n : -2 - n], refs[-2 - n : -2], refs[-2:]
    half, tile = a_tiles.shape[4:6]
    other = 1 - lax.axis_index("col")
    ins, back = [], []
    for i, (p0, count) in enumerate(cuts):
        ins.append(
            [
                pltpu.make_async_copy(
                    a_tiles.at[0, 0, other, p0 + j],
                    bounces[i].at[pl.ds(j * half, half)],
                    in_sem.at[i, j],
                )
                for j in range(count)
            ]
        )
        back.append(pltpu.make_async_copy(bounces[i], outs[i], out_sem.at[i]))
    for moves in ins:
        for move in moves:
            move.start()
    if more:
        atoms = a_offsets.shape[3]
        values = a_offsets[0, 0, pl.ds(other, 1)].reshape(atoms, half).astype(jnp.float32)
        values = jnp.pad(values, ((0, 16 - atoms), (0, tile - half)))
        bounces[0][cuts[0][1] * half, 0:16] = values.astype(jnp.bfloat16)
    for moves, move_back in zip(ins, back, strict=True):
        for move in moves:
            move.wait()
        move_back.start()
    for move in back:
        move.wait()


def cut(a_tiles, cuts, more=()):
    half, tile = a_tiles.shape[4:6]
    n = len(cuts)
    shapes = [(c * half + (bool(more) and i == 0), tile, tile) for i, (_, c) in enumerate(cuts)]
    return pl.pallas_call(
        functools.partial(cut_kernel, cuts, bool(more)),
        out_shape=tuple(jax.ShapeDtypeStruct(s, a_tiles.dtype) for s in shapes),
        in_specs=[ANY] + [VMEM, ANY][: len(more)],
        out_specs=(ANY,) * n,
        scratch_shapes=[pltpu.VMEM(s, a_tiles.dtype) for s in shapes]
        + [
            pltpu.SemaphoreType.DMA((n, max(c for _, c in cuts))),
            pltpu.SemaphoreType.DMA((n,)),
        ],
        name="cut",
        **settings(56),
    )(a_tiles, *more)


def band_kernel(b_offsets, sizes, place, b_own, b_peer, table, tail, head, total):
    atoms, half, tile, _ = b_own.shape
    blocks = sizes.shape[0]
    start, layer = place[0], place[1]
    row_iota = lax.broadcasted_iota(jnp.int32, (tile, tile), 0)
    col_iota = lax.broadcasted_iota(jnp.int32, (tile, tile), 1)

    def one_row(k, _):
        for w in range(WIDTH):
            total[w] = jnp.zeros((tile, tile), jnp.float32)
        for part, ref in ((layer, b_own), (1 - layer, b_peer)):
            for j in range(half):
                w = b_offsets[k, part * half + j] + BAND
                total[w] = total[w] + ref[k, j].astype(jnp.float32)
        rows = sizes[start + k]
        for w in range(WIDTH):
            cols = sizes[lax.rem(start + k + w + blocks - BAND, blocks)]
            value = jnp.where((row_iota < rows) & (col_iota < cols), total[w], 0.0)
            high = value.astype(jnp.bfloat16)
            table[2 * (k * WIDTH + w)] = high
            table[2 * (k * WIDTH + w) + 1] = (value - high.astype(jnp.float32)).astype(jnp.bfloat16)
        return 0

    lax.fori_loop(0, atoms, one_row, 0)
    pair = 2 * WIDTH
    table[pl.ds(atoms * pair, 2)] = jnp.zeros((2, tile, tile), table.dtype)
    tail[...] = table[pl.ds((atoms - BAND + layer) * pair, pair)]
    head[...] = table[pl.ds(layer * pair, pair)]


def band_sums(b_offsets, sizes, place, b_own, b_peer):
    atoms, half, tile, _ = b_own.shape
    shape = lambda tiles: jax.ShapeDtypeStruct((tiles, tile, tile), jnp.bfloat16)
    return pl.pallas_call(
        band_kernel,
        out_shape=(shape(2 * (atoms * WIDTH + 1)), shape(2 * WIDTH), shape(2 * WIDTH)),
        in_specs=[SMEM, SMEM, SMEM, VMEM, VMEM],
        out_specs=(VMEM, VMEM, VMEM),
        scratch_shapes=[pltpu.VMEM((WIDTH, tile, tile), jnp.float32)],
        name="band_sums",
        **settings(16),
    )(b_offsets, sizes, place, b_own, b_peer)


def plan_kernel(two, slots, owner, c_offsets, sizes, place, *refs):
    shifts, far, out = refs[:2], refs[2:4] if two else (), refs[4 if two else 2]
    atoms, half = shifts[0].shape[-2:]
    start, layer, me = place[0], place[1], place[2]
    d = me if two else 0
    mine = owner[0] == me
    if two:
        raw, whole, as_int, sem = refs[5:]
        moves = [
            pltpu.make_async_copy(ref.at[ref.shape[0] - 1, pl.ds(0, 16)], raw.at[h], sem.at[h])
            for h, ref in enumerate(far)
        ]
        for move in moves:
            move.start()
        for move in moves:
            move.wait()
        whole[...] = raw[...].astype(jnp.float32).astype(jnp.int32)
        move = pltpu.make_async_copy(whole, as_int, sem.at[0])
        move.start()
        move.wait()
    out[atoms, 0] = layer
    out[atoms, 1] = me
    out[atoms, 2] = mine.astype(jnp.int32)

    def one_atom(p, _):
        out[p, 2 * half * slots] = sizes[start + p]
        wanted = [c_offsets[p, layer * slots + s] for s in range(slots)]
        for h in range(2):
            for t in range(half):
                shift = shifts[h][0, 0, d, p, t]
                if two:
                    shift = jnp.where(mine, shift, as_int[h, p, t])
                for s in range(slots):
                    w = wanted[s] - shift + BAND
                    at = (p + BAND + shift) * WIDTH + w
                    out[p, (h * half + t) * slots + s] = jnp.where(
                        (w >= 0) & (w < WIDTH), at, -1
                    )
        return 0

    lax.fori_loop(0, atoms, one_atom, 0)


def make_plan(owner, c_offsets, sizes, place, shifts, slots, far=()):
    atoms, half = shifts[0].shape[-2:]
    scratch = []
    if far:
        tile = far[0].shape[-1]
        scratch = [
            pltpu.VMEM((2, 16, tile), jnp.bfloat16),
            pltpu.VMEM((2, 16, tile), jnp.int32),
            pltpu.SMEM((2, 16, tile), jnp.int32),
            pltpu.SemaphoreType.DMA((2,)),
        ]
    return pl.pallas_call(
        functools.partial(plan_kernel, bool(far), slots),
        out_shape=jax.ShapeDtypeStruct((atoms + 1, 2 * half * slots + 1), jnp.int32),
        in_specs=[SMEM] * 6 + [ANY] * len(far),
        out_specs=SMEM,
        scratch_shapes=scratch,
        name="plan",
        **settings(4),
    )(owner, c_offsets, sizes, place, *shifts, *far)


def product_kernel(cfg, plan, *refs):
    refs = list(refs)
    near = refs[:2]
    del refs[:2]
    far = [refs[2 * i : 2 * i + 2] for i in range(cfg["n_far"])]
    del refs[: 2 * cfg["n_far"]]
    table = refs.pop(0)
    halo = refs[: cfg["n_halo"]]
    del refs[: cfg["n_halo"]]
    if cfg["aliased"]:
        refs.pop(0)
    out, a_v, t_v, o_v, a_sem, t_sem, o_sem = refs
    atoms, p0, side = cfg["atoms"], cfg["p0"], cfg["side"]
    count, slots, tile, _ = o_v.shape
    half = a_v.shape[1] // 2
    layer, me, mine = plan[atoms, 0], plan[atoms, 1], plan[atoms, 2]
    d = me if far else 0
    batch = count // max(len(far), 1)

    def moves(n, src):
        if src == 0:
            found = [near[h].at[0, 0, d, p0 + n] for h in range(2)]
        else:
            found = [far[n // batch][h].at[pl.ds(n % batch * half, half)] for h in range(2)]
        return [
            pltpu.make_async_copy(found[h], a_v.at[n, pl.ds(h * half, half)], a_sem.at[n, h])
            for h in range(2)
        ]

    def begin(src):
        for n in range(count):
            for move in moves(n, src):
                move.start()

    if far:
        pl.when(mine == 1)(lambda: begin(0))
        pl.when(mine != 1)(lambda: begin(1))
    else:
        begin(0)
    row0 = BAND
    tiles = table
    if side is not None:
        pair = 2 * WIDTH
        rows = 3 * BAND
        own, own_at, halo_at, row0 = (
            (0, BAND, 0, 0) if side == "low" else (atoms - 2 * BAND, 0, 2 * BAND, atoms - BAND)
        )
        tiles = t_v
        fills = [
            pltpu.make_async_copy(
                table.at[pl.ds(own * pair, 2 * BAND * pair)],
                t_v.at[pl.ds(own_at * pair, 2 * BAND * pair)],
                t_sem.at[0],
            )
        ]
        for i, ref in enumerate(halo):
            at = halo_at + (layer if i == 0 else 1 - layer)
            fills.append(
                pltpu.make_async_copy(ref, t_v.at[pl.ds(at * pair, pair)], t_sem.at[1 + i])
            )
        for fill in fills:
            fill.start()
        t_v[pl.ds(rows * pair, 2)] = jnp.zeros((2, tile, tile), t_v.dtype)
        for fill in fills:
            fill.wait()
    zero_at = tiles.shape[0] // 2 - 1
    row_iota = lax.broadcasted_iota(jnp.int32, (tile, 2 * tile), 0)

    def one_atom(n, _):
        p = p0 + n
        for move in moves(n, 0):
            move.wait()

        def factor(t, s):
            at = plan[p, t * slots + s]
            at = 2 * jnp.where(at < 0, zero_at, at - row0 * WIDTH)
            return jnp.concatenate([tiles[at], tiles[at + 1]], axis=0)

        size = plan[p, 2 * half * slots]
        for q in range(slots // 2):
            total = jnp.zeros((tile, 2 * tile), jnp.float32)
            for t in range(2 * half):
                left = a_v[n, t]
                left = jnp.concatenate([left, left], axis=1)
                right = jnp.concatenate([factor(t, 2 * q), factor(t, 2 * q + 1)], axis=1)
                total += jnp.dot(left, right, preferred_element_type=jnp.float32)
            total = jnp.where(row_iota < size, total, 0.0).astype(jnp.bfloat16)
            o_v[n, 2 * q] = total[:, :tile]
            o_v[n, 2 * q + 1] = total[:, tile:]
        pltpu.make_async_copy(o_v.at[n], out.at[p], o_sem.at[n]).start()
        return 0

    lax.fori_loop(0, count, one_atom, 0)

    def finish(n, _):
        pltpu.make_async_copy(o_v.at[n], out.at[p0 + n], o_sem.at[n]).wait()
        return 0

    lax.fori_loop(0, count, finish, 0)


def products(plan, near, far, table, halo, side, slots, atoms, prior=None):
    tile, half = table.shape[-1], near[0].shape[-3]
    count = atoms - 2 * BAND if side is None else BAND
    operands = [plan, *near, *[f for pair in far for f in pair], table, *halo]
    specs = [SMEM] + [ANY] * (len(operands) - 1)
    specs[1 + 2 + 2 * len(far)] = VMEM
    aliases = {}
    if prior is not None:
        aliases = {len(operands): 0}
        operands.append(prior)
        specs.append(ANY)
    cfg = dict(
        atoms=atoms,
        p0={None: BAND, "low": 0, "top": atoms - BAND}[side],
        n_far=len(far),
        n_halo=len(halo),
        side=side,
        aliased=prior is not None,
    )
    rows = 0 if side is None else 3 * BAND * WIDTH
    return pl.pallas_call(
        functools.partial(product_kernel, cfg),
        out_shape=jax.ShapeDtypeStruct((atoms, slots, tile, tile), jnp.bfloat16),
        in_specs=specs,
        out_specs=ANY,
        scratch_shapes=[
            pltpu.VMEM((count, 2 * half, tile, tile), jnp.bfloat16),
            pltpu.VMEM((2 * (rows + 1), tile, tile), jnp.bfloat16),
            pltpu.VMEM((count, slots, tile, tile), jnp.bfloat16),
            pltpu.SemaphoreType.DMA((count, 2)),
            pltpu.SemaphoreType.DMA((3,)),
            pltpu.SemaphoreType.DMA((count,)),
        ],
        input_output_aliases=aliases,
        name="products" if side is None else "products_" + side,
        **settings(12),
    )(*operands)


def after(x, *others):
    return lax.optimization_barrier((x,) + others)[0]


def local(a_tiles, a_offsets, atom_owner, b_tiles, b_offsets, c_offsets, block_sizes):
    cols = lax.axis_size("col")
    cycle = lax.axis_size("row") * cols
    atoms = atom_owner.shape[0]
    bucket = a_tiles.shape[3]
    slots = c_offsets.shape[1] // 2
    me = lax.axis_index("col")
    layer = lax.axis_index("layer")
    start = (lax.axis_index("row") * cols + me) * atoms
    place = jnp.stack([start, layer, me]).astype(jnp.int32)
    assert atoms * cycle > 8 * BAND and lax.axis_size("layer") == 2 and atoms >= 4 * BAND

    def across(x):
        return lax.ppermute(x, "layer", [(0, 1), (1, 0)])

    def swap(x):
        return lax.ppermute(x, "col", [(0, 1), (1, 0)])

    def onward(x):
        return lax.ppermute(x, ("row", "col"), [(i, (i + 1) % cycle) for i in range(cycle)])

    def back(x):
        return lax.ppermute(x, ("row", "col"), [((i + 1) % cycle, i) for i in range(cycle)])

    b_peer = across(b_tiles)
    if cols == 2 and bucket == atoms:
        firsts = cut(a_tiles, ((BAND, BAND),))
        rest = ((2 * BAND, atoms - 3 * BAND), (0, BAND), (atoms - BAND, BAND))
        mid, low, top = cut(a_tiles, rest, (a_offsets, firsts[0]))
        b_offsets = after(b_offsets, mid)
        near = (a_tiles, across(after(a_tiles, mid)))
        mids = [swap(firsts[0]), swap(mid)]
    own_rows = lax.dynamic_slice_in_dim(b_offsets, start, atoms, 0)
    table, tail, head = band_sums(own_rows, block_sizes, place, b_tiles, b_peer)
    tail, head = onward(tail), back(head)
    if cols == 2 and bucket == atoms:
        low, top = swap(after(low, table)), swap(after(top, table))
        mids = [after(m, table) for m in mids]
        mids = [(m, across(m)) for m in mids]
        shifts = (a_offsets, across(a_offsets))
        plan = make_plan(atom_owner, c_offsets, block_sizes, place, shifts, slots, mids[-1])
        call = functools.partial(products, plan, near, slots=slots, atoms=atoms)
        c = call(mids, table, (), None)
        tail, head = after(tail, c), after(head, c)
        tail, head = (tail, across(tail)), (head, across(head))
        low = ((low, across(low)),)
        c = call(low, table, tail, "low", prior=c)
        top = after(top, c, head[1])
        return call(((top, across(top)),), table, head, "top", prior=c)
    received = lax.all_to_all(a_tiles, "col", split_axis=2, concat_axis=1, tiled=True)
    moved = lax.all_to_all(a_offsets, "col", split_axis=2, concat_axis=1, tiled=True)
    received = received.reshape((-1,) + received.shape[4:])
    moved = moved.reshape((-1,) + moved.shape[4:])
    places = jnp.arange(atoms, dtype=jnp.int32)
    same = atom_owner[:, None] == atom_owner[None, :]
    rank = jnp.sum(same & (places[None, :] < places[:, None]), axis=1)
    source = atom_owner * bucket + rank
    rows = jnp.take(received, source, axis=0)[None, None, None]
    shift = jnp.take(moved, source, axis=0)[None, None, None]
    plan = make_plan(atom_owner, c_offsets, block_sizes, place, (shift, across(shift)), slots)
    call = functools.partial(
        products, plan, (rows, across(rows)), [], table, slots=slots, atoms=atoms
    )
    c = call((), None)
    c = call((tail, across(tail)), "low", prior=c)
    return call((head, across(head)), "top", prior=c)


def solution(mesh):
    placed = (
        P(("groups", "row"), "col", None, None, "layer", None, None),
        P(("groups", "row"), "col", None, None, "layer"),
        P(("groups", "row", "col")),
        P(("groups", "row", "col"), "layer", None, None),
        P("groups", None),
        P(("groups", "row", "col"), None),
        P("groups"),
    )
    return jax.shard_map(
        local,
        mesh=mesh,
        in_specs=placed,
        out_specs=P(("groups", "row", "col"), "layer", None, None),
        check_vma=False,
    )
```

time: 245 us -> 55.5 us (0.23)
  local copies, waits for them, and re-layouts: 70.6 us -> 0.82 us
  matrix products: 63.4 us -> 0 us
  waiting for transfers between devices: 44.8 us -> 11 us
  Pallas kernels: 0 us -> 22.3 us
  loops' own time: 15.2 us -> 0 us
  blocking collectives: 14.9 us -> 0 us
  between operations: 14.2 us -> 0.16 us
  starting transfers between devices: 14.7 us -> 20.8 us
  other arithmetic: 6.13 us -> 0.08 us
    dot_general x25 -> x0, matrix products: 63.4 us -> none  [the longest x8 35 us: per_atom(): jnp.einsum('stu,tuac->sac', matches, products, precision=lax.Precision.HI...]
    all_to_all x2 -> x0, waiting for transfers between devices: 32.9 us -> none  [the longest x1 32.9 us: local(): lax.all_to_all(a_tiles, 'col', split_axis=2, concat_axis=1, tiled=True)]
    transpose x8 -> x0, local copies, waits for them, and re-layouts: 27.4 us -> none  [per_atom(): jnp.einsum('tab,tubc->tuac', tiles_row, picked, preferred_element_type=jn...]
    pallas_call x0 -> x7, Pallas kernels: none -> 22.3 us  [the longest x3 11.1 us: products(): pl.pallas_call(functools.partial(product_kernel, cfg), out_shape=jax.Shap...]
    dynamic_slice x16 -> x1, local copies, waits for them, and re-layouts: 18.2 us -> 0.01 us  [local(): own_rows = lax.dynamic_slice_in_dim(b_offsets, start, atoms, 0)]
    ppermute x2 -> x15, starting transfers between devices: 5.59 us -> 20.8 us  [the longest x4 14.2 us: swap(): return lax.ppermute(x, 'col', [(0, 1), (1, 0)])]
    another operation x1 -> x0, loops' own time: 15.2 us -> none  [local(): lax.map(per_atom, (masked_a, a_shift, band_slot, c_cols, places))]
    unnamed x1 -> x0, blocking collectives: 14.9 us -> none
  transfers between devices with their start and end apart: 5 -> 15, of which waited for: 3 -> 7; matrix products, arithmetic and copies ran while one was open for 5% -> 0% of each run, Pallas kernels for 0% -> 26%
where the time goes in v2:
time: 55.5 us; the launch traced here: 55.2 us
  Pallas kernels  22.3 us (40%)
  starting transfers between devices  20.8 us (37%)
  waiting for transfers between devices  11 us (20%)
  local copies, waits for them, and re-layouts  0.82 us (1%)
    ppermute x4, starting transfers between devices, swap(): return lax.ppermute(x, 'col', [(0, 1), (1, 0)])  14.2 us
    pallas_call x3, Pallas kernels, products(): pl.pallas_call(functools.partial(product_kernel, cfg), out_shape=jax.Shap...  11.1 us
    ppermute x9, waiting for transfers between devices, across(): return lax.ppermute(x, 'layer', [(0, 1), (1, 0)])  5.73 us
    ppermute x4, waiting for transfers between devices, swap(): return lax.ppermute(x, 'col', [(0, 1), (1, 0)])  5.27 us
    pallas_call x2, Pallas kernels, cut(): pl.pallas_call(functools.partial(cut_kernel, cuts, bool(more)), out_shape...  4.53 us
    pallas_call x1, Pallas kernels, band_sums(): pl.pallas_call(band_kernel, out_shape=(shape(2 * (atoms * WIDTH + 1)), sh...  3.38 us
    pallas_call x1, Pallas kernels, make_plan(): pl.pallas_call(functools.partial(plan_kernel, bool(far), slots), out_shap...  3.29 us
    ppermute x1, starting transfers between devices, back(): lax.ppermute(x, ('row', 'col'), [((i + 1) % cycle, i) for i in range(cycl...  3.04 us
  transfers between devices with their start and end apart: 15, of which 7 were waited for; matrix products, arithmetic and copies ran while one was open for 0% of the time, Pallas kernels for 26%

profile of v2, /device:TPU:0, one launch (start us, length us, event | category | flops | bytes accessed | tf_op | source)
XLA Modules:
  0.0 55.2 jit_solution(1243430729226287887)
XLA Ops:
  0.0 1.9 %cut.2.refs_1_ = bf16[8,128,128]{2,1,0:T(8,128)(2,1)} custom-call(bf16[1,1,2,8,4,128,128]{6,5,4,3,2,1,0:T(8,128)(2,1)} %refs_0_.7), custom_call_target="tpu_custom_call" | custom-call | flops 1 | bytes 1 | tf_op jit(solution)/shard_map/cut/pallas_call | solution.py:63
  1.9 0.7 %copy.13.refs_0_ = s32[1,1,2,8,4]{4,3,2,1,0:T(8,128)} copy(s32[1,1,2,8,4]{3,4,2,1,0:T(4,128)S(1)} %copy-done.7) | data formatting | bytes 512 | tf_op args[1]
  2.6 2.7 %cut.3 = (bf16[9,128,128]{2,1,0:T(8,128)(2,1)}, bf16[8,128,128]{2,1,0:T(8,128)(2,1)}, bf16[8,128,128]{2,1,0:T(8,128)(2,1)}) custom-call(bf16[1,1,2,8,4,128,128]{6,5,4,3,2,1,0:T(8,128)(2,1)} %refs_0_.7, s32[1,1,2,8,4]{4,3,2,1,0:T(8,128)} %copy.13.refs_0_, bf16[8,128,128]{2,1,0:T(8,128)(2,1)} %cut.2.refs_1_), custom_call_target="tpu_custom_call" | custom-call | flops 1 | bytes 1 | tf_op jit(solution)/shard_map/cut/pallas_call | solution.py:63
  5.3 0.0 copy-start.2
  5.3 0.0 copy-start.4
  5.3 0.5 collective-permute-start.4
  5.8 0.1 collective-permute-start.2
  5.9 2.9 %collective-permute-start.1 = (bf16[9,128,128]{2,1,0:T(8,128)(2,1)}, bf16[9,128,128]{2,1,0:T(8,128)(2,1)S(1)}, u32[]{:S(2)}, u32[]{:S(2)}) collective-permute-start(bf16[9,128,128]{2,1,0:T(8,128)(2,1)} %get-tuple-element.20), channel_id=1, source_target_pairs={{0,2},{2,0},{1,3},{3,1},{4,6},{6,4},{5,7},{7,5},{8,10},{10,8},{9,1... | collective-permute-start | bytes 884744 | tf_op jit(solution)/shard_map/ppermute | solution.py:347
  8.8 0.0 collective-permute-start.9
  8.9 0.1 copy.12
  9.0 0.1 pad_add_fusion.place
  9.0 3.2 %collective-permute-done.2.b_peer = bf16[8,6,128,128]{3,2,1,0:T(8,128)(2,1)} collective-permute-done((bf16[8,6,128,128]{3,2,1,0:T(8,128)(2,1)}, bf16[8,6,128,128]{3,2,1,0:T(8,128)(2,1)}, u32[]{:S(2)}, u32[]{:S(2)}) %collective-permute-start.2) | collective-permute-done | bytes 1572896 | tf_op jit(solution)/shard_map/ppermute | solution.py:344
  12.2 3.4 %band_sums.1 = (bf16[82,128,128]{2,1,0:T(8,128)(2,1)S(1)}, bf16[10,128,128]{2,1,0:T(8,128)(2,1)S(1)}, bf16[10,128,128]{2,1,0:T(8,128)(2,1)S(1)}) custom-call(s32[8,12]{1,0:T(8,128)S(1)} %constant_dynamic-slice_fusion.b_offsets, s32[64]{0:T(128)S(1)} %copy-done.3, s32[3]{0:T(128)S(1)} %pad_add_fusion.place, bf16[8,6,128,128]{3,2,1,0:T(8,128)(2,1)} %b_own.1, ...), custom_call_target="tpu_custom_call" | custom-call | flops 1 | bytes 1 | tf_op jit(solution)/shard_map/band_sums/pallas_call | solution.py:111
  15.6 1.2 %collective-permute-done.1.refs_2_.refs_4_ = bf16[9,128,128]{2,1,0:T(8,128)(2,1)S(1)} collective-permute-done((bf16[9,128,128]{2,1,0:T(8,128)(2,1)}, bf16[9,128,128]{2,1,0:T(8,128)(2,1)S(1)}, u32[]{:S(2)}, u32[]{:S(2)}) %collective-permute-start.1) | collective-permute-done | bytes 294944 | tf_op jit(solution)/shard_map/ppermute | solution.py:347
  16.9 0.0 collective-permute-start.3
  16.9 2.1 %collective-permute-start.8 = (bf16[10,128,128]{2,1,0:T(8,128)(2,1)S(1)}, bf16[10,128,128]{2,1,0:T(8,128)(2,1)S(1)}, u32[]{:S(2)}, u32[]{:S(2)}) collective-permute-start(bf16[10,128,128]{2,1,0:T(8,128)(2,1)S(1)} %get-tuple-element.29), channel_id=1, source_target_pairs={{0,2},{2,4},{4,6},{6,8},{8,10},{10,12},{12,14},{14,0},{1,3},{3,5},... | collective-permute-start | bytes 983048 | tf_op jit(solution)/shard_map/ppermute | solution.py:350
  18.9 3.0 %collective-permute-start.12 = (bf16[10,128,128]{2,1,0:T(8,128)(2,1)S(1)}, bf16[10,128,128]{2,1,0:T(8,128)(2,1)S(1)}, u32[]{:S(2)}, u32[]{:S(2)}) collective-permute-start(bf16[10,128,128]{2,1,0:T(8,128)(2,1)S(1)} %get-tuple-element.32), channel_id=1, source_target_pairs={{2,0},{4,2},{6,4},{8,6},{10,8},{12,10},{14,12},{0,14},{3,1},{5,3},... | collective-permute-start | bytes 983048 | tf_op jit(solution)/shard_map/ppermute | solution.py:353
  22.0 0.1 collective-permute-done.9.refs_2_
  22.0 0.2 collective-permute-start
  22.2 1.0 %collective-permute-done.refs_1_ = s32[1,1,2,8,4]{4,3,2,1,0:T(8,128)S(1)} collective-permute-done((s32[1,1,2,8,4]{4,3,2,1,0:T(8,128)S(1)}, s32[1,1,2,8,4]{4,3,2,1,0:T(8,128)S(1)}, u32[]{:S(2)}, u32[]{:S(2)}) %collective-permute-start) | collective-permute-done | bytes 288 | tf_op jit(solution)/shard_map/ppermute | solution.py:344
  23.2 0.2 collective-permute-start.10
  23.4 9.5 %collective-permute-start.6 = (bf16[8,128,128]{2,1,0:T(8,128)(2,1)S(1)}, bf16[8,128,128]{2,1,0:T(8,128)(2,1)S(1)}, u32[]{:S(2)}, u32[]{:S(2)}) collective-permute-start(bf16[8,128,128]{2,1,0:T(8,128)(2,1)S(1)} %copy-done.9), channel_id=1, source_target_pairs={{0,2},{2,0},{1,3},{3,1},{4,6},{6,4},{5,7},{7,5},{8,10},{10,8},{9,1... | collective-permute-start | bytes 786440 | tf_op jit(solution)/shard_map/ppermute | solution.py:347
  32.9 3.3 %plan.1 = s32[9,33]{1,0:T(8,128)S(1)} custom-call(s32[8]{0:T(128)S(1)} %copy-done.4, s32[8,8]{1,0:T(8,128)S(1)} %copy-done.2, s32[64]{0:T(128)S(1)} %copy-done.3, s32[3]{0:T(128)S(1)} %pad_add_fusion.place, s32[1,1,2,8,4]{4,3,2,1,0:T(8,128)S(1)} %copy-done.1, s32[1,1,2,8,4]{4,3,2,1,0:T(8,128)S(1)} %collective-permute-done.refs_1_, ...), custom_call_target="tpu_custom_call" | custom-call | flops 1 | bytes 1 | tf_op jit(solution)/shard_map/plan/pallas_call | solution.py:176
  36.2 4.4 %products.1.refs_7_ = bf16[8,4,128,128]{3,2,1,0:T(8,128)(2,1)} custom-call(s32[9,33]{1,0:T(8,128)S(1)} %plan.1, bf16[1,1,2,8,4,128,128]{6,5,4,3,2,1,0:T(8,128)(2,1)S(1)} %copy-done, bf16[1,1,2,8,4,128,128]{6,5,4,3,2,1,0:T(8,128)(2,1)} %collective-permute-done.4.refs_1_, bf16[8,128,128]{2,1,0:T(8,128)(2,1)S(1)} %collective-permute-done.9.refs_2_, ...), custom_call_target="tpu_custom_call" | custom-call | flops 1 | bytes 1 | tf_op jit(solution)/shard_map/products/pallas_call | solution.py:308
  40.6 0.1 collective-permute-start.11
  40.8 0.4 collective-permute-start.13
  41.2 0.4 collective-permute-done.6.refs_2_
  41.6 1.7 %collective-permute-start.5 = (bf16[8,128,128]{2,1,0:T(8,128)(2,1)S(1)}, bf16[8,128,128]{2,1,0:T(8,128)(2,1)S(1)}, u32[]{:S(2)}, u32[]{:S(2)}) collective-permute-start(bf16[8,128,128]{2,1,0:T(8,128)(2,1)S(1)} %copy-done.8), channel_id=1, source_target_pairs={{0,2},{2,0},{1,3},{3,1},{4,6},{6,4},{5,7},{7,5},{8,10},{10,8},{9,1... | collective-permute-start | bytes 786440 | tf_op jit(solution)/shard_map/ppermute | solution.py:347
  43.3 3.4 %products_low.1.refs_7_ = bf16[8,4,128,128]{3,2,1,0:T(8,128)(2,1)} custom-call(s32[9,33]{1,0:T(8,128)S(1)} %plan.1, bf16[1,1,2,8,4,128,128]{6,5,4,3,2,1,0:T(8,128)(2,1)S(1)} %copy-done, bf16[1,1,2,8,4,128,128]{6,5,4,3,2,1,0:T(8,128)(2,1)} %collective-permute-done.4.refs_1_, ...), custom_call_target="tpu_custom_call", output_to_operand_aliasing={{}: (8, {})} | custom-call | flops 1 | bytes 1 | tf_op jit(solution)/shard_map/products_low/pallas_call | solution.py:308
  46.7 3.6 %collective-permute-done.5.refs_2_ = bf16[8,128,128]{2,1,0:T(8,128)(2,1)S(1)} collective-permute-done((bf16[8,128,128]{2,1,0:T(8,128)(2,1)S(1)}, bf16[8,128,128]{2,1,0:T(8,128)(2,1)S(1)}, u32[]{:S(2)}, u32[]{:S(2)}) %collective-permute-start.5) | collective-permute-done | bytes 262176 | tf_op jit(solution)/shard_map/ppermute | solution.py:347
  50.3 1.5 %collective-permute-done.14.refs_3_ = bf16[8,128,128]{2,1,0:T(8,128)(2,1)S(1)} collective-permute-done((bf16[8,128,128]{2,1,0:T(8,128)(2,1)S(1)}, bf16[8,128,128]{2,1,0:T(8,128)(2,1)S(1)}, u32[]{:S(2)}, u32[]{:S(2)}) %collective-permute-start.14) | collective-permute-done | bytes 262176 | tf_op jit(solution)/shard_map/ppermute | solution.py:344
  51.8 3.4 %products_top.1 = bf16[8,4,128,128]{3,2,1,0:T(8,128)(2,1)} custom-call(s32[9,33]{1,0:T(8,128)S(1)} %plan.1, bf16[1,1,2,8,4,128,128]{6,5,4,3,2,1,0:T(8,128)(2,1)S(1)} %copy-done, bf16[1,1,2,8,4,128,128]{6,5,4,3,2,1,0:T(8,128)(2,1)} %collective-permute-done.4.refs_1_, ...), custom_call_target="tpu_custom_call", output_to_operand_aliasing={{}: (8, {})} | custom-call | flops 1 | bytes 1 | tf_op jit(solution)/shard_map/products_top/pallas_call | solution.py:308
  (29 shorter events, 0.1 us)
Async XLA Ops:
  0.0 5.3 %copy-start = (bf16[1,1,2,8,4,128,128]{6,5,4,3,2,1,0:T(8,128)(2,1)S(1)}, bf16[1,1,2,8,4,128,128]{6,5,4,3,2,1,0:T(8,128)(2,1)}, u32[]{:S(2)}) copy-start(bf16[1,1,2,8,4,128,128]{6,5,4,3,2,1,0:T(8,128)(2,1)} %refs_0_.7) | copy-start | bytes 6291460
  0.0 1.9 %copy-start.7 = (s32[1,1,2,8,4]{3,4,2,1,0:T(4,128)S(1)}, s32[1,1,2,8,4]{3,4,2,1,0:T(4,128)}, u32[]{:S(2)}) copy-start(s32[1,1,2,8,4]{3,4,2,1,0:T(4,128)} %param.8) | copy-start | bytes 772
  0.0 8.9 %copy-start.6 = (s32[64,12]{0,1:T(8,128)S(1)}, s32[64,12]{0,1:T(8,128)}, u32[]{:S(2)}) copy-start(s32[64,12]{0,1:T(8,128)} %param.11) | copy-start | bytes 9220
  0.0 12.2 %copy-start.3 = (s32[64]{0:T(128)S(1)}, s32[64]{0:T(128)}, u32[]{:S(2)}) copy-start(s32[64]{0:T(128)} %sizes.3) | copy-start | bytes 772
  1.9 7.0 %copy-start.5 = (bf16[8,128,128]{2,1,0:T(8,128)(2,1)S(1)}, bf16[8,128,128]{2,1,0:T(8,128)(2,1)}, u32[]{:S(2)}) copy-start(bf16[8,128,128]{2,1,0:T(8,128)(2,1)} %cut.2.refs_1_) | copy-start | bytes 786436
  5.3 16.8 %copy-start.1 = (s32[1,1,2,8,4]{4,3,2,1,0:T(8,128)S(1)}, s32[1,1,2,8,4]{4,3,2,1,0:T(8,128)}, u32[]{:S(2)}) copy-start(s32[1,1,2,8,4]{4,3,2,1,0:T(8,128)} %copy.13.refs_0_) | copy-start | bytes 772
  5.3 18.1 %copy-start.9 = (bf16[8,128,128]{2,1,0:T(8,128)(2,1)S(1)}, bf16[8,128,128]{2,1,0:T(8,128)(2,1)}, u32[]{:S(2)}) copy-start(bf16[8,128,128]{2,1,0:T(8,128)(2,1)} %get-tuple-element.28) | copy-start | bytes 786436
  5.3 27.6 %copy-start.2 = (s32[8,8]{1,0:T(8,128)S(1)}, s32[8,8]{1,0:T(8,128)}, u32[]{:S(2)}) copy-start(s32[8,8]{1,0:T(8,128)} %c_offsets.1) | copy-start | bytes 772
  5.3 27.6 %copy-start.4 = (s32[8]{0:T(128)S(1)}, s32[8]{0:T(128)}, u32[]{:S(2)}) copy-start(s32[8]{0:T(128)} %owner.1) | copy-start | bytes 100
  5.3 30.9 %collective-permute-start.4 = (bf16[1,1,2,8,4,128,128]{6,5,4,3,2,1,0:T(8,128)(2,1)S(1)}, bf16[1,1,2,8,4,128,128]{6,5,4,3,2,1,0:T(8,128)(2,1)}, u32[]{:S(2)}, u32[]{:S(2)}) collective-permute-start(bf16[1,1,2,8,4,128,128]{6,5,4,3,2,1,0:T(8,128)(2,1)S(1)} %copy-done), channel_id=1, source_target_pairs={{0,1},{1,0},{2,3},{3,2},{4,5},{5,4},{6,7},{7,6},{8,9},{9,8},{10,11... | collective-permute-start | bytes 6291464 | tf_op jit(solution)/shard_map/ppermute | solution.py:344
  5.8 6.4 %collective-permute-start.2 = (bf16[8,6,128,128]{3,2,1,0:T(8,128)(2,1)}, bf16[8,6,128,128]{3,2,1,0:T(8,128)(2,1)}, u32[]{:S(2)}, u32[]{:S(2)}) collective-permute-start(bf16[8,6,128,128]{3,2,1,0:T(8,128)(2,1)} %b_own.1), channel_id=1, source_target_pairs={{0,1},{1,0},{2,3},{3,2},{4,5},{5,4},{6,7},{7,6},{8,9},{9,8},{10,11... | collective-permute-start | bytes 4718600 | tf_op jit(solution)/shard_map/ppermute | solution.py:344
  5.9 10.9 %collective-permute-start.1 = (bf16[9,128,128]{2,1,0:T(8,128)(2,1)}, bf16[9,128,128]{2,1,0:T(8,128)(2,1)S(1)}, u32[]{:S(2)}, u32[]{:S(2)}) collective-permute-start(bf16[9,128,128]{2,1,0:T(8,128)(2,1)} %get-tuple-element.20), channel_id=1, source_target_pairs={{0,2},{2,0},{1,3},{3,1},{4,6},{6,4},{5,7},{7,5},{8,10},{10,8},{9,1... | collective-permute-start | bytes 884744 | tf_op jit(solution)/shard_map/ppermute | solution.py:347
  8.8 13.2 %collective-permute-start.9 = (bf16[8,128,128]{2,1,0:T(8,128)(2,1)S(1)}, bf16[8,128,128]{2,1,0:T(8,128)(2,1)S(1)}, u32[]{:S(2)}, u32[]{:S(2)}) collective-permute-start(bf16[8,128,128]{2,1,0:T(8,128)(2,1)S(1)} %copy-done.5), channel_id=1, source_target_pairs={{0,2},{2,0},{1,3},{3,1},{4,6},{6,4},{5,7},{7,5},{8,10},{10,8},{9,1... | collective-permute-start | bytes 786440 | tf_op jit(solution)/shard_map/ppermute | solution.py:347
  16.9 6.5 %collective-permute-start.3 = (bf16[9,128,128]{2,1,0:T(8,128)(2,1)S(1)}, bf16[9,128,128]{2,1,0:T(8,128)(2,1)S(1)}, u32[]{:S(2)}, u32[]{:S(2)}) collective-permute-start(bf16[9,128,128]{2,1,0:T(8,128)(2,1)S(1)} %collective-permute-done.1.refs_2_.refs_4_), channel_id=1, source_target_pairs={{0,1},{1,0},{2,3},{3,2},{4,5},{5,4},{6,7},{7,6},{8,9},{9,8},{10,11... | collective-permute-start | bytes 884744 | tf_op jit(solution)/shard_map/ppermute | solution.py:344
  16.9 23.8 %collective-permute-start.8 = (bf16[10,128,128]{2,1,0:T(8,128)(2,1)S(1)}, bf16[10,128,128]{2,1,0:T(8,128)(2,1)S(1)}, u32[]{:S(2)}, u32[]{:S(2)}) collective-permute-start(bf16[10,128,128]{2,1,0:T(8,128)(2,1)S(1)} %get-tuple-element.29), channel_id=1, source_target_pairs={{0,2},{2,4},{4,6},{6,8},{8,10},{10,12},{12,14},{14,0},{1,3},{3,5},... | collective-permute-start | bytes 983048 | tf_op jit(solution)/shard_map/ppermute | solution.py:350
  18.9 21.8 %collective-permute-start.12 = (bf16[10,128,128]{2,1,0:T(8,128)(2,1)S(1)}, bf16[10,128,128]{2,1,0:T(8,128)(2,1)S(1)}, u32[]{:S(2)}, u32[]{:S(2)}) collective-permute-start(bf16[10,128,128]{2,1,0:T(8,128)(2,1)S(1)} %get-tuple-element.32), channel_id=1, source_target_pairs={{2,0},{4,2},{6,4},{8,6},{10,8},{12,10},{14,12},{0,14},{3,1},{5,3},... | collective-permute-start | bytes 983048 | tf_op jit(solution)/shard_map/ppermute | solution.py:353
  22.0 1.2 %collective-permute-start = (s32[1,1,2,8,4]{4,3,2,1,0:T(8,128)S(1)}, s32[1,1,2,8,4]{4,3,2,1,0:T(8,128)S(1)}, u32[]{:S(2)}, u32[]{:S(2)}) collective-permute-start(s32[1,1,2,8,4]{4,3,2,1,0:T(8,128)S(1)} %copy-done.1), channel_id=1, source_target_pairs={{0,1},{1,0},{2,3},{3,2},{4,5},{5,4},{6,7},{7,6},{8,9},{9,8},{10,11... | collective-permute-start | bytes 776 | tf_op jit(solution)/shard_map/ppermute | solution.py:344
  23.2 13.0 %collective-permute-start.10 = (bf16[8,128,128]{2,1,0:T(8,128)(2,1)S(1)}, bf16[8,128,128]{2,1,0:T(8,128)(2,1)S(1)}, u32[]{:S(2)}, u32[]{:S(2)}) collective-permute-start(bf16[8,128,128]{2,1,0:T(8,128)(2,1)S(1)} %collective-permute-done.9.refs_2_), channel_id=1, source_target_pairs={{0,1},{1,0},{2,3},{3,2},{4,5},{5,4},{6,7},{7,6},{8,9},{9,8},{10,11... | collective-permute-start | bytes 786440 | tf_op jit(solution)/shard_map/ppermute | solution.py:344
  23.4 18.2 %collective-permute-start.6 = (bf16[8,128,128]{2,1,0:T(8,128)(2,1)S(1)}, bf16[8,128,128]{2,1,0:T(8,128)(2,1)S(1)}, u32[]{:S(2)}, u32[]{:S(2)}) collective-permute-start(bf16[8,128,128]{2,1,0:T(8,128)(2,1)S(1)} %copy-done.9), channel_id=1, source_target_pairs={{0,2},{2,0},{1,3},{3,1},{4,6},{6,4},{5,7},{7,5},{8,10},{10,8},{9,1... | collective-permute-start | bytes 786440 | tf_op jit(solution)/shard_map/ppermute | solution.py:347
  36.2 5.4 %copy-start.8 = (bf16[8,128,128]{2,1,0:T(8,128)(2,1)S(1)}, bf16[8,128,128]{2,1,0:T(8,128)(2,1)}, u32[]{:S(2)}) copy-start(bf16[8,128,128]{2,1,0:T(8,128)(2,1)} %get-tuple-element.26) | copy-start | bytes 786436
  40.6 2.7 %collective-permute-start.11 = (bf16[10,128,128]{2,1,0:T(8,128)(2,1)S(1)}, bf16[10,128,128]{2,1,0:T(8,128)(2,1)S(1)}, u32[]{:S(2)}, u32[]{:S(2)}) collective-permute-start(bf16[10,128,128]{2,1,0:T(8,128)(2,1)S(1)} %collective-permute-done.8.refs_5_), channel_id=1, source_target_pairs={{0,1},{1,0},{2,3},{3,2},{4,5},{5,4},{6,7},{7,6},{8,9},{9,8},{10,11... | collective-permute-start | bytes 983048 | tf_op jit(solution)/shard_map/ppermute | solution.py:344
  40.8 9.6 %collective-permute-start.13 = (bf16[10,128,128]{2,1,0:T(8,128)(2,1)S(1)}, bf16[10,128,128]{2,1,0:T(8,128)(2,1)S(1)}, u32[]{:S(2)}, u32[]{:S(2)}) collective-permute-start(bf16[10,128,128]{2,1,0:T(8,128)(2,1)S(1)} %collective-permute-done.12.refs_5_), channel_id=1, source_target_pairs={{0,1},{1,0},{2,3},{3,2},{4,5},{5,4},{6,7},{7,6},{8,9},{9,8},{10,11... | collective-permute-start | bytes 983048 | tf_op jit(solution)/shard_map/ppermute | solution.py:344
  41.6 1.8 %collective-permute-start.7 = (bf16[8,128,128]{2,1,0:T(8,128)(2,1)S(1)}, bf16[8,128,128]{2,1,0:T(8,128)(2,1)S(1)}, u32[]{:S(2)}, u32[]{:S(2)}) collective-permute-start(bf16[8,128,128]{2,1,0:T(8,128)(2,1)S(1)} %collective-permute-done.6.refs_2_), channel_id=1, source_target_pairs={{0,1},{1,0},{2,3},{3,2},{4,5},{5,4},{6,7},{7,6},{8,9},{9,8},{10,11... | collective-permute-start | bytes 786440 | tf_op jit(solution)/shard_map/ppermute | solution.py:344
  41.6 8.7 %collective-permute-start.5 = (bf16[8,128,128]{2,1,0:T(8,128)(2,1)S(1)}, bf16[8,128,128]{2,1,0:T(8,128)(2,1)S(1)}, u32[]{:S(2)}, u32[]{:S(2)}) collective-permute-start(bf16[8,128,128]{2,1,0:T(8,128)(2,1)S(1)} %copy-done.8), channel_id=1, source_target_pairs={{0,2},{2,0},{1,3},{3,1},{4,6},{6,4},{5,7},{7,5},{8,10},{10,8},{9,1... | collective-permute-start | bytes 786440 | tf_op jit(solution)/shard_map/ppermute | solution.py:347
  50.3 1.5 %collective-permute-start.14 = (bf16[8,128,128]{2,1,0:T(8,128)(2,1)S(1)}, bf16[8,128,128]{2,1,0:T(8,128)(2,1)S(1)}, u32[]{:S(2)}, u32[]{:S(2)}) collective-permute-start(bf16[8,128,128]{2,1,0:T(8,128)(2,1)S(1)} %collective-permute-done.5.refs_2_), channel_id=1, source_target_pairs={{0,1},{1,0},{2,3},{3,2},{4,5},{5,4},{6,7},{7,6},{8,9},{9,8},{10,11... | collective-permute-start | bytes 786440 | tf_op jit(solution)/shard_map/ppermute | solution.py:344

commit v3 on v2

v3 whole, which is shorter than its diff:
```python
import functools

import jax
import jax.numpy as jnp
from jax import lax
from jax.experimental import pallas as pl
from jax.experimental.pallas import tpu as pltpu
from jax.sharding import PartitionSpec as P

BAND = 2
WIDTH = 2 * BAND + 1
SMEM = pl.BlockSpec(memory_space=pltpu.SMEM)
VMEM = pl.BlockSpec(memory_space=pltpu.VMEM)
ANY = pl.BlockSpec(memory_space=pl.ANY)


def settings(mib):
    return dict(
        compiler_params=pltpu.CompilerParams(vmem_limit_bytes=mib * 2**20),
        cost_estimate=pl.CostEstimate(flops=1, bytes_accessed=1, transcendentals=0),
    )


def cut_kernel(cuts, away, more, a_rows, *refs):
    n = len(cuts)
    offsets = refs[0]
    raw, in_sem, out_sem = refs[-3:]
    outs, bounces = refs[-3 - 2 * n : -3 - n], refs[-3 - n : -3]
    height, tile = a_rows.shape[4:]
    me = lax.axis_index("col")
    d = 1 - me if away else me
    ins, back = [], []
    for i, chosen in enumerate(cuts):
        ins.append(
            [
                pltpu.make_async_copy(
                    a_rows.at[0, 0, d, p],
                    bounces[i].at[pl.ds(j * height, height)],
                    in_sem.at[i, j],
                )
                for j, p in enumerate(chosen)
            ]
        )
        back.append(pltpu.make_async_copy(bounces[i], outs[i], out_sem.at[i]))
    for moves in ins:
        for move in moves:
            move.start()
    if more:
        half, atoms = offsets.shape[3:]
        move = pltpu.make_async_copy(offsets.at[0, 0, d], raw, out_sem.at[0])
        move.start()
        move.wait()
        values = jnp.pad(raw[...].astype(jnp.float32), ((0, 16 - half), (0, tile - atoms)))
        bounces[-1][pl.ds(len(cuts[-1]) * height, 16)] = values.astype(jnp.bfloat16)
    for moves, move_back in zip(ins, back, strict=True):
        for move in moves:
            move.wait()
        move_back.start()
    for move in back:
        move.wait()


def cut(a_rows, cuts, mib, away=True, offsets=None, earlier=()):
    height, tile = a_rows.shape[4:]
    n = len(cuts)
    more = offsets is not None
    shapes = [(len(c) * height + 16 * (more and i == n - 1), tile) for i, c in enumerate(cuts)]
    return pl.pallas_call(
        functools.partial(cut_kernel, cuts, away, more),
        out_shape=tuple(jax.ShapeDtypeStruct(s, a_rows.dtype) for s in shapes),
        in_specs=[ANY] + [ANY] * more + [ANY] * len(earlier),
        out_specs=(ANY,) * n,
        scratch_shapes=[pltpu.VMEM(s, a_rows.dtype) for s in shapes]
        + [
            pltpu.VMEM(offsets.shape[3:] if more else (8, 128), jnp.int32),
            pltpu.SemaphoreType.DMA((n, max(map(len, cuts)))),
            pltpu.SemaphoreType.DMA((n,)),
        ],
        name="cut",
        **settings(mib),
    )(a_rows, *([offsets] if more else []), *earlier)


def choose_kernel(chosen, owner, a_rows, offsets, far, first, second, raw, sem):
    height, tile = a_rows.shape[4:]
    me = lax.axis_index("col")
    mine = owner[0] == me
    split = first.shape[0] // height
    count = len(chosen)

    def run(here):
        if here:
            pairs = []
            for i, p in enumerate(chosen):
                out, at = (first, i) if i < split else (second, i - split)
                pairs.append((a_rows.at[0, 0, me, p], out.at[pl.ds(at * height, height)]))
        else:
            pairs = [
                (far.at[pl.ds(0, split * height)], first),
                (far.at[pl.ds(split * height, second.shape[0])], second),
            ]
        moves = [pltpu.make_async_copy(*p, sem.at[i]) for i, p in enumerate(pairs)]
        for move in moves:
            move.start()
        if here:
            half, atoms = offsets.shape[3:]
            move = pltpu.make_async_copy(offsets.at[0, 0, me], raw, sem.at[count])
            move.start()
            move.wait()
            values = jnp.pad(raw[...].astype(jnp.float32), ((0, 16 - half), (0, tile - atoms)))
            second[pl.ds((count - split) * height, 16)] = values.astype(second.dtype)
        for move in moves:
            move.wait()

    pl.when(mine)(lambda: run(True))
    pl.when(jnp.logical_not(mine))(lambda: run(False))


def choose(owner, a_rows, offsets, far, chosen):
    height, tile = a_rows.shape[4:]
    one = len(chosen) // 2 * height
    shape = lambda n: jax.ShapeDtypeStruct((n, tile), a_rows.dtype)
    return pl.pallas_call(
        functools.partial(choose_kernel, chosen),
        out_shape=(shape(one), shape(far.shape[0] - one)),
        in_specs=[SMEM, ANY, ANY, ANY],
        out_specs=(VMEM, VMEM),
        scratch_shapes=[
            pltpu.VMEM(offsets.shape[3:], jnp.int32),
            pltpu.SemaphoreType.DMA((len(chosen) + 1,)),
        ],
        name="choose",
        **settings(8),
    )(owner, a_rows, offsets, far)


def band_kernel(b_offsets, sizes, place, b_own, b_peer, table, tail, head, total):
    atoms, half, tile, _ = b_own.shape
    blocks = sizes.shape[0]
    start, layer = place[0], place[1]
    row_iota = lax.broadcasted_iota(jnp.int32, (tile, tile), 0)
    col_iota = lax.broadcasted_iota(jnp.int32, (tile, tile), 1)

    def one_row(k, _):
        for w in range(WIDTH):
            total[w] = jnp.zeros((tile, tile), jnp.float32)
        for part, ref in ((layer, b_own), (1 - layer, b_peer)):
            for j in range(half):
                w = b_offsets[k, part * half + j] + BAND
                total[w] = total[w] + ref[k, j].astype(jnp.float32)
        rows = sizes[start + k]
        for w in range(WIDTH):
            cols = sizes[lax.rem(start + k + w + blocks - BAND, blocks)]
            value = jnp.where((row_iota < rows) & (col_iota < cols), total[w], 0.0)
            high = value.astype(jnp.bfloat16)
            table[2 * (k * WIDTH + w)] = high
            table[2 * (k * WIDTH + w) + 1] = (value - high.astype(jnp.float32)).astype(jnp.bfloat16)
        return 0

    lax.fori_loop(0, atoms, one_row, 0)
    pair = 2 * WIDTH
    table[pl.ds(atoms * pair, 2)] = jnp.zeros((2, tile, tile), table.dtype)
    tail[...] = table[pl.ds((atoms - BAND + layer) * pair, pair)]
    head[...] = table[pl.ds(layer * pair, pair)]


def band_sums(b_offsets, sizes, place, b_own, b_peer):
    atoms, half, tile, _ = b_own.shape
    shape = lambda tiles: jax.ShapeDtypeStruct((tiles, tile, tile), jnp.bfloat16)
    return pl.pallas_call(
        band_kernel,
        out_shape=(shape(2 * (atoms * WIDTH + 1)), shape(2 * WIDTH), shape(2 * WIDTH)),
        in_specs=[SMEM, SMEM, SMEM, VMEM, VMEM],
        out_specs=(VMEM, VMEM, VMEM),
        scratch_shapes=[pltpu.VMEM((WIDTH, tile, tile), jnp.float32)],
        name="band_sums",
        **settings(16),
    )(b_offsets, sizes, place, b_own, b_peer)


def join_kernel(table, tail, other_tail, head, other_head, out, sem):
    layer = lax.axis_index("layer")
    pair = 2 * WIDTH
    rows = table.shape[0] // pair
    parts = (
        (table.at[pl.ds(0, rows * pair)], BAND, rows),
        (tail, layer, 1),
        (other_tail, 1 - layer, 1),
        (head, BAND + rows + layer, 1),
        (other_head, BAND + rows + 1 - layer, 1),
    )
    moves = [
        pltpu.make_async_copy(src, out.at[pl.ds(at * pair, n * pair)], sem.at[i])
        for i, (src, at, n) in enumerate(parts)
    ]
    for move in moves:
        move.start()
    out[pl.ds((rows + 2 * BAND) * pair, 2)] = jnp.zeros((2,) + out.shape[1:], out.dtype)
    for move in moves:
        move.wait()


def join(table, tail, head):
    more = 2 * BAND * 2 * WIDTH
    return pl.pallas_call(
        join_kernel,
        out_shape=jax.ShapeDtypeStruct((table.shape[0] + more,) + table.shape[1:], table.dtype),
        in_specs=[ANY] * 5,
        out_specs=VMEM,
        scratch_shapes=[pltpu.SemaphoreType.DMA((5,))],
        name="join",
        **settings(12),
    )(table, *tail, *head)


def plan_kernel(half, owner, sizes, place, c_offsets, own, other, out, raw, spots, sem):
    moves = [
        pltpu.make_async_copy(ref.at[pl.ds(ref.shape[0] - 16, 16)], raw.at[h], sem.at[h])
        for h, ref in enumerate((own, other))
    ]
    for move in moves:
        move.start()
    atoms = c_offsets.shape[0]
    slots = c_offsets.shape[1] // 2
    start, layer, me = place[0], place[1], place[2]
    width = slots * atoms
    iota = lambda dim: lax.broadcasted_iota(jnp.int32, (atoms, width), dim)
    spread = (lax.rem(iota(1), atoms) == iota(0)).astype(jnp.float32)
    pick = lax.broadcasted_iota(jnp.int32, (2 * slots, width), 0)
    slot = lax.broadcasted_iota(jnp.int32, (2 * slots, width), 1) // atoms + layer * slots
    dot = functools.partial(jnp.dot, preferred_element_type=jnp.float32)
    aim = dot(c_offsets[...].astype(jnp.float32), (pick == slot).astype(jnp.float32))
    aim = dot(jnp.ones((2 * half, atoms), jnp.float32), aim * spread)
    for move in moves:
        move.wait()
    shift = [raw[h].astype(jnp.float32)[:half, :atoms] for h in range(2)]
    shift = dot(jnp.concatenate(shift, axis=0), spread)
    shift, aim = shift.astype(jnp.int32), aim.astype(jnp.int32)
    atom = lax.rem(lax.broadcasted_iota(jnp.int32, (2 * half, width), 1), atoms)
    w = aim - shift + BAND
    spots[:, :width] = jnp.where((w >= 0) & (w < WIDTH), (atom + BAND + shift) * WIDTH + w, -1)
    move = pltpu.make_async_copy(spots, out, sem.at[0])
    move.start()
    move.wait()
    for p in range(atoms):
        out[0, width + p] = sizes[start + p]
    out[1, width] = (owner[0] == me).astype(jnp.int32)


def make_plan(owner, sizes, place, c_offsets, half, own, other):
    return pl.pallas_call(
        functools.partial(plan_kernel, half),
        out_shape=jax.ShapeDtypeStruct((2 * half, 128), jnp.int32),
        in_specs=[SMEM] * 3 + [VMEM, ANY, ANY],
        out_specs=SMEM,
        scratch_shapes=[
            pltpu.VMEM((2, 16, 128), jnp.bfloat16),
            pltpu.VMEM((2 * half, 128), jnp.int32),
            pltpu.SemaphoreType.DMA((2,)),
        ],
        name="plan",
        **settings(4),
    )(owner, sizes, place, c_offsets, own, other)


def product_kernel(cfg, plan, *refs):
    refs = list(refs)
    near = refs[: cfg["n_near"]]
    del refs[: cfg["n_near"]]
    far = [refs[2 * i : 2 * i + 2] for i in range(cfg["n_far"])]
    del refs[: 2 * cfg["n_far"]]
    table = refs.pop(0)
    out, a_v, o_v, a_sem, o_sem = refs[cfg["aliased"] :]
    chosen, row0, atoms = cfg["chosen"], cfg["row0"], cfg["atoms"]
    count, slots, tile, _ = o_v.shape
    height = a_v.shape[1] // count
    half = height // tile

    def fetch(pieces):
        moves, at = [], 0
        for pair in pieces:
            n = pair[0].shape[0] // height * height
            for h in range(2):
                move = pltpu.make_async_copy(
                    pair[h].at[pl.ds(0, n)], a_v.at[h, pl.ds(at, n)], a_sem.at[len(moves)]
                )
                moves.append(move)
            at += n
        for move in moves:
            move.start()
        for move in moves:
            move.wait()

    if near:
        mine = plan[1, slots * atoms]
        pl.when(mine == 1)(lambda: fetch([near]))
        pl.when(mine != 1)(lambda: fetch(far))
    else:
        fetch(far)
    zero_at = table.shape[0] // 2 - 1
    row_iota = lax.broadcasted_iota(jnp.int32, (tile, 2 * tile), 0)
    first = [p == chosen[0] + n for n, p in enumerate(chosen)].count(True)
    jump = chosen[-1] - chosen[0] + 1 - count

    def one_atom(n, _):
        p = chosen[0] + n + jnp.where(n < first, 0, jump)

        def factor(t, s):
            at = plan[t, s * atoms + p]
            at = 2 * jnp.where(at < 0, zero_at, at - row0 * WIDTH)
            return jnp.concatenate([table[at], table[at + 1]], axis=0)

        size = plan[0, slots * atoms + p]
        for q in range(slots // 2):
            total = jnp.zeros((tile, 2 * tile), jnp.float32)
            for t in range(2 * half):
                left = a_v[t // half, pl.ds(n * height + t % half * tile, tile)]
                left = jnp.concatenate([left, left], axis=1)
                right = jnp.concatenate([factor(t, 2 * q), factor(t, 2 * q + 1)], axis=1)
                total += jnp.dot(left, right, preferred_element_type=jnp.float32)
            total = jnp.where(row_iota < size, total, 0.0).astype(jnp.bfloat16)
            o_v[n, 2 * q] = total[:, :tile]
            o_v[n, 2 * q + 1] = total[:, tile:]
        pltpu.make_async_copy(o_v.at[n], out.at[p], o_sem.at[n]).start()
        return 0

    lax.fori_loop(0, count, one_atom, 0)
    for n, p in enumerate(chosen):
        pltpu.make_async_copy(o_v.at[n], out.at[p], o_sem.at[n]).wait()


def products(plan, far, table, row0, chosen, slots, atoms, half, near=(), prior=None):
    tile = table.shape[-1]
    count = len(chosen)
    operands = [plan, *near, *[f for pair in far for f in pair], table]
    specs = [SMEM] + [ANY] * (len(operands) - 2) + [VMEM]
    aliases = {}
    if prior is not None:
        aliases = {len(operands): 0}
        operands.append(prior)
        specs.append(ANY)
    cfg = dict(
        atoms=atoms,
        chosen=chosen,
        row0=row0,
        n_near=len(near),
        n_far=len(far),
        aliased=len(aliases),
    )
    return pl.pallas_call(
        functools.partial(product_kernel, cfg),
        out_shape=jax.ShapeDtypeStruct((atoms, slots, tile, tile), jnp.bfloat16),
        in_specs=specs,
        out_specs=ANY,
        scratch_shapes=[
            pltpu.VMEM((2, count * half * tile, tile), jnp.bfloat16),
            pltpu.VMEM((count, slots, tile, tile), jnp.bfloat16),
            pltpu.SemaphoreType.DMA((2 * len(far),)),
            pltpu.SemaphoreType.DMA((count,)),
        ],
        input_output_aliases=aliases,
        name="products",
        **settings(12),
    )(*operands)


def after(x, *others):
    return lax.optimization_barrier((x,) + others)[0]


def local(a_tiles, a_offsets, atom_owner, b_tiles, b_offsets, c_offsets, block_sizes):
    cols = lax.axis_size("col")
    cycle = lax.axis_size("row") * cols
    atoms = atom_owner.shape[0]
    bucket = a_tiles.shape[3]
    slots = c_offsets.shape[1] // 2
    me = lax.axis_index("col")
    layer = lax.axis_index("layer")
    start = (lax.axis_index("row") * cols + me) * atoms
    place = jnp.stack([start, layer, me]).astype(jnp.int32)
    assert atoms * cycle > 8 * BAND and lax.axis_size("layer") == 2 and atoms >= 4 * BAND

    def across(x):
        return lax.ppermute(x, "layer", [(0, 1), (1, 0)])

    def swap(x):
        return lax.ppermute(x, "col", [(0, 1), (1, 0)])

    def onward(x):
        return lax.ppermute(x, ("row", "col"), [(i, (i + 1) % cycle) for i in range(cycle)])

    def back(x):
        return lax.ppermute(x, ("row", "col"), [((i + 1) % cycle, i) for i in range(cycle)])

    half, tile = a_tiles.shape[4:6]
    inner = tuple(range(BAND, atoms - BAND))
    outer = tuple(range(BAND)) + tuple(range(atoms - BAND, atoms))
    offsets = jnp.swapaxes(a_offsets, 3, 4)
    a_rows = a_tiles.reshape(a_tiles.shape[:4] + (half * tile, tile))
    whole = cols == 2 and bucket == atoms
    common = dict(slots=slots, atoms=atoms, half=half)
    if whole:
        (sent,) = cut(a_rows, (inner,), 56, offsets=offsets)
        b_offsets = after(b_offsets, sent)
        b_peer = across(b_tiles)
        own_rows = lax.dynamic_slice_in_dim(b_offsets, start, atoms, 0)
        far = swap(sent)
        table, tail, head = band_sums(own_rows, block_sizes, place, b_tiles, b_peer)
        (rest,) = cut(a_rows, (outer,), 8, earlier=(tail,))
        tail, head = onward(tail), back(head)
        rest = swap(rest)
        far = choose(atom_owner, a_rows, offsets, after(far, table), inner)
        far = [(f, across(f)) for f in far]
        plan = make_plan(atom_owner, block_sizes, place, c_offsets, half, *far[-1])
        c = products(plan, far, table, BAND, inner, **common)
        joined = join(table, (tail, across(tail)), (head, across(head)))
        (near,) = cut(a_rows, (outer,), 8, away=False, earlier=(table,))
        near = (near, across(near))
        rest = after(rest, c, joined)
        rest = [(rest, across(rest))]
        return products(plan, rest, joined, 0, outer, near=near, prior=c, **common)
    b_peer = across(b_tiles)
    own_rows = lax.dynamic_slice_in_dim(b_offsets, start, atoms, 0)
    table, tail, head = band_sums(own_rows, block_sizes, place, b_tiles, b_peer)
    tail, head = onward(tail), back(head)
    received = lax.all_to_all(a_tiles, "col", split_axis=2, concat_axis=1, tiled=True)
    moved = lax.all_to_all(a_offsets, "col", split_axis=2, concat_axis=1, tiled=True)
    received = received.reshape((-1,) + received.shape[4:])
    moved = moved.reshape((-1,) + moved.shape[4:])
    places = jnp.arange(atoms, dtype=jnp.int32)
    same = atom_owner[:, None] == atom_owner[None, :]
    rank = jnp.sum(same & (places[None, :] < places[:, None]), axis=1)
    source = atom_owner * bucket + rank
    rows = jnp.take(received, source, axis=0).reshape(-1, tile)
    shift = jnp.take(moved, source, axis=0).T.astype(jnp.bfloat16)
    rows = jnp.concatenate([rows, jnp.pad(shift, ((0, 16 - half), (0, tile - atoms)))], axis=0)
    other = across(rows)
    plan = make_plan(atom_owner, block_sizes, place, c_offsets, half, rows, other)
    cuts = [p * half * tile for p in (0, BAND, atoms - BAND, atoms)]
    low, mid, top = ((rows[i:j], other[i:j]) for i, j in zip(cuts[:-1], cuts[1:], strict=True))
    c = products(plan, [mid], table, BAND, inner, **common)
    table = join(table, (tail, across(tail)), (head, across(head)))
    return products(plan, [low, top], table, 0, outer, prior=c, **common)


def solution(mesh):
    placed = (
        P(("groups", "row"), "col", None, None, "layer", None, None),
        P(("groups", "row"), "col", None, None, "layer"),
        P(("groups", "row", "col")),
        P(("groups", "row", "col"), "layer", None, None),
        P("groups", None),
        P(("groups", "row", "col"), None),
        P("groups"),
    )
    return jax.shard_map(
        local,
        mesh=mesh,
        in_specs=placed,
        out_specs=P(("groups", "row", "col"), "layer", None, None),
        check_vma=False,
    )
```

time: 55.5 us -> 48.4 us (0.87)
  starting transfers between devices: 20.8 us -> 8.91 us
  waiting for transfers between devices: 11 us -> 20.6 us
  Pallas kernels: 22.3 us -> 16.9 us
  local copies, waits for them, and re-layouts: 0.82 us -> 1.53 us
    ppermute x1, waiting for transfers between devices: 0.01 us -> 16.4 us  [onward(): lax.ppermute(x, ('row', 'col'), [(i, (i + 1) % cycle) for i in range(cycl...]
    ppermute x4 -> x2, starting transfers between devices: 14.2 us -> 2.65 us  [swap(): return lax.ppermute(x, 'col', [(0, 1), (1, 0)])]
    pallas_call x3 -> x2, Pallas kernels: 11.1 us -> 6.45 us  [products(): pl.pallas_call(functools.partial(product_kernel, cfg), out_shape=jax.Shap...]
    ppermute x4 -> x2, waiting for transfers between devices: 5.27 us -> 1.47 us  [swap(): return lax.ppermute(x, 'col', [(0, 1), (1, 0)])]
    ppermute x9 -> x7, waiting for transfers between devices: 5.73 us -> 2.26 us  [across(): return lax.ppermute(x, 'layer', [(0, 1), (1, 0)])]
    unnamed x21 -> x14, local copies, waits for them, and re-layouts: 0.73 us -> 1.43 us
    pallas_call x3 -> x6, Pallas kernels: 7.82 us -> 7.54 us  [the longest x3 3.4 us: cut(): pl.pallas_call(functools.partial(cut_kernel, cuts, away, more), out_shape...]
    ppermute x9 -> x7, starting transfers between devices: 1.52 us -> 1.49 us  [across(): return lax.ppermute(x, 'layer', [(0, 1), (1, 0)])]
  transfers between devices with their start and end apart: 15 -> 11, of which waited for: 7 -> 5; matrix products, arithmetic and copies ran while one was open for 0% -> 0% of each run, Pallas kernels for 26% -> 28%
where the time goes in v3:
time: 48.4 us; the launch traced here: 48.3 us
  waiting for transfers between devices  20.6 us (43%)
  Pallas kernels  16.9 us (35%)
  starting transfers between devices  8.91 us (18%)
  local copies, waits for them, and re-layouts  1.53 us (3%)
    ppermute x1, waiting for transfers between devices, onward(): lax.ppermute(x, ('row', 'col'), [(i, (i + 1) % cycle) for i in range(cycl...  16.4 us
    pallas_call x2, Pallas kernels, products(): pl.pallas_call(functools.partial(product_kernel, cfg), out_shape=jax.Shap...  6.45 us
    pallas_call x3, Pallas kernels, cut(): pl.pallas_call(functools.partial(cut_kernel, cuts, away, more), out_shape...  3.4 us
    ppermute x1, starting transfers between devices, back(): lax.ppermute(x, ('row', 'col'), [((i + 1) % cycle, i) for i in range(cycl...  3.2 us
    pallas_call x1, Pallas kernels, band_sums(): pl.pallas_call(band_kernel, out_shape=(shape(2 * (atoms * WIDTH + 1)), sh...  2.95 us
    ppermute x2, starting transfers between devices, swap(): return lax.ppermute(x, 'col', [(0, 1), (1, 0)])  2.65 us
    ppermute x7, waiting for transfers between devices, across(): return lax.ppermute(x, 'layer', [(0, 1), (1, 0)])  2.26 us
    pallas_call x1, Pallas kernels, make_plan(): pl.pallas_call(functools.partial(plan_kernel, half), out_shape=jax.ShapeD...  2.2 us
  transfers between devices with their start and end apart: 11, of which 5 were waited for; matrix products, arithmetic and copies ran while one was open for 0% of the time, Pallas kernels for 28%

profile of v3, /device:TPU:0, one launch (start us, length us, event | category | flops | bytes accessed | tf_op | source)
XLA Modules:
  0.0 48.3 jit_solution(3546393990769389987)
XLA Ops:
  0.0 0.5 collective-permute-start.1
  0.5 1.9 %cut.3 = bf16[2064,128]{1,0:T(8,128)(2,1)} custom-call(bf16[1,1,2,8,512,128]{5,4,3,2,1,0:T(8,128)(2,1)} %bitcast.5, s32[1,1,2,4,8]{4,3,2,1,0:T(4,128)} %bitcast.9), custom_call_target="tpu_custom_call" | custom-call | flops 1 | bytes 1 | tf_op jit(solution)/shard_map/cut/pallas_call | solution.py:68
  2.4 0.0 copy-start
  2.4 2.6 %collective-permute-start = (bf16[2064,128]{1,0:T(8,128)(2,1)}, bf16[2064,128]{1,0:T(8,128)(2,1)S(1)}, u32[]{:S(2)}, u32[]{:S(2)}) collective-permute-start(bf16[2064,128]{1,0:T(8,128)(2,1)} %cut.3), channel_id=1, source_target_pairs={{0,2},{2,0},{1,3},{3,1},{4,6},{6,4},{5,7},{7,5},{8,10},{10,8},{9,1... | collective-permute-start | bytes 1585160 | tf_op jit(solution)/shard_map/ppermute | solution.py:387
  5.0 0.1 pad_add_fusion.place
  5.1 0.1 copy.9
  5.2 0.0 collective-permute-done.1.b_peer
  5.2 0.0 copy-start.1
  5.2 1.4 %copy-done.1 = bf16[8,6,128,128]{3,2,1,0:T(8,128)(2,1)S(1)} copy-done((bf16[8,6,128,128]{3,2,1,0:T(8,128)(2,1)S(1)}, bf16[8,6,128,128]{3,2,1,0:T(8,128)(2,1)}, u32[]{:S(2)}) %copy-start.1) | copy-done | bytes 1572888
  6.6 2.9 %band_sums.1 = (bf16[82,128,128]{2,1,0:T(8,128)(2,1)S(1)}, bf16[10,128,128]{2,1,0:T(8,128)(2,1)S(1)}, bf16[10,128,128]{2,1,0:T(8,128)(2,1)S(1)}) custom-call(s32[8,12]{1,0:T(8,128)S(1)} %constant_dynamic-slice_fusion.b_offsets, s32[64]{0:T(128)S(1)} %copy-done.4, s32[3]{0:T(128)S(1)} %pad_add_fusion.place, bf16[8,6,128,128]{3,2,1,0:T(8,128)(2,1)S(1)} %copy-done.1, ...), custom_call_target="tpu_custom_call" | custom-call | flops 1 | bytes 1 | tf_op jit(solution)/shard_map/band_sums/pallas_call | solution.py:170
  9.5 0.0 copy-start.2
  9.6 0.0 copy-start.5
  9.6 1.6 %collective-permute-start.6 = (bf16[10,128,128]{2,1,0:T(8,128)(2,1)S(1)}, bf16[10,128,128]{2,1,0:T(8,128)(2,1)S(1)}, u32[]{:S(2)}, u32[]{:S(2)}) collective-permute-start(bf16[10,128,128]{2,1,0:T(8,128)(2,1)S(1)} %get-tuple-element.17.refs_0_), channel_id=1, source_target_pairs={{0,2},{2,4},{4,6},{6,8},{8,10},{10,12},{12,14},{14,0},{1,3},{3,5},... | collective-permute-start | bytes 983048 | tf_op jit(solution)/shard_map/ppermute | solution.py:390
  11.1 3.2 %collective-permute-start.8 = (bf16[10,128,128]{2,1,0:T(8,128)(2,1)S(1)}, bf16[10,128,128]{2,1,0:T(8,128)(2,1)S(1)}, u32[]{:S(2)}, u32[]{:S(2)}) collective-permute-start(bf16[10,128,128]{2,1,0:T(8,128)(2,1)S(1)} %get-tuple-element.19), channel_id=1, source_target_pairs={{2,0},{4,2},{6,4},{8,6},{10,8},{12,10},{14,12},{0,14},{3,1},{5,3},... | collective-permute-start | bytes 983048 | tf_op jit(solution)/shard_map/ppermute | solution.py:393
  14.3 0.7 %cut.5 = bf16[2048,128]{1,0:T(8,128)(2,1)S(1)} custom-call(bf16[1,1,2,8,512,128]{5,4,3,2,1,0:T(8,128)(2,1)S(1)} %bitcast.6, bf16[10,128,128]{2,1,0:T(8,128)(2,1)S(1)} %get-tuple-element.17.refs_0_), custom_call_target="tpu_custom_call" | custom-call | flops 1 | bytes 1 | tf_op jit(solution)/shard_map/cut/pallas_call | solution.py:68
  15.1 0.1 collective-permute-start.4
  15.2 16.4 %collective-permute-done.6.tail = bf16[10,128,128]{2,1,0:T(8,128)(2,1)S(1)} collective-permute-done((bf16[10,128,128]{2,1,0:T(8,128)(2,1)S(1)}, bf16[10,128,128]{2,1,0:T(8,128)(2,1)S(1)}, u32[]{:S(2)}, u32[]{:S(2)}) %collective-permute-start.6) | collective-permute-done | bytes 327712 | tf_op jit(solution)/shard_map/ppermute | solution.py:390
  31.6 0.5 %collective-permute-done.8.head = bf16[10,128,128]{2,1,0:T(8,128)(2,1)S(1)} collective-permute-done((bf16[10,128,128]{2,1,0:T(8,128)(2,1)S(1)}, bf16[10,128,128]{2,1,0:T(8,128)(2,1)S(1)}, u32[]{:S(2)}, u32[]{:S(2)}) %collective-permute-start.8) | collective-permute-done | bytes 327712 | tf_op jit(solution)/shard_map/ppermute | solution.py:393
  32.1 0.0 collective-permute-start.9
  32.1 0.0 collective-permute-done.far
  32.1 1.3 %choose.1 = (bf16[1024,128]{1,0:T(8,128)(2,1)S(1)}, bf16[1040,128]{1,0:T(8,128)(2,1)S(1)}) custom-call(s32[8]{0:T(128)S(1)} %copy-done.5, bf16[1,1,2,8,512,128]{5,4,3,2,1,0:T(8,128)(2,1)S(1)} %bitcast.7, s32[1,1,2,4,8]{4,3,2,1,0:T(4,128)S(1)} %bitcast.10, bf16[2064,128]{1,0:T(8,128)(2,1)S(1)} %collective-permute-done.far), custom_call_target="tpu_custom_call" | custom-call | flops 1 | bytes 1 | tf_op jit(solution)/shard_map/choose/pallas_call | solution.py:123
  33.4 0.6 %collective-permute-start.2 = (bf16[1040,128]{1,0:T(8,128)(2,1)S(1)}, bf16[1040,128]{1,0:T(8,128)(2,1)S(1)}, u32[]{:S(2)}, u32[]{:S(2)}) collective-permute-start(bf16[1040,128]{1,0:T(8,128)(2,1)S(1)} %get-tuple-element.16.own.refs_2_), channel_id=1, source_target_pairs={{0,1},{1,0},{2,3},{3,2},{4,5},{5,4},{6,7},{7,6},{8,9},{9,8},{10,11... | collective-permute-start | bytes 798728 | tf_op jit(solution)/shard_map/ppermute | solution.py:384
  34.0 0.1 collective-permute-start.5
  34.1 0.7 %cut.4.refs_0_ = bf16[2048,128]{1,0:T(8,128)(2,1)S(1)} custom-call(bf16[1,1,2,8,512,128]{5,4,3,2,1,0:T(8,128)(2,1)S(1)} %bitcast.8, bf16[82,128,128]{2,1,0:T(8,128)(2,1)S(1)} %get-tuple-element.14.refs_0_.refs_4_.table), custom_call_target="tpu_custom_call" | custom-call | flops 1 | bytes 1 | tf_op jit(solution)/shard_map/cut/pallas_call | solution.py:68
  34.8 0.3 collective-permute-done.2.other.refs_3_
  35.2 0.4 collective-permute-start.3
  35.5 2.2 %plan.1 = s32[8,128]{1,0:T(8,128)S(1)} custom-call(s32[8]{0:T(128)S(1)} %copy-done.5, s32[64]{0:T(128)S(1)} %copy-done.4, s32[3]{0:T(128)S(1)} %pad_add_fusion.place, s32[8,8]{1,0:T(8,128)S(1)} %copy-done.3, bf16[1040,128]{1,0:T(8,128)(2,1)S(1)} %get-tuple-element.16.own.refs_2_, bf16[1040,128]{1,0:T(8,128)(2,1)S(1)} %collective-permute-done.2.other.refs_3_), custom_call_target="tpu_custom_call" | custom-call | flops 1 | bytes 1 | tf_op jit(solution)/shard_map/plan/pallas_call | solution.py:251
  37.7 3.2 %products.2.refs_5_ = bf16[8,4,128,128]{3,2,1,0:T(8,128)(2,1)} custom-call(s32[8,128]{1,0:T(8,128)S(1)} %plan.1, bf16[1024,128]{1,0:T(8,128)(2,1)S(1)} %get-tuple-element.18.refs_0_, bf16[1024,128]{1,0:T(8,128)(2,1)S(1)} %collective-permute-done.5.refs_1_, bf16[1040,128]{1,0:T(8,128)(2,1)S(1)} %get-tuple-element.16.own.refs_2_, ...), custom_call_target="tpu_custom_call" | custom-call | flops 1 | bytes 1 | tf_op jit(solution)/shard_map/products/pallas_call | solution.py:350
  41.0 0.7 %join.1.refs_4_ = bf16[122,128,128]{2,1,0:T(8,128)(2,1)S(1)} custom-call(bf16[82,128,128]{2,1,0:T(8,128)(2,1)S(1)} %get-tuple-element.14.refs_0_.refs_4_.table, bf16[10,128,128]{2,1,0:T(8,128)(2,1)S(1)} %collective-permute-done.6.tail, bf16[10,128,128]{2,1,0:T(8,128)(2,1)S(1)} %collective-permute-done.7.other_tail, ...), custom_call_target="tpu_custom_call" | custom-call | flops 1 | bytes 1 | tf_op jit(solution)/shard_map/join/pallas_call | solution.py:205
  41.7 1.5 %collective-permute-done.4.refs_2_ = bf16[2048,128]{1,0:T(8,128)(2,1)S(1)} collective-permute-done((bf16[2048,128]{1,0:T(8,128)(2,1)S(1)}, bf16[2048,128]{1,0:T(8,128)(2,1)S(1)}, u32[]{:S(2)}, u32[]{:S(2)}) %collective-permute-start.4) | collective-permute-done | bytes 524320 | tf_op jit(solution)/shard_map/ppermute | solution.py:387
  43.1 1.9 %collective-permute-done.10.refs_3_ = bf16[2048,128]{1,0:T(8,128)(2,1)S(1)} collective-permute-done((bf16[2048,128]{1,0:T(8,128)(2,1)S(1)}, bf16[2048,128]{1,0:T(8,128)(2,1)S(1)}, u32[]{:S(2)}, u32[]{:S(2)}) %collective-permute-start.10) | collective-permute-done | bytes 524320 | tf_op jit(solution)/shard_map/ppermute | solution.py:384
  45.0 3.2 %products.3 = bf16[8,4,128,128]{3,2,1,0:T(8,128)(2,1)} custom-call(s32[8,128]{1,0:T(8,128)S(1)} %plan.1, bf16[2048,128]{1,0:T(8,128)(2,1)S(1)} %cut.4.refs_0_, bf16[2048,128]{1,0:T(8,128)(2,1)S(1)} %collective-permute-done.3.refs_1_, bf16[2048,128]{1,0:T(8,128)(2,1)S(1)} %collective-permute-done.4.refs_2_, ...), custom_call_target="tpu_custom_call", output_to_operand_aliasing={{}: (6, {})} | custom-call | flops 1 | bytes 1 | tf_op jit(solution)/shard_map/products/pallas_call | solution.py:350
  (16 shorter events, 0.0 us)
Async XLA Ops:
  0.0 5.1 %copy-start.6 = (s32[64,12]{0,1:T(8,128)S(1)}, s32[64,12]{0,1:T(8,128)}, u32[]{:S(2)}) copy-start(s32[64,12]{0,1:T(8,128)} %param.11) | copy-start | bytes 9220
  0.0 5.2 %copy-start.4 = (s32[64]{0:T(128)S(1)}, s32[64]{0:T(128)}, u32[]{:S(2)}) copy-start(s32[64]{0:T(128)} %sizes.3) | copy-start | bytes 772
  0.0 5.2 %collective-permute-start.1 = (bf16[8,6,128,128]{3,2,1,0:T(8,128)(2,1)}, bf16[8,6,128,128]{3,2,1,0:T(8,128)(2,1)}, u32[]{:S(2)}, u32[]{:S(2)}) collective-permute-start(bf16[8,6,128,128]{3,2,1,0:T(8,128)(2,1)} %b_own.1), channel_id=1, source_target_pairs={{0,1},{1,0},{2,3},{3,2},{4,5},{5,4},{6,7},{7,6},{8,9},{9,8},{10,11... | collective-permute-start | bytes 4718600 | tf_op jit(solution)/shard_map/ppermute | solution.py:384
  2.4 12.0 %copy-start = (bf16[1,1,2,8,4,128,128]{6,5,4,3,2,1,0:T(8,128)(2,1)S(1)}, bf16[1,1,2,8,4,128,128]{6,5,4,3,2,1,0:T(8,128)(2,1)}, u32[]{:S(2)}) copy-start(bf16[1,1,2,8,4,128,128]{6,5,4,3,2,1,0:T(8,128)(2,1)} %param.7) | copy-start | bytes 6291460
  2.4 29.7 %collective-permute-start = (bf16[2064,128]{1,0:T(8,128)(2,1)}, bf16[2064,128]{1,0:T(8,128)(2,1)S(1)}, u32[]{:S(2)}, u32[]{:S(2)}) collective-permute-start(bf16[2064,128]{1,0:T(8,128)(2,1)} %cut.3), channel_id=1, source_target_pairs={{0,2},{2,0},{1,3},{3,1},{4,6},{6,4},{5,7},{7,5},{8,10},{10,8},{9,1... | collective-permute-start | bytes 1585160 | tf_op jit(solution)/shard_map/ppermute | solution.py:387
  5.2 1.4 %copy-start.1 = (bf16[8,6,128,128]{3,2,1,0:T(8,128)(2,1)S(1)}, bf16[8,6,128,128]{3,2,1,0:T(8,128)(2,1)}, u32[]{:S(2)}) copy-start(bf16[8,6,128,128]{3,2,1,0:T(8,128)(2,1)} %b_own.1) | copy-start | bytes 4718596
  9.5 22.6 %copy-start.2 = (s32[1,1,2,8,4]{3,4,2,1,0:T(4,128)S(1)}, s32[1,1,2,8,4]{3,4,2,1,0:T(4,128)}, u32[]{:S(2)}) copy-start(s32[1,1,2,8,4]{3,4,2,1,0:T(4,128)} %param.8) | copy-start | bytes 772
  9.6 22.6 %copy-start.5 = (s32[8]{0:T(128)S(1)}, s32[8]{0:T(128)}, u32[]{:S(2)}) copy-start(s32[8]{0:T(128)} %owner.3) | copy-start | bytes 100
  9.6 22.0 %collective-permute-start.6 = (bf16[10,128,128]{2,1,0:T(8,128)(2,1)S(1)}, bf16[10,128,128]{2,1,0:T(8,128)(2,1)S(1)}, u32[]{:S(2)}, u32[]{:S(2)}) collective-permute-start(bf16[10,128,128]{2,1,0:T(8,128)(2,1)S(1)} %get-tuple-element.17.refs_0_), channel_id=1, source_target_pairs={{0,2},{2,4},{4,6},{6,8},{8,10},{10,12},{12,14},{14,0},{1,3},{3,5},... | collective-permute-start | bytes 983048 | tf_op jit(solution)/shard_map/ppermute | solution.py:390
  11.1 21.0 %collective-permute-start.8 = (bf16[10,128,128]{2,1,0:T(8,128)(2,1)S(1)}, bf16[10,128,128]{2,1,0:T(8,128)(2,1)S(1)}, u32[]{:S(2)}, u32[]{:S(2)}) collective-permute-start(bf16[10,128,128]{2,1,0:T(8,128)(2,1)S(1)} %get-tuple-element.19), channel_id=1, source_target_pairs={{2,0},{4,2},{6,4},{8,6},{10,8},{12,10},{14,12},{0,14},{3,1},{5,3},... | collective-permute-start | bytes 983048 | tf_op jit(solution)/shard_map/ppermute | solution.py:393
  15.1 28.0 %collective-permute-start.4 = (bf16[2048,128]{1,0:T(8,128)(2,1)S(1)}, bf16[2048,128]{1,0:T(8,128)(2,1)S(1)}, u32[]{:S(2)}, u32[]{:S(2)}) collective-permute-start(bf16[2048,128]{1,0:T(8,128)(2,1)S(1)} %cut.5), channel_id=1, source_target_pairs={{0,2},{2,0},{1,3},{3,1},{4,6},{6,4},{5,7},{7,5},{8,10},{10,8},{9,1... | collective-permute-start | bytes 1572872 | tf_op jit(solution)/shard_map/ppermute | solution.py:387
  31.6 9.4 %collective-permute-start.7 = (bf16[10,128,128]{2,1,0:T(8,128)(2,1)S(1)}, bf16[10,128,128]{2,1,0:T(8,128)(2,1)S(1)}, u32[]{:S(2)}, u32[]{:S(2)}) collective-permute-start(bf16[10,128,128]{2,1,0:T(8,128)(2,1)S(1)} %collective-permute-done.6.tail), channel_id=1, source_target_pairs={{0,1},{1,0},{2,3},{3,2},{4,5},{5,4},{6,7},{7,6},{8,9},{9,8},{10,11... | collective-permute-start | bytes 983048 | tf_op jit(solution)/shard_map/ppermute | solution.py:384
  32.1 8.9 %collective-permute-start.9 = (bf16[10,128,128]{2,1,0:T(8,128)(2,1)S(1)}, bf16[10,128,128]{2,1,0:T(8,128)(2,1)S(1)}, u32[]{:S(2)}, u32[]{:S(2)}) collective-permute-start(bf16[10,128,128]{2,1,0:T(8,128)(2,1)S(1)} %collective-permute-done.8.head), channel_id=1, source_target_pairs={{0,1},{1,0},{2,3},{3,2},{4,5},{5,4},{6,7},{7,6},{8,9},{9,8},{10,11... | collective-permute-start | bytes 983048 | tf_op jit(solution)/shard_map/ppermute | solution.py:384
  33.4 1.7 %collective-permute-start.2 = (bf16[1040,128]{1,0:T(8,128)(2,1)S(1)}, bf16[1040,128]{1,0:T(8,128)(2,1)S(1)}, u32[]{:S(2)}, u32[]{:S(2)}) collective-permute-start(bf16[1040,128]{1,0:T(8,128)(2,1)S(1)} %get-tuple-element.16.own.refs_2_), channel_id=1, source_target_pairs={{0,1},{1,0},{2,3},{3,2},{4,5},{5,4},{6,7},{7,6},{8,9},{9,8},{10,11... | collective-permute-start | bytes 798728 | tf_op jit(solution)/shard_map/ppermute | solution.py:384
  34.0 1.5 %copy-start.3 = (s32[8,8]{1,0:T(8,128)S(1)}, s32[8,8]{1,0:T(8,128)}, u32[]{:S(2)}) copy-start(s32[8,8]{1,0:T(8,128)} %c_offsets.1) | copy-start | bytes 772
  34.0 3.8 %collective-permute-start.5 = (bf16[1024,128]{1,0:T(8,128)(2,1)S(1)}, bf16[1024,128]{1,0:T(8,128)(2,1)S(1)}, u32[]{:S(2)}, u32[]{:S(2)}) collective-permute-start(bf16[1024,128]{1,0:T(8,128)(2,1)S(1)} %get-tuple-element.18.refs_0_), channel_id=1, source_target_pairs={{0,1},{1,0},{2,3},{3,2},{4,5},{5,4},{6,7},{7,6},{8,9},{9,8},{10,11... | collective-permute-start | bytes 786440 | tf_op jit(solution)/shard_map/ppermute | solution.py:384
  35.2 8.0 %collective-permute-start.3 = (bf16[2048,128]{1,0:T(8,128)(2,1)S(1)}, bf16[2048,128]{1,0:T(8,128)(2,1)S(1)}, u32[]{:S(2)}, u32[]{:S(2)}) collective-permute-start(bf16[2048,128]{1,0:T(8,128)(2,1)S(1)} %cut.4.refs_0_), channel_id=1, source_target_pairs={{0,1},{1,0},{2,3},{3,2},{4,5},{5,4},{6,7},{7,6},{8,9},{9,8},{10,11... | collective-permute-start | bytes 1572872 | tf_op jit(solution)/shard_map/ppermute | solution.py:384
  43.1 1.9 %collective-permute-start.10 = (bf16[2048,128]{1,0:T(8,128)(2,1)S(1)}, bf16[2048,128]{1,0:T(8,128)(2,1)S(1)}, u32[]{:S(2)}, u32[]{:S(2)}) collective-permute-start(bf16[2048,128]{1,0:T(8,128)(2,1)S(1)} %collective-permute-done.4.refs_2_), channel_id=1, source_target_pairs={{0,1},{1,0},{2,3},{3,2},{4,5},{5,4},{6,7},{7,6},{8,9},{9,8},{10,11... | collective-permute-start | bytes 1572872 | tf_op jit(solution)/shard_map/ppermute | solution.py:384

commit v4 on v3

--- a/solution.py
+++ b/solution.py
@@ -21,67 +21,44 @@
     )
 
 
-def cut_kernel(cuts, away, more, a_rows, *refs):
-    n = len(cuts)
-    offsets = refs[0]
-    raw, in_sem, out_sem = refs[-3:]
-    outs, bounces = refs[-3 - 2 * n : -3 - n], refs[-3 - n : -3]
-    height, tile = a_rows.shape[4:]
+def cut_kernel(chosen, away, a_rows, *refs):
+    out, held, in_sem, out_sem = refs[-4:]
+    height = a_rows.shape[4]
     me = lax.axis_index("col")
     d = 1 - me if away else me
-    ins, back = [], []
-    for i, chosen in enumerate(cuts):
-        ins.append(
-            [
-                pltpu.make_async_copy(
-                    a_rows.at[0, 0, d, p],
-                    bounces[i].at[pl.ds(j * height, height)],
-                    in_sem.at[i, j],
-                )
-                for j, p in enumerate(chosen)
-            ]
+    moves = [
+        pltpu.make_async_copy(
+            a_rows.at[0, 0, d, p], held.at[pl.ds(j * height, height)], in_sem.at[j]
         )
-        back.append(pltpu.make_async_copy(bounces[i], outs[i], out_sem.at[i]))
-    for moves in ins:
-        for move in moves:
-            move.start()
-    if more:
-        half, atoms = offsets.shape[3:]
-        move = pltpu.make_async_copy(offsets.at[0, 0, d], raw, out_sem.at[0])
+        for j, p in enumerate(chosen)
+    ]
+    for move in moves:
         move.start()
+    for move in moves:
         move.wait()
-        values = jnp.pad(raw[...].astype(jnp.float32), ((0, 16 - half), (0, tile - atoms)))
-        bounces[-1][pl.ds(len(cuts[-1]) * height, 16)] = values.astype(jnp.bfloat16)
-    for moves, move_back in zip(ins, back, strict=True):
-        for move in moves:
-            move.wait()
-        move_back.start()
-    for move in back:
-        move.wait()
-
-
-def cut(a_rows, cuts, mib, away=True, offsets=None, earlier=()):
-    height, tile = a_rows.shape[4:]
-    n = len(cuts)
-    more = offsets is not None
-    shapes = [(len(c) * height + 16 * (more and i == n - 1), tile) for i, c in enumerate(cuts)]
-    return pl.pallas_call(
-        functools.partial(cut_kernel, cuts, away, more),
-        out_shape=tuple(jax.ShapeDtypeStruct(s, a_rows.dtype) for s in shapes),
-        in_specs=[ANY] + [ANY] * more + [ANY] * len(earlier),
-        out_specs=(ANY,) * n,
-        scratch_shapes=[pltpu.VMEM(s, a_rows.dtype) for s in shapes]
-        + [
-            pltpu.VMEM(offsets.shape[3:] if more else (8, 128), jnp.int32),
-            pltpu.SemaphoreType.DMA((n, max(map(len, cuts)))),
-            pltpu.SemaphoreType.DMA((n,)),
+    back = pltpu.make_async_copy(held, out, out_sem)
+    back.start()
+    back.wait()
+
+
+def cut(a_rows, chosen, earlier, away=True):
+    shape = jax.ShapeDtypeStruct((len(chosen) * a_rows.shape[4], a_rows.shape[5]), a_rows.dtype)
+    return pl.pallas_call(
+        functools.partial(cut_kernel, chosen, away),
+        out_shape=shape,
+        in_specs=[ANY, ANY],
+        out_specs=ANY,
+        scratch_shapes=[
+            pltpu.VMEM(shape.shape, shape.dtype),
+            pltpu.SemaphoreType.DMA((len(chosen),)),
+            pltpu.SemaphoreType.DMA,
         ],
         name="cut",
-        **settings(mib),
-    )(a_rows, *([offsets] if more else []), *earlier)
-
-
-def choose_kernel(chosen, owner, a_rows, offsets, far, first, second, raw, sem):
+        **settings(8),
+    )(a_rows, earlier)
+
+
+def choose_kernel(chosen, owner, a_rows, offsets, far, tail, head, first, second, raw, sem):
     height, tile = a_rows.shape[4:]
     me = lax.axis_index("col")
     mine = owner[0] == me
@@ -95,9 +72,10 @@
                 out, at = (first, i) if i < split else (second, i - split)
                 pairs.append((a_rows.at[0, 0, me, p], out.at[pl.ds(at * height, height)]))
         else:
+            n = (count - split) * height
             pairs = [
                 (far.at[pl.ds(0, split * height)], first),
-                (far.at[pl.ds(split * height, second.shape[0])], second),
+                (far.at[pl.ds(split * height, n)], second.at[pl.ds(0, n)]),
             ]
         moves = [pltpu.make_async_copy(*p, sem.at[i]) for i, p in enumerate(pairs)]
         for move in moves:
@@ -109,6 +87,16 @@
             move.wait()
             values = jnp.pad(raw[...].astype(jnp.float32), ((0, 16 - half), (0, tile - atoms)))
             second[pl.ds((count - split) * height, 16)] = values.astype(second.dtype)
+        else:
+            def ends(ref):
+                src = ref.at[pl.ds(ref.shape[0] - 16, 16)]
+                dst = second.at[pl.ds((count - split) * height, 16)]
+                move = pltpu.make_async_copy(src, dst, sem.at[count])
+                move.start()
+                move.wait()
+
+            pl.when(me == 0)(lambda: ends(head))
+            pl.when(me != 0)(lambda: ends(tail))
         for move in moves:
             move.wait()
 
@@ -116,14 +104,14 @@
     pl.when(jnp.logical_not(mine))(lambda: run(False))
 
 
-def choose(owner, a_rows, offsets, far, chosen):
+def choose(owner, a_rows, offsets, far, tail, head, chosen):
     height, tile = a_rows.shape[4:]
     one = len(chosen) // 2 * height
     shape = lambda n: jax.ShapeDtypeStruct((n, tile), a_rows.dtype)
     return pl.pallas_call(
         functools.partial(choose_kernel, chosen),
-        out_shape=(shape(one), shape(far.shape[0] - one)),
-        in_specs=[SMEM, ANY, ANY, ANY],
+        out_shape=(shape(one), shape(far.shape[0] - one + 16)),
+        in_specs=[SMEM] + [ANY] * 5,
         out_specs=(VMEM, VMEM),
         scratch_shapes=[
             pltpu.VMEM(offsets.shape[3:], jnp.int32),
@@ -131,10 +119,10 @@
         ],
         name="choose",
         **settings(8),
-    )(owner, a_rows, offsets, far)
-
-
-def band_kernel(b_offsets, sizes, place, b_own, b_peer, table, tail, head, total):
+    )(owner, a_rows, offsets, far, tail, head)
+
+
+def band_kernel(b_offsets, sizes, place, offsets, b_own, b_peer, table, tail, head, total):
     atoms, half, tile, _ = b_own.shape
     blocks = sizes.shape[0]
     start, layer = place[0], place[1]
@@ -153,58 +141,68 @@
             cols = sizes[lax.rem(start + k + w + blocks - BAND, blocks)]
             value = jnp.where((row_iota < rows) & (col_iota < cols), total[w], 0.0)
             high = value.astype(jnp.bfloat16)
-            table[2 * (k * WIDTH + w)] = high
-            table[2 * (k * WIDTH + w) + 1] = (value - high.astype(jnp.float32)).astype(jnp.bfloat16)
+            at = 2 * tile * (k * WIDTH + w)
+            table[pl.ds(at, tile)] = high
+            table[pl.ds(at + tile, tile)] = (value - high.astype(jnp.float32)).astype(jnp.bfloat16)
         return 0
 
     lax.fori_loop(0, atoms, one_row, 0)
-    pair = 2 * WIDTH
-    table[pl.ds(atoms * pair, 2)] = jnp.zeros((2, tile, tile), table.dtype)
-    tail[...] = table[pl.ds((atoms - BAND + layer) * pair, pair)]
-    head[...] = table[pl.ds(layer * pair, pair)]
-
-
-def band_sums(b_offsets, sizes, place, b_own, b_peer):
+    height = 2 * WIDTH * tile
+    table[pl.ds(atoms * height, 2 * tile)] = jnp.zeros((2 * tile, tile), table.dtype)
+    places = offsets.shape[3:]
+    there = 1 - place[2] if offsets.shape[2] == 2 else 0
+    values = offsets[0, 0, pl.ds(there, 1)].reshape(places).astype(jnp.float32)
+    values = jnp.pad(values, ((0, 16 - places[0]), (0, tile - places[1]))).astype(jnp.bfloat16)
+    for out, row in ((tail, atoms - BAND + layer), (head, layer)):
+        out[pl.ds(0, height)] = table[pl.ds(row * height, height)]
+        out[pl.ds(height, 16)] = values
+
+
+def band_sums(b_offsets, sizes, place, offsets, b_own, b_peer):
     atoms, half, tile, _ = b_own.shape
-    shape = lambda tiles: jax.ShapeDtypeStruct((tiles, tile, tile), jnp.bfloat16)
+    shape = lambda *dims: jax.ShapeDtypeStruct(dims + (tile,), jnp.bfloat16)
+    row = shape(2 * WIDTH * tile + 16)
     return pl.pallas_call(
         band_kernel,
-        out_shape=(shape(2 * (atoms * WIDTH + 1)), shape(2 * WIDTH), shape(2 * WIDTH)),
-        in_specs=[SMEM, SMEM, SMEM, VMEM, VMEM],
+        out_shape=(shape(2 * (atoms * WIDTH + 1) * tile), row, row),
+        in_specs=[SMEM, SMEM, SMEM, VMEM, VMEM, VMEM],
         out_specs=(VMEM, VMEM, VMEM),
         scratch_shapes=[pltpu.VMEM((WIDTH, tile, tile), jnp.float32)],
         name="band_sums",
         **settings(16),
-    )(b_offsets, sizes, place, b_own, b_peer)
+    )(b_offsets, sizes, place, offsets, b_own, b_peer)
 
 
 def join_kernel(table, tail, other_tail, head, other_head, out, sem):
     layer = lax.axis_index("layer")
-    pair = 2 * WIDTH
-    rows = table.shape[0] // pair
+    tile = table.shape[-1]
+    height = 2 * WIDTH * tile
+    rows = table.shape[0] // height
     parts = (
-        (table.at[pl.ds(0, rows * pair)], BAND, rows),
+        (table, BAND, rows),
         (tail, layer, 1),
         (other_tail, 1 - layer, 1),
         (head, BAND + rows + layer, 1),
         (other_head, BAND + rows + 1 - layer, 1),
     )
     moves = [
-        pltpu.make_async_copy(src, out.at[pl.ds(at * pair, n * pair)], sem.at[i])
+        pltpu.make_async_copy(
+            src.at[pl.ds(0, n * height)], out.at[pl.ds(at * height, n * height)], sem.at[i]
+        )
         for i, (src, at, n) in enumerate(parts)
     ]
     for move in moves:
         move.start()
-    out[pl.ds((rows + 2 * BAND) * pair, 2)] = jnp.zeros((2,) + out.shape[1:], out.dtype)
+    out[pl.ds((rows + 2 * BAND) * height, 2 * tile)] = jnp.zeros((2 * tile, tile), out.dtype)
     for move in moves:
         move.wait()
 
 
 def join(table, tail, head):
-    more = 2 * BAND * 2 * WIDTH
+    more = 2 * BAND * 2 * WIDTH * table.shape[1]
     return pl.pallas_call(
         join_kernel,
-        out_shape=jax.ShapeDtypeStruct((table.shape[0] + more,) + table.shape[1:], table.dtype),
+        out_shape=jax.ShapeDtypeStruct((table.shape[0] + more, table.shape[1]), table.dtype),
         in_specs=[ANY] * 5,
         out_specs=VMEM,
         scratch_shapes=[pltpu.SemaphoreType.DMA((5,))],
@@ -270,61 +268,49 @@
     far = [refs[2 * i : 2 * i + 2] for i in range(cfg["n_far"])]
     del refs[: 2 * cfg["n_far"]]
     table = refs.pop(0)
-    out, a_v, o_v, a_sem, o_sem = refs[cfg["aliased"] :]
+    out, o_v, o_sem = refs[cfg["aliased"] :]
     chosen, row0, atoms = cfg["chosen"], cfg["row0"], cfg["atoms"]
     count, slots, tile, _ = o_v.shape
-    height = a_v.shape[1] // count
+    height = cfg["height"]
     half = height // tile
-
-    def fetch(pieces):
-        moves, at = [], 0
-        for pair in pieces:
-            n = pair[0].shape[0] // height * height
-            for h in range(2):
-                move = pltpu.make_async_copy(
-                    pair[h].at[pl.ds(0, n)], a_v.at[h, pl.ds(at, n)], a_sem.at[len(moves)]
-                )
-                moves.append(move)
+    zero_at = table.shape[0] // (2 * tile) - 1
+    row_iota = lax.broadcasted_iota(jnp.int32, (tile, 2 * tile), 0)
+
+    def run(pair, part):
+        for n, p in enumerate(part):
+            slot = chosen.index(p)
+
+            def factor(t, s, p=p):
+                at = plan[t, s * atoms + p]
+                at = 2 * tile * jnp.where(at < 0, zero_at, at - row0 * WIDTH)
+                return table[pl.ds(pl.multiple_of(at, 2 * tile), 2 * tile)]
+
+            size = plan[0, slots * atoms + p]
+            for q in range(slots // 2):
+                total = jnp.zeros((tile, 2 * tile), jnp.float32)
+                for t in range(2 * half):
+                    left = pair[t // half][pl.ds(n * height + t % half * tile, tile)]
+                    left = jnp.concatenate([left, left], axis=1)
+                    right = jnp.concatenate([factor(t, 2 * q), factor(t, 2 * q + 1)], axis=1)
+                    total += jnp.dot(left, right, preferred_element_type=jnp.float32)
+                total = jnp.where(row_iota < size, total, 0.0).astype(jnp.bfloat16)
+                o_v[slot, 2 * q] = total[:, :tile]
+                o_v[slot, 2 * q + 1] = total[:, tile:]
+            pltpu.make_async_copy(o_v.at[slot], out.at[p], o_sem.at[slot]).start()
+
+    def run_far():
+        at = 0
+        for pair in far:
+            n = pair[0].shape[0] // height
+            run(pair, chosen[at : at + n])
             at += n
-        for move in moves:
-            move.start()
-        for move in moves:
-            move.wait()
 
     if near:
         mine = plan[1, slots * atoms]
-        pl.when(mine == 1)(lambda: fetch([near]))
-        pl.when(mine != 1)(lambda: fetch(far))
+        pl.when(mine == 1)(lambda: run(near, chosen))
+        pl.when(mine != 1)(run_far)
     else:
-        fetch(far)
-    zero_at = table.shape[0] // 2 - 1
-    row_iota = lax.broadcasted_iota(jnp.int32, (tile, 2 * tile), 0)
-    first = [p == chosen[0] + n for n, p in enumerate(chosen)].count(True)
-    jump = chosen[-1] - chosen[0] + 1 - count
-
-    def one_atom(n, _):
-        p = chosen[0] + n + jnp.where(n < first, 0, jump)
-
-        def factor(t, s):
-            at = plan[t, s * atoms + p]
-            at = 2 * jnp.where(at < 0, zero_at, at - row0 * WIDTH)
-            return jnp.concatenate([table[at], table[at + 1]], axis=0)
-
-        size = plan[0, slots * atoms + p]
-        for q in range(slots // 2):
-            total = jnp.zeros((tile, 2 * tile), jnp.float32)
-            for t in range(2 * half):
-                left = a_v[t // half, pl.ds(n * height + t % half * tile, tile)]
-                left = jnp.concatenate([left, left], axis=1)
-                right = jnp.concatenate([factor(t, 2 * q), factor(t, 2 * q + 1)], axis=1)
-                total += jnp.dot(left, right, preferred_element_type=jnp.float32)
-            total = jnp.where(row_iota < size, total, 0.0).astype(jnp.bfloat16)
-            o_v[n, 2 * q] = total[:, :tile]
-            o_v[n, 2 * q + 1] = total[:, tile:]
-        pltpu.make_async_copy(o_v.at[n], out.at[p], o_sem.at[n]).start()
-        return 0
-
-    lax.fori_loop(0, count, one_atom, 0)
+        run_far()
     for n, p in enumerate(chosen):
         pltpu.make_async_copy(o_v.at[n], out.at[p], o_sem.at[n]).wait()
 
@@ -333,7 +319,7 @@
     tile = table.shape[-1]
     count = len(chosen)
     operands = [plan, *near, *[f for pair in far for f in pair], table]
-    specs = [SMEM] + [ANY] * (len(operands) - 2) + [VMEM]
+    specs = [SMEM] + [VMEM] * (len(operands) - 1)
     aliases = {}
     if prior is not None:
         aliases = {len(operands): 0}
@@ -343,6 +329,7 @@
         atoms=atoms,
         chosen=chosen,
         row0=row0,
+        height=half * tile,
         n_near=len(near),
         n_far=len(far),
         aliased=len(aliases),
@@ -353,9 +340,7 @@
         in_specs=specs,
         out_specs=ANY,
         scratch_shapes=[
-            pltpu.VMEM((2, count * half * tile, tile), jnp.bfloat16),
             pltpu.VMEM((count, slots, tile, tile), jnp.bfloat16),
-            pltpu.SemaphoreType.DMA((2 * len(far),)),
             pltpu.SemaphoreType.DMA((count,)),
         ],
         input_output_aliases=aliases,
@@ -400,28 +385,30 @@
     whole = cols == 2 and bucket == atoms
     common = dict(slots=slots, atoms=atoms, half=half)
     if whole:
-        (sent,) = cut(a_rows, (inner,), 56, offsets=offsets)
+        at = (0, 0, 1 - me, BAND, 0, 0)
+        sent = lax.dynamic_slice(a_rows, at, (1, 1, 1, len(inner)) + a_rows.shape[4:])
+        sent = sent.reshape(-1, tile)
         b_offsets = after(b_offsets, sent)
         b_peer = across(b_tiles)
         own_rows = lax.dynamic_slice_in_dim(b_offsets, start, atoms, 0)
         far = swap(sent)
-        table, tail, head = band_sums(own_rows, block_sizes, place, b_tiles, b_peer)
-        (rest,) = cut(a_rows, (outer,), 8, earlier=(tail,))
+        table, tail, head = band_sums(own_rows, block_sizes, place, offsets, b_tiles, b_peer)
+        rest = cut(a_rows, outer, tail)
         tail, head = onward(tail), back(head)
         rest = swap(rest)
-        far = choose(atom_owner, a_rows, offsets, after(far, table), inner)
+        far = choose(atom_owner, a_rows, offsets, after(far, table), tail, head, inner)
         far = [(f, across(f)) for f in far]
         plan = make_plan(atom_owner, block_sizes, place, c_offsets, half, *far[-1])
         c = products(plan, far, table, BAND, inner, **common)
         joined = join(table, (tail, across(tail)), (head, across(head)))
-        (near,) = cut(a_rows, (outer,), 8, away=False, earlier=(table,))
+        near = cut(a_rows, outer, table, away=False)
         near = (near, across(near))
         rest = after(rest, c, joined)
         rest = [(rest, across(rest))]
         return products(plan, rest, joined, 0, outer, near=near, prior=c, **common)
     b_peer = across(b_tiles)
     own_rows = lax.dynamic_slice_in_dim(b_offsets, start, atoms, 0)
-    table, tail, head = band_sums(own_rows, block_sizes, place, b_tiles, b_peer)
+    table, tail, head = band_sums(own_rows, block_sizes, place, offsets, b_tiles, b_peer)
     tail, head = onward(tail), back(head)
     received = lax.all_to_all(a_tiles, "col", split_axis=2, concat_axis=1, tiled=True)
     moved = lax.all_to_all(a_offsets, "col", split_axis=2, concat_axis=1, tiled=True)

time: 48.4 us -> 47.1 us (0.973)
  Pallas kernels: 16.9 us -> 13.2 us
  local copies, waits for them, and re-layouts: 1.53 us -> 4.78 us
  waiting for transfers between devices: 20.6 us -> 19.7 us
    ppermute x1, waiting for transfers between devices: 16.4 us -> 14.2 us  [onward(): lax.ppermute(x, ('row', 'col'), [(i, (i + 1) % cycle) for i in range(cycl...]
    pallas_call x4 -> x3, Pallas kernels: 6.34 us -> 4.45 us  [the longest x1 2.98 us: band_sums(): pl.pallas_call(band_kernel, out_shape=(shape(2 * (atoms * WIDTH + 1) * ti...]
    unnamed x14 -> x16, local copies, waits for them, and re-layouts: 1.43 us -> 2.77 us
    ppermute x2, waiting for transfers between devices: 1.47 us -> 2.73 us  [swap(): return lax.ppermute(x, 'col', [(0, 1), (1, 0)])]
    pallas_call x2, Pallas kernels: 6.45 us -> 5.21 us  [products(): pl.pallas_call(functools.partial(product_kernel, cfg), out_shape=jax.Shap...]
    dynamic_slice x0 -> x1, local copies, waits for them, and re-layouts: none -> 1.23 us  [local(): lax.dynamic_slice(a_rows, at, (1, 1, 1, len(inner)) + a_rows.shape[4:])]
    optimization_barrier x1, local copies, waits for them, and re-layouts: 0.09 us -> 0.78 us  [after(): return lax.optimization_barrier((x,) + others)[0]]
    pallas_call x1, Pallas kernels: 1.29 us -> 0.66 us  [choose(): pl.pallas_call(functools.partial(choose_kernel, chosen), out_shape=(shape...]
  transfers between devices with their start and end apart: 11 -> 11, of which waited for: 5 -> 5; matrix products, arithmetic and copies ran while one was open for 0% -> 4% of each run, Pallas kernels for 28% -> 23%
where the time goes in v4:
time: 47.1 us; the launch traced here: 46.8 us
  waiting for transfers between devices  19.7 us (42%)
  Pallas kernels  13.2 us (28%)
  starting transfers between devices  8.9 us (19%)
  local copies, waits for them, and re-layouts  4.78 us (10%)
    ppermute x1, waiting for transfers between devices, onward(): lax.ppermute(x, ('row', 'col'), [(i, (i + 1) % cycle) for i in range(cycl...  14.2 us
    pallas_call x2, Pallas kernels, products(): pl.pallas_call(functools.partial(product_kernel, cfg), out_shape=jax.Shap...  5.21 us
    ppermute x1, starting transfers between devices, back(): lax.ppermute(x, ('row', 'col'), [((i + 1) % cycle, i) for i in range(cycl...  3.14 us
    pallas_call x1, Pallas kernels, band_sums(): pl.pallas_call(band_kernel, out_shape=(shape(2 * (atoms * WIDTH + 1) * ti...  2.98 us
    unnamed x16, local copies, waits for them, and re-layouts  2.77 us
    ppermute x2, waiting for transfers between devices, swap(): return lax.ppermute(x, 'col', [(0, 1), (1, 0)])  2.73 us
    ppermute x2, starting transfers between devices, swap(): return lax.ppermute(x, 'col', [(0, 1), (1, 0)])  2.63 us
    ppermute x7, waiting for transfers between devices, across(): return lax.ppermute(x, 'layer', [(0, 1), (1, 0)])  2.25 us
  transfers between devices with their start and end apart: 11, of which 5 were waited for; matrix products, arithmetic and copies ran while one was open for 4% of the time, Pallas kernels for 23%

profile of v4, /device:TPU:0, one launch (start us, length us, event | category | flops | bytes accessed | tf_op | source)
XLA Modules:
  0.0 46.8 jit_solution(14832804408240334037)
XLA Ops:
  0.0 0.5 collective-permute-start.1
  0.5 1.2 %constant_dynamic-slice_fusion.1 = bf16[1,1,1,4,512,128]{5,4,3,2,1,0:T(8,128)(2,1)S(1)} fusion(bf16[1,1,2,8,512,128]{5,4,3,2,1,0:T(8,128)(2,1)} %bitcast.6, s32[]{:T(128)S(6)} %select_n.6), kind=kLoop, calls=%fused_computation.2 | loop fusion | bytes 1048580 | tf_op jit(solution)/shard_map/dynamic_slice | solution.py:389
  1.7 2.6 %collective-permute-start = (bf16[2048,128]{1,0:T(8,128)(2,1)S(1)}, bf16[2048,128]{1,0:T(8,128)(2,1)S(1)}, u32[]{:S(2)}, u32[]{:S(2)}) collective-permute-start(bf16[2048,128]{1,0:T(8,128)(2,1)S(1)} %bitcast.12), channel_id=1, source_target_pairs={{0,2},{2,0},{1,3},{3,1},{4,6},{6,4},{5,7},{7,5},{8,10},{10,8},{9,1... | collective-permute-start | bytes 1572872 | tf_op jit(solution)/shard_map/ppermute | solution.py:372
  4.2 0.1 pad_add_fusion.place
  4.3 0.8 %copy.9 = s32[64,12]{1,0:T(8,128)S(1)} copy(s32[64,12]{0,1:T(8,128)} %param.11) | data formatting | bytes 6144 | tf_op jit(solution)/shard_map/optimization_barrier | solution.py:353
  5.1 0.0 collective-permute-done.1.b_peer
  5.1 0.0 copy-start.1
  5.1 1.4 %copy-done.1 = bf16[8,6,128,128]{3,2,1,0:T(8,128)(2,1)S(1)} copy-done((bf16[8,6,128,128]{3,2,1,0:T(8,128)(2,1)S(1)}, bf16[8,6,128,128]{3,2,1,0:T(8,128)(2,1)}, u32[]{:S(2)}) %copy-start.1) | copy-done | bytes 1572888
  6.5 0.7 %copy-done.2 = s32[1,1,2,8,4]{3,4,2,1,0:T(4,128)S(1)} copy-done((s32[1,1,2,8,4]{3,4,2,1,0:T(4,128)S(1)}, s32[1,1,2,8,4]{3,4,2,1,0:T(4,128)}, u32[]{:S(2)}) %copy-start.2) | copy-done | bytes 280
  7.2 0.7 %copy-done.5 = s32[64]{0:T(128)S(1)} copy-done((s32[64]{0:T(128)S(1)}, s32[64]{0:T(128)}, u32[]{:S(2)}) %copy-start.5) | copy-done | bytes 280
  7.9 3.0 %band_sums.1 = (bf16[10496,128]{1,0:T(8,128)(2,1)S(1)}, bf16[1296,128]{1,0:T(8,128)(2,1)S(1)}, bf16[1296,128]{1,0:T(8,128)(2,1)S(1)}) custom-call(s32[8,12]{1,0:T(8,128)S(1)} %constant_dynamic-slice_fusion.b_offsets, s32[64]{0:T(128)S(1)} %copy-done.5, s32[3]{0:T(128)S(1)} %pad_add_fusion.place, s32[1,1,2,4,8]{4,3,2,1,0:T(4,128)S(1)} %bitcast.10, ...), custom_call_target="tpu_custom_call" | custom-call | flops 1 | bytes 1 | tf_op jit(solution)/shard_map/band_sums/pallas_call | solution.py:165
  10.9 0.0 copy-start.3
  10.9 0.0 copy-start.7
  10.9 1.6 %collective-permute-start.2 = (bf16[1296,128]{1,0:T(8,128)(2,1)S(1)}, bf16[1296,128]{1,0:T(8,128)(2,1)S(1)}, u32[]{:S(2)}, u32[]{:S(2)}) collective-permute-start(bf16[1296,128]{1,0:T(8,128)(2,1)S(1)} %get-tuple-element.16.refs_0_), channel_id=1, source_target_pairs={{0,2},{2,4},{4,6},{6,8},{8,10},{10,12},{12,14},{14,0},{1,3},{3,5},... | collective-permute-start | bytes 995336 | tf_op jit(solution)/shard_map/ppermute | solution.py:375
  12.5 3.1 %collective-permute-start.3 = (bf16[1296,128]{1,0:T(8,128)(2,1)S(1)}, bf16[1296,128]{1,0:T(8,128)(2,1)S(1)}, u32[]{:S(2)}, u32[]{:S(2)}) collective-permute-start(bf16[1296,128]{1,0:T(8,128)(2,1)S(1)} %get-tuple-element.17), channel_id=1, source_target_pairs={{2,0},{4,2},{6,4},{8,6},{10,8},{12,10},{14,12},{0,14},{3,1},{5,3},... | collective-permute-start | bytes 995336 | tf_op jit(solution)/shard_map/ppermute | solution.py:378
  15.7 0.7 %cut.3 = bf16[2048,128]{1,0:T(8,128)(2,1)S(1)} custom-call(bf16[1,1,2,8,512,128]{5,4,3,2,1,0:T(8,128)(2,1)S(1)} %bitcast.7, bf16[1296,128]{1,0:T(8,128)(2,1)S(1)} %get-tuple-element.16.refs_0_), custom_call_target="tpu_custom_call" | custom-call | flops 1 | bytes 1 | tf_op jit(solution)/shard_map/cut/pallas_call | solution.py:46
  16.4 0.1 collective-permute-start.6
  16.5 14.2 %collective-permute-done.2.tail = bf16[1296,128]{1,0:T(8,128)(2,1)S(1)} collective-permute-done((bf16[1296,128]{1,0:T(8,128)(2,1)S(1)}, bf16[1296,128]{1,0:T(8,128)(2,1)S(1)}, u32[]{:S(2)}, u32[]{:S(2)}) %collective-permute-start.2) | collective-permute-done | bytes 331808 | tf_op jit(solution)/shard_map/ppermute | solution.py:375
  30.7 0.5 %collective-permute-done.3.head = bf16[1296,128]{1,0:T(8,128)(2,1)S(1)} collective-permute-done((bf16[1296,128]{1,0:T(8,128)(2,1)S(1)}, bf16[1296,128]{1,0:T(8,128)(2,1)S(1)}, u32[]{:S(2)}, u32[]{:S(2)}) %collective-permute-start.3) | collective-permute-done | bytes 331808 | tf_op jit(solution)/shard_map/ppermute | solution.py:378
  31.2 0.0 collective-permute-start.9
  31.3 0.7 %choose.1 = (bf16[1024,128]{1,0:T(8,128)(2,1)S(1)}, bf16[1040,128]{1,0:T(8,128)(2,1)S(1)}) custom-call(s32[8]{0:T(128)S(1)} %copy-done.7, bf16[1,1,2,8,512,128]{5,4,3,2,1,0:T(8,128)(2,1)S(1)} %bitcast.8, s32[1,1,2,4,8]{4,3,2,1,0:T(4,128)S(1)} %bitcast.11, bf16[2048,128]{1,0:T(8,128)(2,1)S(1)} %collective-permute-done.far, ...), custom_call_target="tpu_custom_call" | custom-call | flops 1 | bytes 1 | tf_op jit(solution)/shard_map/choose/pallas_call | solution.py:111
  31.9 0.6 %collective-permute-start.4 = (bf16[1040,128]{1,0:T(8,128)(2,1)S(1)}, bf16[1040,128]{1,0:T(8,128)(2,1)S(1)}, u32[]{:S(2)}, u32[]{:S(2)}) collective-permute-start(bf16[1040,128]{1,0:T(8,128)(2,1)S(1)} %get-tuple-element.18.own.refs_2_), channel_id=1, source_target_pairs={{0,1},{1,0},{2,3},{3,2},{4,5},{5,4},{6,7},{7,6},{8,9},{9,8},{10,11... | collective-permute-start | bytes 798728 | tf_op jit(solution)/shard_map/ppermute | solution.py:369
  32.5 0.1 collective-permute-start.7
  32.6 0.7 %cut.2.refs_0_ = bf16[2048,128]{1,0:T(8,128)(2,1)S(1)} custom-call(bf16[1,1,2,8,512,128]{5,4,3,2,1,0:T(8,128)(2,1)S(1)} %bitcast.9, bf16[10496,128]{1,0:T(8,128)(2,1)S(1)} %get-tuple-element.14.refs_0_.refs_4_.table), custom_call_target="tpu_custom_call" | custom-call | flops 1 | bytes 1 | tf_op jit(solution)/shard_map/cut/pallas_call | solution.py:46
  33.3 0.3 collective-permute-done.4.other.refs_3_
  33.7 0.4 collective-permute-start.5
  34.0 2.2 %plan.1 = s32[8,128]{1,0:T(8,128)S(1)} custom-call(s32[8]{0:T(128)S(1)} %copy-done.7, s32[64]{0:T(128)S(1)} %copy-done.6, s32[3]{0:T(128)S(1)} %pad_add_fusion.place, s32[8,8]{1,0:T(8,128)S(1)} %copy-done.4, bf16[1040,128]{1,0:T(8,128)(2,1)S(1)} %get-tuple-element.18.own.refs_2_, bf16[1040,128]{1,0:T(8,128)(2,1)S(1)} %collective-permute-done.4.other.refs_3_), custom_call_target="tpu_custom_call" | custom-call | flops 1 | bytes 1 | tf_op jit(solution)/shard_map/plan/pallas_call | solution.py:249
  36.3 2.6 %products.2.refs_5_ = bf16[8,4,128,128]{3,2,1,0:T(8,128)(2,1)} custom-call(s32[8,128]{1,0:T(8,128)S(1)} %plan.1, bf16[1024,128]{1,0:T(8,128)(2,1)S(1)} %get-tuple-element.19.refs_0_, bf16[1024,128]{1,0:T(8,128)(2,1)S(1)} %collective-permute-done.7.refs_1_, bf16[1040,128]{1,0:T(8,128)(2,1)S(1)} %get-tuple-element.18.own.refs_2_, ...), custom_call_target="tpu_custom_call" | custom-call | flops 1 | bytes 1 | tf_op jit(solution)/shard_map/products/pallas_call | solution.py:337
  38.9 0.7 %join.1.refs_4_ = bf16[15616,128]{1,0:T(8,128)(2,1)S(1)} custom-call(bf16[10496,128]{1,0:T(8,128)(2,1)S(1)} %get-tuple-element.14.refs_0_.refs_4_.table, bf16[1296,128]{1,0:T(8,128)(2,1)S(1)} %collective-permute-done.2.tail, bf16[1296,128]{1,0:T(8,128)(2,1)S(1)} %collective-permute-done.8.other_tail, bf16[1296,128]{1,0:T(8,128)(2,1)S(1)} %collective-permute-done.3.head, ...), custom_call_target="tpu_custom_call" | custom-call | flops 1 | bytes 1 | tf_op jit(solution)/shard_map/join/pallas_call | solution.py:203
  39.6 2.7 %collective-permute-done.6.refs_2_ = bf16[2048,128]{1,0:T(8,128)(2,1)S(1)} collective-permute-done((bf16[2048,128]{1,0:T(8,128)(2,1)S(1)}, bf16[2048,128]{1,0:T(8,128)(2,1)S(1)}, u32[]{:S(2)}, u32[]{:S(2)}) %collective-permute-start.6) | collective-permute-done | bytes 524320 | tf_op jit(solution)/shard_map/ppermute | solution.py:372
  42.3 1.9 %collective-permute-done.10.refs_3_ = bf16[2048,128]{1,0:T(8,128)(2,1)S(1)} collective-permute-done((bf16[2048,128]{1,0:T(8,128)(2,1)S(1)}, bf16[2048,128]{1,0:T(8,128)(2,1)S(1)}, u32[]{:S(2)}, u32[]{:S(2)}) %collective-permute-start.10) | collective-permute-done | bytes 524320 | tf_op jit(solution)/shard_map/ppermute | solution.py:369
  44.2 2.6 %products.3 = bf16[8,4,128,128]{3,2,1,0:T(8,128)(2,1)} custom-call(s32[8,128]{1,0:T(8,128)S(1)} %plan.1, bf16[2048,128]{1,0:T(8,128)(2,1)S(1)} %cut.2.refs_0_, bf16[2048,128]{1,0:T(8,128)(2,1)S(1)} %collective-permute-done.5.refs_1_, bf16[2048,128]{1,0:T(8,128)(2,1)S(1)} %collective-permute-done.6.refs_2_, ...), custom_call_target="tpu_custom_call", output_to_operand_aliasing={{}: (6, {})} | custom-call | flops 1 | bytes 1 | tf_op jit(solution)/shard_map/products/pallas_call | solution.py:337
  (18 shorter events, 0.0 us)
Async XLA Ops:
  0.0 5.1 %collective-permute-start.1 = (bf16[8,6,128,128]{3,2,1,0:T(8,128)(2,1)}, bf16[8,6,128,128]{3,2,1,0:T(8,128)(2,1)}, u32[]{:S(2)}, u32[]{:S(2)}) collective-permute-start(bf16[8,6,128,128]{3,2,1,0:T(8,128)(2,1)} %b_own.1), channel_id=1, source_target_pairs={{0,1},{1,0},{2,3},{3,2},{4,5},{5,4},{6,7},{7,6},{8,9},{9,8},{10,11... | collective-permute-start | bytes 4718600 | tf_op jit(solution)/shard_map/ppermute | solution.py:369
  0.5 15.2 %copy-start = (bf16[1,1,2,8,4,128,128]{6,5,4,3,2,1,0:T(8,128)(2,1)S(1)}, bf16[1,1,2,8,4,128,128]{6,5,4,3,2,1,0:T(8,128)(2,1)}, u32[]{:S(2)}) copy-start(bf16[1,1,2,8,4,128,128]{6,5,4,3,2,1,0:T(8,128)(2,1)} %param.7) | copy-start | bytes 6291460
  1.7 29.6 %collective-permute-start = (bf16[2048,128]{1,0:T(8,128)(2,1)S(1)}, bf16[2048,128]{1,0:T(8,128)(2,1)S(1)}, u32[]{:S(2)}, u32[]{:S(2)}) collective-permute-start(bf16[2048,128]{1,0:T(8,128)(2,1)S(1)} %bitcast.12), channel_id=1, source_target_pairs={{0,2},{2,0},{1,3},{3,1},{4,6},{6,4},{5,7},{7,5},{8,10},{10,8},{9,1... | collective-permute-start | bytes 1572872 | tf_op jit(solution)/shard_map/ppermute | solution.py:372
  5.1 1.4 %copy-start.1 = (bf16[8,6,128,128]{3,2,1,0:T(8,128)(2,1)S(1)}, bf16[8,6,128,128]{3,2,1,0:T(8,128)(2,1)}, u32[]{:S(2)}) copy-start(bf16[8,6,128,128]{3,2,1,0:T(8,128)(2,1)} %b_own.1) | copy-start | bytes 4718596
  6.5 0.7 %copy-start.2 = (s32[1,1,2,8,4]{3,4,2,1,0:T(4,128)S(1)}, s32[1,1,2,8,4]{3,4,2,1,0:T(4,128)}, u32[]{:S(2)}) copy-start(s32[1,1,2,8,4]{3,4,2,1,0:T(4,128)} %param.8) | copy-start | bytes 772
  7.2 0.7 %copy-start.5 = (s32[64]{0:T(128)S(1)}, s32[64]{0:T(128)}, u32[]{:S(2)}) copy-start(s32[64]{0:T(128)} %sizes.3) | copy-start | bytes 772
  10.9 20.4 %copy-start.3 = (s32[1,1,2,8,4]{3,4,2,1,0:T(4,128)S(1)}, s32[1,1,2,8,4]{3,4,2,1,0:T(4,128)}, u32[]{:S(2)}) copy-start(s32[1,1,2,8,4]{3,4,2,1,0:T(4,128)} %param.8) | copy-start | bytes 772
  10.9 20.4 %copy-start.7 = (s32[8]{0:T(128)S(1)}, s32[8]{0:T(128)}, u32[]{:S(2)}) copy-start(s32[8]{0:T(128)} %owner.3) | copy-start | bytes 100
  10.9 19.8 %collective-permute-start.2 = (bf16[1296,128]{1,0:T(8,128)(2,1)S(1)}, bf16[1296,128]{1,0:T(8,128)(2,1)S(1)}, u32[]{:S(2)}, u32[]{:S(2)}) collective-permute-start(bf16[1296,128]{1,0:T(8,128)(2,1)S(1)} %get-tuple-element.16.refs_0_), channel_id=1, source_target_pairs={{0,2},{2,4},{4,6},{6,8},{8,10},{10,12},{12,14},{14,0},{1,3},{3,5},... | collective-permute-start | bytes 995336 | tf_op jit(solution)/shard_map/ppermute | solution.py:375
  12.5 18.7 %collective-permute-start.3 = (bf16[1296,128]{1,0:T(8,128)(2,1)S(1)}, bf16[1296,128]{1,0:T(8,128)(2,1)S(1)}, u32[]{:S(2)}, u32[]{:S(2)}) collective-permute-start(bf16[1296,128]{1,0:T(8,128)(2,1)S(1)} %get-tuple-element.17), channel_id=1, source_target_pairs={{2,0},{4,2},{6,4},{8,6},{10,8},{12,10},{14,12},{0,14},{3,1},{5,3},... | collective-permute-start | bytes 995336 | tf_op jit(solution)/shard_map/ppermute | solution.py:378
  16.4 25.9 %collective-permute-start.6 = (bf16[2048,128]{1,0:T(8,128)(2,1)S(1)}, bf16[2048,128]{1,0:T(8,128)(2,1)S(1)}, u32[]{:S(2)}, u32[]{:S(2)}) collective-permute-start(bf16[2048,128]{1,0:T(8,128)(2,1)S(1)} %cut.3), channel_id=1, source_target_pairs={{0,2},{2,0},{1,3},{3,1},{4,6},{6,4},{5,7},{7,5},{8,10},{10,8},{9,1... | collective-permute-start | bytes 1572872 | tf_op jit(solution)/shard_map/ppermute | solution.py:372
  30.7 8.2 %collective-permute-start.8 = (bf16[1296,128]{1,0:T(8,128)(2,1)S(1)}, bf16[1296,128]{1,0:T(8,128)(2,1)S(1)}, u32[]{:S(2)}, u32[]{:S(2)}) collective-permute-start(bf16[1296,128]{1,0:T(8,128)(2,1)S(1)} %collective-permute-done.2.tail), channel_id=1, source_target_pairs={{0,1},{1,0},{2,3},{3,2},{4,5},{5,4},{6,7},{7,6},{8,9},{9,8},{10,11... | collective-permute-start | bytes 995336 | tf_op jit(solution)/shard_map/ppermute | solution.py:369
  31.2 7.7 %collective-permute-start.9 = (bf16[1296,128]{1,0:T(8,128)(2,1)S(1)}, bf16[1296,128]{1,0:T(8,128)(2,1)S(1)}, u32[]{:S(2)}, u32[]{:S(2)}) collective-permute-start(bf16[1296,128]{1,0:T(8,128)(2,1)S(1)} %collective-permute-done.3.head), channel_id=1, source_target_pairs={{0,1},{1,0},{2,3},{3,2},{4,5},{5,4},{6,7},{7,6},{8,9},{9,8},{10,11... | collective-permute-start | bytes 995336 | tf_op jit(solution)/shard_map/ppermute | solution.py:369
  31.9 1.7 %collective-permute-start.4 = (bf16[1040,128]{1,0:T(8,128)(2,1)S(1)}, bf16[1040,128]{1,0:T(8,128)(2,1)S(1)}, u32[]{:S(2)}, u32[]{:S(2)}) collective-permute-start(bf16[1040,128]{1,0:T(8,128)(2,1)S(1)} %get-tuple-element.18.own.refs_2_), channel_id=1, source_target_pairs={{0,1},{1,0},{2,3},{3,2},{4,5},{5,4},{6,7},{7,6},{8,9},{9,8},{10,11... | collective-permute-start | bytes 798728 | tf_op jit(solution)/shard_map/ppermute | solution.py:369
  32.5 1.5 %copy-start.4 = (s32[8,8]{1,0:T(8,128)S(1)}, s32[8,8]{1,0:T(8,128)}, u32[]{:S(2)}) copy-start(s32[8,8]{1,0:T(8,128)} %c_offsets.1) | copy-start | bytes 772
  32.5 1.5 %copy-start.6 = (s32[64]{0:T(128)S(1)}, s32[64]{0:T(128)}, u32[]{:S(2)}) copy-start(s32[64]{0:T(128)} %sizes.3) | copy-start | bytes 772
  32.5 3.8 %collective-permute-start.7 = (bf16[1024,128]{1,0:T(8,128)(2,1)S(1)}, bf16[1024,128]{1,0:T(8,128)(2,1)S(1)}, u32[]{:S(2)}, u32[]{:S(2)}) collective-permute-start(bf16[1024,128]{1,0:T(8,128)(2,1)S(1)} %get-tuple-element.19.refs_0_), channel_id=1, source_target_pairs={{0,1},{1,0},{2,3},{3,2},{4,5},{5,4},{6,7},{7,6},{8,9},{9,8},{10,11... | collective-permute-start | bytes 786440 | tf_op jit(solution)/shard_map/ppermute | solution.py:369
  33.7 8.6 %collective-permute-start.5 = (bf16[2048,128]{1,0:T(8,128)(2,1)S(1)}, bf16[2048,128]{1,0:T(8,128)(2,1)S(1)}, u32[]{:S(2)}, u32[]{:S(2)}) collective-permute-start(bf16[2048,128]{1,0:T(8,128)(2,1)S(1)} %cut.2.refs_0_), channel_id=1, source_target_pairs={{0,1},{1,0},{2,3},{3,2},{4,5},{5,4},{6,7},{7,6},{8,9},{9,8},{10,11... | collective-permute-start | bytes 1572872 | tf_op jit(solution)/shard_map/ppermute | solution.py:369
  42.3 1.9 %collective-permute-start.10 = (bf16[2048,128]{1,0:T(8,128)(2,1)S(1)}, bf16[2048,128]{1,0:T(8,128)(2,1)S(1)}, u32[]{:S(2)}, u32[]{:S(2)}) collective-permute-start(bf16[2048,128]{1,0:T(8,128)(2,1)S(1)} %collective-permute-done.6.refs_2_), channel_id=1, source_target_pairs={{0,1},{1,0},{2,3},{3,2},{4,5},{5,4},{6,7},{7,6},{8,9},{9,8},{10,11... | collective-permute-start | bytes 1572872 | tf_op jit(solution)/shard_map/ppermute | solution.py:369

commit v5 on v4

--- a/solution.py
+++ b/solution.py
@@ -58,68 +58,60 @@
     )(a_rows, earlier)
 
 
-def choose_kernel(chosen, owner, a_rows, offsets, far, tail, head, first, second, raw, sem):
+def choose_kernel(chosen, owner, a_rows, offsets, far, first, second, raw, sem):
     height, tile = a_rows.shape[4:]
     me = lax.axis_index("col")
     mine = owner[0] == me
-    split = first.shape[0] // height
     count = len(chosen)
+    split, end = first.shape[0], count * height
+    rest = end - split
+    move = pltpu.make_async_copy(offsets.at[0, 0, me], raw, sem.at[count + 1])
+    move.start()
 
     def run(here):
         if here:
             pairs = []
             for i, p in enumerate(chosen):
-                out, at = (first, i) if i < split else (second, i - split)
-                pairs.append((a_rows.at[0, 0, me, p], out.at[pl.ds(at * height, height)]))
+                low, high = i * height, (i + 1) * height
+                middle = min(max(split, low), high)
+                for out, base, i0, i1 in ((first, 0, low, middle), (second, split, middle, high)):
+                    if i0 < i1:
+                        src = a_rows.at[0, 0, me, p, pl.ds(i0 - low, i1 - i0)]
+                        pairs.append((src, out.at[pl.ds(i0 - base, i1 - i0)]))
         else:
-            n = (count - split) * height
             pairs = [
-                (far.at[pl.ds(0, split * height)], first),
-                (far.at[pl.ds(split * height, n)], second.at[pl.ds(0, n)]),
+                (far.at[pl.ds(0, split)], first),
+                (far.at[pl.ds(split, rest)], second.at[pl.ds(0, rest)]),
             ]
         moves = [pltpu.make_async_copy(*p, sem.at[i]) for i, p in enumerate(pairs)]
-        for move in moves:
-            move.start()
-        if here:
-            half, atoms = offsets.shape[3:]
-            move = pltpu.make_async_copy(offsets.at[0, 0, me], raw, sem.at[count])
-            move.start()
-            move.wait()
-            values = jnp.pad(raw[...].astype(jnp.float32), ((0, 16 - half), (0, tile - atoms)))
-            second[pl.ds((count - split) * height, 16)] = values.astype(second.dtype)
-        else:
-            def ends(ref):
-                src = ref.at[pl.ds(ref.shape[0] - 16, 16)]
-                dst = second.at[pl.ds((count - split) * height, 16)]
-                move = pltpu.make_async_copy(src, dst, sem.at[count])
-                move.start()
-                move.wait()
-
-            pl.when(me == 0)(lambda: ends(head))
-            pl.when(me != 0)(lambda: ends(tail))
-        for move in moves:
-            move.wait()
+        for m in moves:
+            m.start()
+        for m in moves:
+            m.wait()
 
     pl.when(mine)(lambda: run(True))
     pl.when(jnp.logical_not(mine))(lambda: run(False))
-
-
-def choose(owner, a_rows, offsets, far, tail, head, chosen):
-    height, tile = a_rows.shape[4:]
-    one = len(chosen) // 2 * height
+    move.wait()
+    half, atoms = offsets.shape[3:]
+    values = jnp.pad(raw[...].astype(jnp.float32), ((0, 16 - half), (0, tile - atoms)))
+    second[pl.ds(rest, 16)] = values.astype(second.dtype)
+
+
+def choose(owner, a_rows, offsets, far, chosen, split):
+    tile = a_rows.shape[5]
     shape = lambda n: jax.ShapeDtypeStruct((n, tile), a_rows.dtype)
     return pl.pallas_call(
         functools.partial(choose_kernel, chosen),
-        out_shape=(shape(one), shape(far.shape[0] - one + 16)),
-        in_specs=[SMEM] + [ANY] * 5,
+        out_shape=(shape(split), shape(far.shape[0] - split + 16)),
+        in_specs=[SMEM] + [ANY] * 3,
         out_specs=(VMEM, VMEM),
         scratch_shapes=[
             pltpu.VMEM(offsets.shape[3:], jnp.int32),
-            pltpu.SemaphoreType.DMA((len(chosen) + 1,)),
+            pltpu.SemaphoreType.DMA((len(chosen) + 2,)),
         ],
         name="choose",
         **settings(8),
-    )(owner, a_rows, offsets, far, tail, head)
+    )(owner, a_rows, offsets, far)
 
 
 def band_kernel(b_offsets, sizes, place, offsets, b_own, b_peer, table, tail, head, total):
@@ -211,13 +203,27 @@
     )(table, *tail, *head)
 
 
-def plan_kernel(half, owner, sizes, place, c_offsets, own, other, out, raw, spots, sem):
-    moves = [
-        pltpu.make_async_copy(ref.at[pl.ds(ref.shape[0] - 16, 16)], raw.at[h], sem.at[h])
-        for h, ref in enumerate((own, other))
-    ]
-    for move in moves:
-        move.start()
+def plan_kernel(half, n_src, owner, sizes, place, c_offsets, *refs):
+    pairs = [refs[2 * i : 2 * i + 2] for i in range(n_src)]
+    out, raw, spots, sem = refs[2 * n_src :]
+
+    def load(pair):
+        moves = [
+            pltpu.make_async_copy(ref.at[pl.ds(ref.shape[0] - 16, 16)], raw.at[h], sem.at[h])
+            for h, ref in enumerate(pair)
+        ]
+        for move in moves:
+            move.start()
+        for move in moves:
+            move.wait()
+
+    if n_src == 1:
+        load(pairs[0])
+    else:
+        mine = owner[0] == place[2]
+        pl.when(mine)(lambda: load(pairs[0]))
+        pl.when(jnp.logical_not(mine) & (place[2] == 0))(lambda: load(pairs[1]))
+        pl.when(jnp.logical_not(mine) & (place[2] != 0))(lambda: load(pairs[2]))
     atoms = c_offsets.shape[0]
     slots = c_offsets.shape[1] // 2
     start, layer, me = place[0], place[1], place[2]
@@ -229,8 +235,6 @@
     dot = functools.partial(jnp.dot, preferred_element_type=jnp.float32)
     aim = dot(c_offsets[...].astype(jnp.float32), (pick == slot).astype(jnp.float32))
     aim = dot(jnp.ones((2 * half, atoms), jnp.float32), aim * spread)
-    for move in moves:
-        move.wait()
     shift = [raw[h].astype(jnp.float32)[:half, :atoms] for h in range(2)]
     shift = dot(jnp.concatenate(shift, axis=0), spread)
     shift, aim = shift.astype(jnp.int32), aim.astype(jnp.int32)
@@ -245,11 +249,11 @@
     out[1, width] = (owner[0] == me).astype(jnp.int32)
 
 
-def make_plan(owner, sizes, place, c_offsets, half, own, other):
-    return pl.pallas_call(
-        functools.partial(plan_kernel, half),
+def make_plan(owner, sizes, place, c_offsets, half, *pairs):
+    return pl.pallas_call(
+        functools.partial(plan_kernel, half, len(pairs)),
         out_shape=jax.ShapeDtypeStruct((2 * half, 128), jnp.int32),
-        in_specs=[SMEM] * 3 + [VMEM, ANY, ANY],
+        in_specs=[SMEM] * 3 + [VMEM] + [ANY] * (2 * len(pairs)),
         out_specs=SMEM,
         scratch_shapes=[
             pltpu.VMEM((2, 16, 128), jnp.bfloat16),
@@ -258,67 +262,73 @@
         ],
         name="plan",
         **settings(4),
-    )(owner, sizes, place, c_offsets, own, other)
+    )(owner, sizes, place, c_offsets, *[ref for pair in pairs for ref in pair])
 
 
 def product_kernel(cfg, plan, *refs):
     refs = list(refs)
-    near = refs[: cfg["n_near"]]
-    del refs[: cfg["n_near"]]
-    far = [refs[2 * i : 2 * i + 2] for i in range(cfg["n_far"])]
-    del refs[: 2 * cfg["n_far"]]
-    table = refs.pop(0)
-    out, o_v, o_sem = refs[cfg["aliased"] :]
-    chosen, row0, atoms = cfg["chosen"], cfg["row0"], cfg["atoms"]
-    count, slots, tile, _ = o_v.shape
-    height = cfg["height"]
-    half = height // tile
+    halves = cfg["halves"]
+    take = lambda n: [refs.pop(0) for _ in range(n)]
+    near = dict(zip(halves, take(cfg["n_near"]), strict=False))
+    far = [dict(zip(halves, take(len(halves)), strict=True)) for _ in range(cfg["n_far"])]
+    (table,) = take(1)
+    begun = take(cfg["begun"])
+    take(cfg["aliased"])
+    out = refs[0]
+    chosen, atoms, half, slots = cfg["chosen"], cfg["atoms"], cfg["half"], cfg["slots"]
+    tile = table.shape[-1]
     zero_at = table.shape[0] // (2 * tile) - 1
     row_iota = lax.broadcasted_iota(jnp.int32, (tile, 2 * tile), 0)
 
-    def run(pair, part):
-        for n, p in enumerate(part):
-            slot = chosen.index(p)
+    def run(pieces):
+        spots = [(p, i) for p in pieces for i in range(p[halves[0]].shape[0] // tile)]
+        for n, p in enumerate(chosen):
 
             def factor(t, s, p=p):
                 at = plan[t, s * atoms + p]
-                at = 2 * tile * jnp.where(at < 0, zero_at, at - row0 * WIDTH)
+                at = 2 * tile * jnp.where(at < 0, zero_at, at)
                 return table[pl.ds(pl.multiple_of(at, 2 * tile), 2 * tile)]
 
             size = plan[0, slots * atoms + p]
             for q in range(slots // 2):
-                total = jnp.zeros((tile, 2 * tile), jnp.float32)
+                total = begun[0][n, q] if begun else jnp.zeros((tile, 2 * tile), jnp.float32)
                 for t in range(2 * half):
-                    left = pair[t // half][pl.ds(n * height + t % half * tile, tile)]
+                    if t // half not in halves:
+                        continue
+                    piece, i = spots[n * half + t % half]
+                    left = piece[t // half][pl.ds(i * tile, tile)]
                     left = jnp.concatenate([left, left], axis=1)
                     right = jnp.concatenate([factor(t, 2 * q), factor(t, 2 * q + 1)], axis=1)
                     total += jnp.dot(left, right, preferred_element_type=jnp.float32)
+                if cfg["partial"]:
+                    out[n, q] = total
+                    continue
                 total = jnp.where(row_iota < size, total, 0.0).astype(jnp.bfloat16)
-                o_v[slot, 2 * q] = total[:, :tile]
-                o_v[slot, 2 * q + 1] = total[:, tile:]
-            pltpu.make_async_copy(o_v.at[slot], out.at[p], o_sem.at[slot]).start()
-
-    def run_far():
-        at = 0
-        for pair in far:
-            n = pair[0].shape[0] // height
-            run(pair, chosen[at : at + n])
-            at += n
+                o_v, o_sem = refs[1:]
+                o_v[n, 2 * q] = total[:, :tile]
+                o_v[n, 2 * q + 1] = total[:, tile:]
+            if not cfg["partial"]:
+                pltpu.make_async_copy(o_v.at[n], out.at[p], o_sem.at[n]).start()
 
     if near:
         mine = plan[1, slots * atoms]
-        pl.when(mine == 1)(lambda: run(near, chosen))
-        pl.when(mine != 1)(run_far)
+        pl.when(mine == 1)(lambda: run([near]))
+        pl.when(mine != 1)(lambda: run(far))
     else:
-        run_far()
-    for n, p in enumerate(chosen):
-        pltpu.make_async_copy(o_v.at[n], out.at[p], o_sem.at[n]).wait()
-
-
-def products(plan, far, table, row0, chosen, slots, atoms, half, near=(), prior=None):
+        run(far)
+    if not cfg["partial"]:
+        o_v, o_sem = refs[1:]
+        for n, p in enumerate(chosen):
+            pltpu.make_async_copy(o_v.at[n], out.at[p], o_sem.at[n]).wait()
+
+
+def products(
+    plan, far, table, chosen, slots, atoms, half, near=(), prior=None, halves=(0, 1), begun=None, partial=False
+):
     tile = table.shape[-1]
     count = len(chosen)
     operands = [plan, *near, *[f for pair in far for f in pair], table]
+    operands += [] if begun is None else [begun]
     specs = [SMEM] + [VMEM] * (len(operands) - 1)
     aliases = {}
     if prior is not None:
@@ -328,18 +338,26 @@
     cfg = dict(
         atoms=atoms,
         chosen=chosen,
-        row0=row0,
-        height=half * tile,
+        half=half,
+        slots=slots,
+        halves=halves,
         n_near=len(near),
         n_far=len(far),
+        begun=int(begun is not None),
+        partial=partial,
         aliased=len(aliases),
     )
+    out_shape = jax.ShapeDtypeStruct((atoms, slots, tile, tile), jnp.bfloat16)
+    if partial:
+        out_shape = jax.ShapeDtypeStruct((count, slots // 2, tile, 2 * tile), jnp.float32)
     return pl.pallas_call(
         functools.partial(product_kernel, cfg),
-        out_shape=jax.ShapeDtypeStruct((atoms, slots, tile, tile), jnp.bfloat16),
+        out_shape=out_shape,
         in_specs=specs,
-        out_specs=ANY,
-        scratch_shapes=[
+        out_specs=VMEM if partial else ANY,
+        scratch_shapes=[]
+        if partial
+        else [
             pltpu.VMEM((count, slots, tile, tile), jnp.bfloat16),
             pltpu.SemaphoreType.DMA((count,)),
         ],
@@ -378,14 +396,14 @@
         return lax.ppermute(x, ("row", "col"), [((i + 1) % cycle, i) for i in range(cycle)])
 
     half, tile = a_tiles.shape[4:6]
-    inner = tuple(range(BAND, atoms - BAND))
-    outer = tuple(range(BAND)) + tuple(range(atoms - BAND, atoms))
+    inner = tuple(range(1, atoms - BAND))
+    outer = (0,) + tuple(range(atoms - BAND, atoms))
     offsets = jnp.swapaxes(a_offsets, 3, 4)
     a_rows = a_tiles.reshape(a_tiles.shape[:4] + (half * tile, tile))
     whole = cols == 2 and bucket == atoms
     common = dict(slots=slots, atoms=atoms, half=half)
     if whole:
-        at = (0, 0, 1 - me, BAND, 0, 0)
+        at = (0, 0, 1 - me, inner[0], 0, 0)
         sent = lax.dynamic_slice(a_rows, at, (1, 1, 1, len(inner)) + a_rows.shape[4:])
         sent = sent.reshape(-1, tile)
         b_offsets = after(b_offsets, sent)
@@ -396,16 +414,21 @@
         rest = cut(a_rows, outer, tail)
         tail, head = onward(tail), back(head)
         rest = swap(rest)
-        far = choose(atom_owner, a_rows, offsets, after(far, table), tail, head, inner)
+        split = (len(inner) * half // 2 + 1) * tile
+        far = choose(atom_owner, a_rows, offsets, after(far, table), inner, split)
         far = [(f, across(f)) for f in far]
-        plan = make_plan(atom_owner, block_sizes, place, c_offsets, half, *far[-1])
-        c = products(plan, far, table, BAND, inner, **common)
-        joined = join(table, (tail, across(tail)), (head, across(head)))
-        near = cut(a_rows, outer, table, away=False)
+        tail, head = (tail, across(tail)), (head, across(head))
+        plan = make_plan(atom_owner, block_sizes, place, c_offsets, half, far[-1], head, tail)
+        table = join(table, tail, head)
+        c = products(plan, far, table, inner, **common)
+        near = cut(a_rows, outer, own_rows, away=False)
         near = (near, across(near))
-        rest = after(rest, c, joined)
-        rest = [(rest, across(rest))]
-        return products(plan, rest, joined, 0, outer, near=near, prior=c, **common)
+        rest = after(rest, c)
+        rest = (rest, across(rest))
+        common = dict(common, table=table, chosen=outer)
+        begun = products(plan, [rest[:1]], near=near[:1], halves=(0,), partial=True, **common)
+        common = dict(common, prior=c, begun=begun)
+        return products(plan, [rest[1:]], near=near[1:], halves=(1,), **common)
     b_peer = across(b_tiles)
     own_rows = lax.dynamic_slice_in_dim(b_offsets, start, atoms, 0)
     table, tail, head = band_sums(own_rows, block_sizes, place, offsets, b_tiles, b_peer)
@@ -422,12 +445,9 @@
     shift = jnp.take(moved, source, axis=0).T.astype(jnp.bfloat16)
     rows = jnp.concatenate([rows, jnp.pad(shift, ((0, 16 - half), (0, tile - atoms)))], axis=0)
     other = across(rows)
-    plan = make_plan(atom_owner, block_sizes, place, c_offsets, half, rows, other)
-    cuts = [p * half * tile for p in (0, BAND, atoms - BAND, atoms)]
-    low, mid, top = ((rows[i:j], other[i:j]) for i, j in zip(cuts[:-1], cuts[1:], strict=True))
-    c = products(plan, [mid], table, BAND, inner, **common)
+    plan = make_plan(atom_owner, block_sizes, place, c_offsets, half, (rows, other))
     table = join(table, (tail, across(tail)), (head, across(head)))
-    return products(plan, [low, top], table, 0, outer, prior=c, **common)
+    return products(plan, [(rows, other)], table, tuple(range(atoms)), **common)
 
 
 def solution(mesh):

time: 47.1 us -> 46.2 us (0.981)
  waiting for transfers between devices: 19.7 us -> 18.4 us
  Pallas kernels: 13.2 us -> 14 us
    ppermute x2, waiting for transfers between devices: 2.73 us -> 11.4 us  [swap(): return lax.ppermute(x, 'col', [(0, 1), (1, 0)])]
    ppermute x1, waiting for transfers between devices: 14.2 us -> 5.64 us  [onward(): lax.ppermute(x, ('row', 'col'), [(i, (i + 1) % cycle) for i in range(cycl...]
    ppermute x7, waiting for transfers between devices: 2.25 us -> 0.81 us  [across(): return lax.ppermute(x, 'layer', [(0, 1), (1, 0)])]
    pallas_call x3 -> x4, Pallas kernels: 7.41 us -> 8.11 us  [the longest x3 6 us: products(): pl.pallas_call(functools.partial(product_kernel, cfg), out_shape=out_shap...]
  transfers between devices with their start and end apart: 11 -> 11, of which waited for: 5 -> 6; matrix products, arithmetic and copies ran while one was open for 4% -> 5% of each run, Pallas kernels for 23% -> 26%
where the time goes in v5:
time: 46.2 us; the launch traced here: 46 us
  waiting for transfers between devices  18.4 us (40%)
  Pallas kernels  14 us (30%)
  starting transfers between devices  8.52 us (18%)
  local copies, waits for them, and re-layouts  4.84 us (10%)
    ppermute x2, waiting for transfers between devices, swap(): return lax.ppermute(x, 'col', [(0, 1), (1, 0)])  11.4 us
    pallas_call x3, Pallas kernels, products(): pl.pallas_call(functools.partial(product_kernel, cfg), out_shape=out_shap...  6 us
    ppermute x1, waiting for transfers between devices, onward(): lax.ppermute(x, ('row', 'col'), [(i, (i + 1) % cycle) for i in range(cycl...  5.64 us
    ppermute x1, starting transfers between devices, back(): lax.ppermute(x, ('row', 'col'), [((i + 1) % cycle, i) for i in range(cycl...  3.19 us
    pallas_call x1, Pallas kernels, band_sums(): pl.pallas_call(band_kernel, out_shape=(shape(2 * (atoms * WIDTH + 1) * ti...  2.98 us
    unnamed x16, local copies, waits for them, and re-layouts  2.78 us
    ppermute x2, starting transfers between devices, swap(): return lax.ppermute(x, 'col', [(0, 1), (1, 0)])  2.63 us
    pallas_call x1, Pallas kernels, make_plan(): pl.pallas_call(functools.partial(plan_kernel, half, len(pairs)), out_shap...  2.11 us
  transfers between devices with their start and end apart: 11, of which 6 were waited for; matrix products, arithmetic and copies ran while one was open for 5% of the time, Pallas kernels for 26%

profile of v5, /device:TPU:0, one launch (start us, length us, event | category | flops | bytes accessed | tf_op | source)
XLA Modules:
  0.0 46.0 jit_solution(1320519198502327883)
XLA Ops:
  0.0 0.5 collective-permute-start.1
  0.5 1.3 %constant_dynamic-slice_fusion.1 = bf16[1,1,1,5,512,128]{5,4,3,2,1,0:T(8,128)(2,1)S(1)} fusion(bf16[1,1,2,8,512,128]{5,4,3,2,1,0:T(8,128)(2,1)} %bitcast.6, s32[]{:T(128)S(6)} %select_n.6), kind=kLoop, calls=%fused_computation.2 | loop fusion | bytes 1310724 | tf_op jit(solution)/shard_map/dynamic_slice | solution.py:407
  1.7 2.6 %collective-permute-start = (bf16[2560,128]{1,0:T(8,128)(2,1)S(1)}, bf16[2560,128]{1,0:T(8,128)(2,1)S(1)}, u32[]{:S(2)}, u32[]{:S(2)}) collective-permute-start(bf16[2560,128]{1,0:T(8,128)(2,1)S(1)} %bitcast.12), channel_id=1, source_target_pairs={{0,2},{2,0},{1,3},{3,1},{4,6},{6,4},{5,7},{7,5},{8,10},{10,8},{9,1... | collective-permute-start | bytes 1966088 | tf_op jit(solution)/shard_map/ppermute | solution.py:390
  4.3 0.8 %copy.9 = s32[64,12]{1,0:T(8,128)S(1)} copy(s32[64,12]{0,1:T(8,128)} %param.11) | data formatting | bytes 6144 | tf_op jit(solution)/shard_map/optimization_barrier | solution.py:371
  5.1 0.1 pad_add_fusion.place
  5.2 1.4 %copy-done.1 = bf16[8,6,128,128]{3,2,1,0:T(8,128)(2,1)S(1)} copy-done((bf16[8,6,128,128]{3,2,1,0:T(8,128)(2,1)S(1)}, bf16[8,6,128,128]{3,2,1,0:T(8,128)(2,1)}, u32[]{:S(2)}) %copy-start.1) | copy-done | bytes 1572888
  6.6 0.7 %copy-done.2 = s32[1,1,2,8,4]{3,4,2,1,0:T(4,128)S(1)} copy-done((s32[1,1,2,8,4]{3,4,2,1,0:T(4,128)S(1)}, s32[1,1,2,8,4]{3,4,2,1,0:T(4,128)}, u32[]{:S(2)}) %copy-start.2) | copy-done | bytes 280
  7.3 0.7 %copy-done.6 = s32[64]{0:T(128)S(1)} copy-done((s32[64]{0:T(128)S(1)}, s32[64]{0:T(128)}, u32[]{:S(2)}) %copy-start.6) | copy-done | bytes 280
  7.9 3.0 %band_sums.1 = (bf16[10496,128]{1,0:T(8,128)(2,1)S(1)}, bf16[1296,128]{1,0:T(8,128)(2,1)S(1)}, bf16[1296,128]{1,0:T(8,128)(2,1)S(1)}) custom-call(s32[8,12]{1,0:T(8,128)S(1)} %constant_dynamic-slice_fusion.b_offsets.refs_0_, s32[64]{0:T(128)S(1)} %copy-done.6, s32[3]{0:T(128)S(1)} %pad_add_fusion.place, s32[1,1,2,4,8]{4,3,2,1,0:T(4,128)S(1)} %bitcast.10, ...), custom_call_target="tpu_custom_call" | custom-call | flops 1 | bytes 1 | tf_op jit(solution)/shard_map/band_sums/pallas_call | solution.py:157
  10.9 0.0 copy-start.3
  10.9 0.0 copy-start.5
  10.9 1.6 %collective-permute-start.5 = (bf16[1296,128]{1,0:T(8,128)(2,1)S(1)}, bf16[1296,128]{1,0:T(8,128)(2,1)S(1)}, u32[]{:S(2)}, u32[]{:S(2)}) collective-permute-start(bf16[1296,128]{1,0:T(8,128)(2,1)S(1)} %get-tuple-element.18.refs_0_), channel_id=1, source_target_pairs={{0,2},{2,4},{4,6},{6,8},{8,10},{10,12},{12,14},{14,0},{1,3},{3,5},... | collective-permute-start | bytes 995336 | tf_op jit(solution)/shard_map/ppermute | solution.py:393
  12.5 3.2 %collective-permute-start.3 = (bf16[1296,128]{1,0:T(8,128)(2,1)S(1)}, bf16[1296,128]{1,0:T(8,128)(2,1)S(1)}, u32[]{:S(2)}, u32[]{:S(2)}) collective-permute-start(bf16[1296,128]{1,0:T(8,128)(2,1)S(1)} %get-tuple-element.17), channel_id=1, source_target_pairs={{2,0},{4,2},{6,4},{8,6},{10,8},{12,10},{14,12},{0,14},{3,1},{5,3},... | collective-permute-start | bytes 995336 | tf_op jit(solution)/shard_map/ppermute | solution.py:396
  15.7 0.7 %cut.3 = bf16[1536,128]{1,0:T(8,128)(2,1)S(1)} custom-call(bf16[1,1,2,8,512,128]{5,4,3,2,1,0:T(8,128)(2,1)S(1)} %bitcast.7, bf16[1296,128]{1,0:T(8,128)(2,1)S(1)} %get-tuple-element.18.refs_0_), custom_call_target="tpu_custom_call" | custom-call | flops 1 | bytes 1 | tf_op jit(solution)/shard_map/cut/pallas_call | solution.py:46
  16.4 0.1 collective-permute-start.8
  16.5 10.5 %collective-permute-done.far = bf16[2560,128]{1,0:T(8,128)(2,1)S(1)} collective-permute-done((bf16[2560,128]{1,0:T(8,128)(2,1)S(1)}, bf16[2560,128]{1,0:T(8,128)(2,1)S(1)}, u32[]{:S(2)}, u32[]{:S(2)}) %collective-permute-start) | collective-permute-done | bytes 655392 | tf_op jit(solution)/shard_map/ppermute | solution.py:390
  27.0 0.8 %choose.1 = (bf16[1408,128]{1,0:T(8,128)(2,1)S(1)}, bf16[1168,128]{1,0:T(8,128)(2,1)S(1)}) custom-call(s32[8]{0:T(128)S(1)} %copy-done.5, bf16[1,1,2,8,512,128]{5,4,3,2,1,0:T(8,128)(2,1)S(1)} %bitcast.8, s32[1,1,2,4,8]{4,3,2,1,0:T(4,128)S(1)} %bitcast.11, bf16[2560,128]{1,0:T(8,128)(2,1)S(1)} %collective-permute-done.far), custom_call_target="tpu_custom_call" | custom-call | flops 1 | bytes 1 | tf_op jit(solution)/shard_map/choose/pallas_call | solution.py:103
  27.8 0.1 collective-permute-start.9
  27.9 5.6 %collective-permute-done.5.refs_4_.tail = bf16[1296,128]{1,0:T(8,128)(2,1)S(1)} collective-permute-done((bf16[1296,128]{1,0:T(8,128)(2,1)S(1)}, bf16[1296,128]{1,0:T(8,128)(2,1)S(1)}, u32[]{:S(2)}, u32[]{:S(2)}) %collective-permute-start.5) | collective-permute-done | bytes 331808 | tf_op jit(solution)/shard_map/ppermute | solution.py:393
  33.6 0.5 %collective-permute-done.3.refs_2_.head = bf16[1296,128]{1,0:T(8,128)(2,1)S(1)} collective-permute-done((bf16[1296,128]{1,0:T(8,128)(2,1)S(1)}, bf16[1296,128]{1,0:T(8,128)(2,1)S(1)}, u32[]{:S(2)}, u32[]{:S(2)}) %collective-permute-start.3) | collective-permute-done | bytes 331808 | tf_op jit(solution)/shard_map/ppermute | solution.py:396
  34.1 0.5 %collective-permute-start.2 = (bf16[1168,128]{1,0:T(8,128)(2,1)S(1)}, bf16[1168,128]{1,0:T(8,128)(2,1)S(1)}, u32[]{:S(2)}, u32[]{:S(2)}) collective-permute-start(bf16[1168,128]{1,0:T(8,128)(2,1)S(1)} %get-tuple-element.16.refs_0_.refs_2_), channel_id=1, source_target_pairs={{0,1},{1,0},{2,3},{3,2},{4,5},{5,4},{6,7},{7,6},{8,9},{9,8},{10,11... | collective-permute-start | bytes 897032 | tf_op jit(solution)/shard_map/ppermute | solution.py:387
  34.6 0.7 %cut.2.refs_0_ = bf16[1536,128]{1,0:T(8,128)(2,1)S(1)} custom-call(bf16[1,1,2,8,512,128]{5,4,3,2,1,0:T(8,128)(2,1)S(1)} %bitcast.9, s32[8,12]{1,0:T(8,128)S(1)} %constant_dynamic-slice_fusion.b_offsets.refs_0_), custom_call_target="tpu_custom_call" | custom-call | flops 1 | bytes 1 | tf_op jit(solution)/shard_map/cut/pallas_call | solution.py:46
  35.3 0.0 copy-start.4
  35.4 0.1 collective-permute-start.7
  35.4 0.3 collective-permute-done.4.refs_3_.other_head
  35.7 0.6 %join.1.refs_4_.refs_2_ = bf16[15616,128]{1,0:T(8,128)(2,1)S(1)} custom-call(bf16[10496,128]{1,0:T(8,128)(2,1)S(1)} %get-tuple-element.14.table, bf16[1296,128]{1,0:T(8,128)(2,1)S(1)} %collective-permute-done.5.refs_4_.tail, bf16[1296,128]{1,0:T(8,128)(2,1)S(1)} %collective-permute-done.6.refs_5_.other_tail, ...), custom_call_target="tpu_custom_call" | custom-call | flops 1 | bytes 1 | tf_op jit(solution)/shard_map/join/pallas_call | solution.py:195
  36.4 2.1 %plan.1 = s32[8,128]{1,0:T(8,128)S(1)} custom-call(s32[8]{0:T(128)S(1)} %copy-done.5, s32[64]{0:T(128)S(1)} %copy-done.7, s32[3]{0:T(128)S(1)} %pad_add_fusion.place, s32[8,8]{1,0:T(8,128)S(1)} %copy-done.4, bf16[1168,128]{1,0:T(8,128)(2,1)S(1)} %get-tuple-element.16.refs_0_.refs_2_, bf16[1168,128]{1,0:T(8,128)(2,1)S(1)} %collective-permute-done.2.refs_1_.refs_3_, ...), custom_call_target="tpu_custom_call" | custom-call | flops 1 | bytes 1 | tf_op jit(solution)/shard_map/plan/pallas_call | solution.py:253
  38.5 2.9 %products.3.refs_4_ = bf16[8,4,128,128]{3,2,1,0:T(8,128)(2,1)} custom-call(s32[8,128]{1,0:T(8,128)S(1)} %plan.1, bf16[1408,128]{1,0:T(8,128)(2,1)S(1)} %get-tuple-element.19.refs_0_, bf16[1408,128]{1,0:T(8,128)(2,1)S(1)} %collective-permute-done.9.refs_1_, bf16[1168,128]{1,0:T(8,128)(2,1)S(1)} %get-tuple-element.16.refs_0_.refs_2_, ...), custom_call_target="tpu_custom_call" | custom-call | flops 1 | bytes 1 | tf_op jit(solution)/shard_map/products/pallas_call | solution.py:353
  41.4 0.9 %collective-permute-done.8.refs_1_ = bf16[1536,128]{1,0:T(8,128)(2,1)S(1)} collective-permute-done((bf16[1536,128]{1,0:T(8,128)(2,1)S(1)}, bf16[1536,128]{1,0:T(8,128)(2,1)S(1)}, u32[]{:S(2)}, u32[]{:S(2)}) %collective-permute-start.8) | collective-permute-done | bytes 393248 | tf_op jit(solution)/shard_map/ppermute | solution.py:390
  42.4 1.2 %products.4.refs_3_ = f32[3,2,128,256]{3,2,1,0:T(8,128)S(1)} custom-call(s32[8,128]{1,0:T(8,128)S(1)} %plan.1, bf16[1536,128]{1,0:T(8,128)(2,1)S(1)} %cut.2.refs_0_, bf16[1536,128]{1,0:T(8,128)(2,1)S(1)} %collective-permute-done.8.refs_1_, bf16[15616,128]{1,0:T(8,128)(2,1)S(1)} %join.1.refs_4_.refs_2_), custom_call_target="tpu_custom_call" | custom-call | flops 1 | bytes 1 | tf_op jit(solution)/shard_map/products/pallas_call | solution.py:353
  43.6 0.5 %collective-permute-done.10.refs_1_ = bf16[1536,128]{1,0:T(8,128)(2,1)S(1)} collective-permute-done((bf16[1536,128]{1,0:T(8,128)(2,1)S(1)}, bf16[1536,128]{1,0:T(8,128)(2,1)S(1)}, u32[]{:S(2)}, u32[]{:S(2)}) %collective-permute-start.10) | collective-permute-done | bytes 393248 | tf_op jit(solution)/shard_map/ppermute | solution.py:387
  44.1 1.9 %products.5 = bf16[8,4,128,128]{3,2,1,0:T(8,128)(2,1)} custom-call(s32[8,128]{1,0:T(8,128)S(1)} %plan.1, bf16[1536,128]{1,0:T(8,128)(2,1)S(1)} %collective-permute-done.7.refs_0_, bf16[1536,128]{1,0:T(8,128)(2,1)S(1)} %collective-permute-done.10.refs_1_, bf16[15616,128]{1,0:T(8,128)(2,1)S(1)} %join.1.refs_4_.refs_2_, ...), custom_call_target="tpu_custom_call", output_to_operand_aliasing={{}: (5, {})} | custom-call | flops 1 | bytes 1 | tf_op jit(solution)/shard_map/products/pallas_call | solution.py:353
  (19 shorter events, 0.0 us)
Async XLA Ops:
  0.0 5.2 %collective-permute-start.1 = (bf16[8,6,128,128]{3,2,1,0:T(8,128)(2,1)}, bf16[8,6,128,128]{3,2,1,0:T(8,128)(2,1)}, u32[]{:S(2)}, u32[]{:S(2)}) collective-permute-start(bf16[8,6,128,128]{3,2,1,0:T(8,128)(2,1)} %b_own.1), channel_id=1, source_target_pairs={{0,1},{1,0},{2,3},{3,2},{4,5},{5,4},{6,7},{7,6},{8,9},{9,8},{10,11... | collective-permute-start | bytes 4718600 | tf_op jit(solution)/shard_map/ppermute | solution.py:387
  0.5 15.3 %copy-start = (bf16[1,1,2,8,4,128,128]{6,5,4,3,2,1,0:T(8,128)(2,1)S(1)}, bf16[1,1,2,8,4,128,128]{6,5,4,3,2,1,0:T(8,128)(2,1)}, u32[]{:S(2)}) copy-start(bf16[1,1,2,8,4,128,128]{6,5,4,3,2,1,0:T(8,128)(2,1)} %param.7) | copy-start | bytes 6291460
  1.7 25.2 %collective-permute-start = (bf16[2560,128]{1,0:T(8,128)(2,1)S(1)}, bf16[2560,128]{1,0:T(8,128)(2,1)S(1)}, u32[]{:S(2)}, u32[]{:S(2)}) collective-permute-start(bf16[2560,128]{1,0:T(8,128)(2,1)S(1)} %bitcast.12), channel_id=1, source_target_pairs={{0,2},{2,0},{1,3},{3,1},{4,6},{6,4},{5,7},{7,5},{8,10},{10,8},{9,1... | collective-permute-start | bytes 1966088 | tf_op jit(solution)/shard_map/ppermute | solution.py:390
  5.2 1.4 %copy-start.1 = (bf16[8,6,128,128]{3,2,1,0:T(8,128)(2,1)S(1)}, bf16[8,6,128,128]{3,2,1,0:T(8,128)(2,1)}, u32[]{:S(2)}) copy-start(bf16[8,6,128,128]{3,2,1,0:T(8,128)(2,1)} %b_own.1) | copy-start | bytes 4718596
  6.6 0.7 %copy-start.2 = (s32[1,1,2,8,4]{3,4,2,1,0:T(4,128)S(1)}, s32[1,1,2,8,4]{3,4,2,1,0:T(4,128)}, u32[]{:S(2)}) copy-start(s32[1,1,2,8,4]{3,4,2,1,0:T(4,128)} %param.8) | copy-start | bytes 772
  7.3 0.7 %copy-start.6 = (s32[64]{0:T(128)S(1)}, s32[64]{0:T(128)}, u32[]{:S(2)}) copy-start(s32[64]{0:T(128)} %sizes.3) | copy-start | bytes 772
  10.9 16.1 %copy-start.3 = (s32[1,1,2,8,4]{3,4,2,1,0:T(4,128)S(1)}, s32[1,1,2,8,4]{3,4,2,1,0:T(4,128)}, u32[]{:S(2)}) copy-start(s32[1,1,2,8,4]{3,4,2,1,0:T(4,128)} %param.8) | copy-start | bytes 772
  10.9 16.1 %copy-start.5 = (s32[8]{0:T(128)S(1)}, s32[8]{0:T(128)}, u32[]{:S(2)}) copy-start(s32[8]{0:T(128)} %owner.3) | copy-start | bytes 100
  10.9 22.6 %collective-permute-start.5 = (bf16[1296,128]{1,0:T(8,128)(2,1)S(1)}, bf16[1296,128]{1,0:T(8,128)(2,1)S(1)}, u32[]{:S(2)}, u32[]{:S(2)}) collective-permute-start(bf16[1296,128]{1,0:T(8,128)(2,1)S(1)} %get-tuple-element.18.refs_0_), channel_id=1, source_target_pairs={{0,2},{2,4},{4,6},{6,8},{8,10},{10,12},{12,14},{14,0},{1,3},{3,5},... | collective-permute-start | bytes 995336 | tf_op jit(solution)/shard_map/ppermute | solution.py:393
  12.5 21.6 %collective-permute-start.3 = (bf16[1296,128]{1,0:T(8,128)(2,1)S(1)}, bf16[1296,128]{1,0:T(8,128)(2,1)S(1)}, u32[]{:S(2)}, u32[]{:S(2)}) collective-permute-start(bf16[1296,128]{1,0:T(8,128)(2,1)S(1)} %get-tuple-element.17), channel_id=1, source_target_pairs={{2,0},{4,2},{6,4},{8,6},{10,8},{12,10},{14,12},{0,14},{3,1},{5,3},... | collective-permute-start | bytes 995336 | tf_op jit(solution)/shard_map/ppermute | solution.py:396
  16.4 25.9 %collective-permute-start.8 = (bf16[1536,128]{1,0:T(8,128)(2,1)S(1)}, bf16[1536,128]{1,0:T(8,128)(2,1)S(1)}, u32[]{:S(2)}, u32[]{:S(2)}) collective-permute-start(bf16[1536,128]{1,0:T(8,128)(2,1)S(1)} %cut.3), channel_id=1, source_target_pairs={{0,2},{2,0},{1,3},{3,1},{4,6},{6,4},{5,7},{7,5},{8,10},{10,8},{9,1... | collective-permute-start | bytes 1179656 | tf_op jit(solution)/shard_map/ppermute | solution.py:390
  27.8 10.7 %collective-permute-start.9 = (bf16[1408,128]{1,0:T(8,128)(2,1)S(1)}, bf16[1408,128]{1,0:T(8,128)(2,1)S(1)}, u32[]{:S(2)}, u32[]{:S(2)}) collective-permute-start(bf16[1408,128]{1,0:T(8,128)(2,1)S(1)} %get-tuple-element.19.refs_0_), channel_id=1, source_target_pairs={{0,1},{1,0},{2,3},{3,2},{4,5},{5,4},{6,7},{7,6},{8,9},{9,8},{10,11... | collective-permute-start | bytes 1081352 | tf_op jit(solution)/shard_map/ppermute | solution.py:387
  33.6 1.8 %collective-permute-start.6 = (bf16[1296,128]{1,0:T(8,128)(2,1)S(1)}, bf16[1296,128]{1,0:T(8,128)(2,1)S(1)}, u32[]{:S(2)}, u32[]{:S(2)}) collective-permute-start(bf16[1296,128]{1,0:T(8,128)(2,1)S(1)} %collective-permute-done.5.refs_4_.tail), channel_id=1, source_target_pairs={{0,1},{1,0},{2,3},{3,2},{4,5},{5,4},{6,7},{7,6},{8,9},{9,8},{10,11... | collective-permute-start | bytes 995336 | tf_op jit(solution)/shard_map/ppermute | solution.py:387
  34.1 1.6 %collective-permute-start.4 = (bf16[1296,128]{1,0:T(8,128)(2,1)S(1)}, bf16[1296,128]{1,0:T(8,128)(2,1)S(1)}, u32[]{:S(2)}, u32[]{:S(2)}) collective-permute-start(bf16[1296,128]{1,0:T(8,128)(2,1)S(1)} %collective-permute-done.3.refs_2_.head), channel_id=1, source_target_pairs={{0,1},{1,0},{2,3},{3,2},{4,5},{5,4},{6,7},{7,6},{8,9},{9,8},{10,11... | collective-permute-start | bytes 995336 | tf_op jit(solution)/shard_map/ppermute | solution.py:387
  34.1 2.3 %collective-permute-start.2 = (bf16[1168,128]{1,0:T(8,128)(2,1)S(1)}, bf16[1168,128]{1,0:T(8,128)(2,1)S(1)}, u32[]{:S(2)}, u32[]{:S(2)}) collective-permute-start(bf16[1168,128]{1,0:T(8,128)(2,1)S(1)} %get-tuple-element.16.refs_0_.refs_2_), channel_id=1, source_target_pairs={{0,1},{1,0},{2,3},{3,2},{4,5},{5,4},{6,7},{7,6},{8,9},{9,8},{10,11... | collective-permute-start | bytes 897032 | tf_op jit(solution)/shard_map/ppermute | solution.py:387
  35.3 1.1 %copy-start.4 = (s32[8,8]{1,0:T(8,128)S(1)}, s32[8,8]{1,0:T(8,128)}, u32[]{:S(2)}) copy-start(s32[8,8]{1,0:T(8,128)} %c_offsets.1) | copy-start | bytes 772
  35.3 1.1 %copy-start.7 = (s32[64]{0:T(128)S(1)}, s32[64]{0:T(128)}, u32[]{:S(2)}) copy-start(s32[64]{0:T(128)} %sizes.3) | copy-start | bytes 772
  35.4 8.2 %collective-permute-start.7 = (bf16[1536,128]{1,0:T(8,128)(2,1)S(1)}, bf16[1536,128]{1,0:T(8,128)(2,1)S(1)}, u32[]{:S(2)}, u32[]{:S(2)}) collective-permute-start(bf16[1536,128]{1,0:T(8,128)(2,1)S(1)} %cut.2.refs_0_), channel_id=1, source_target_pairs={{0,1},{1,0},{2,3},{3,2},{4,5},{5,4},{6,7},{7,6},{8,9},{9,8},{10,11... | collective-permute-start | bytes 1179656 | tf_op jit(solution)/shard_map/ppermute | solution.py:387
  42.3 1.7 %collective-permute-start.10 = (bf16[1536,128]{1,0:T(8,128)(2,1)S(1)}, bf16[1536,128]{1,0:T(8,128)(2,1)S(1)}, u32[]{:S(2)}, u32[]{:S(2)}) collective-permute-start(bf16[1536,128]{1,0:T(8,128)(2,1)S(1)} %collective-permute-done.8.refs_1_), channel_id=1, source_target_pairs={{0,1},{1,0},{2,3},{3,2},{4,5},{5,4},{6,7},{7,6},{8,9},{9,8},{10,11... | collective-permute-start | bytes 1179656 | tf_op jit(solution)/shard_map/ppermute | solution.py:387

commit v6 on v5

--- a/solution.py
+++ b/solution.py
@@ -58,7 +58,7 @@
     )(a_rows, earlier)
 
 
-def choose_kernel(chosen, owner, a_rows, offsets, far, first, second, raw, sem):
+def choose_kernel(chosen, owner, a_rows, offsets, far_first, far_second, first, second, raw, sem):
     height, tile = a_rows.shape[4:]
     me = lax.axis_index("col")
     mine = owner[0] == me
@@ -70,20 +70,17 @@
 
     def run(here):
         if here:
-            pairs = []
-            for i, p in enumerate(chosen):
-                low, high = i * height, (i + 1) * height
-                middle = min(max(split, low), high)
-                for out, base, i0, i1 in ((first, 0, low, middle), (second, split, middle, high)):
-                    if i0 < i1:
-                        src = a_rows.at[0, 0, me, p, pl.ds(i0 - low, i1 - i0)]
-                        pairs.append((src, out.at[pl.ds(i0 - base, i1 - i0)]))
+            sources = [(a_rows.at[0, 0, me, p], i * height, height) for i, p in enumerate(chosen)]
         else:
-            pairs = [
-                (far.at[pl.ds(0, split)], first),
-                (far.at[pl.ds(split, rest)], second.at[pl.ds(0, rest)]),
-            ]
-        moves = [pltpu.make_async_copy(*p, sem.at[i]) for i, p in enumerate(pairs)]
+            n = far_first.shape[0]
+            sources = [(far_first, 0, n), (far_second, n, end - n)]
+        moves = []
+        for ref, start, size in sources:
+            for out, low, high in ((first, 0, split), (second, split, end)):
+                i0, i1 = max(start, low), min(start + size, high)
+                if i0 < i1:
+                    src, dst = ref.at[pl.ds(i0 - start, i1 - i0)], out.at[pl.ds(i0 - low, i1 - i0)]
+                    moves.append(pltpu.make_async_copy(src, dst, sem.at[len(moves)]))
         for m in moves:
             m.start()
         for m in moves:
@@ -98,12 +95,12 @@
 
 
 def choose(owner, a_rows, offsets, far, chosen, split):
-    tile = a_rows.shape[5]
+    height, tile = a_rows.shape[4:]
     shape = lambda n: jax.ShapeDtypeStruct((n, tile), a_rows.dtype)
     return pl.pallas_call(
         functools.partial(choose_kernel, chosen),
-        out_shape=(shape(split), shape(far.shape[0] - split + 16)),
-        in_specs=[SMEM] + [ANY] * 3,
+        out_shape=(shape(split), shape(len(chosen) * height - split + 16)),
+        in_specs=[SMEM] + [ANY] * 4,
         out_specs=(VMEM, VMEM),
         scratch_shapes=[
             pltpu.VMEM(offsets.shape[3:], jnp.int32),
@@ -111,7 +108,7 @@
         ],
         name="choose",
         **settings(8),
-    )(owner, a_rows, offsets, far)
+    )(owner, a_rows, offsets, *far)
 
 
 def band_kernel(b_offsets, sizes, place, offsets, b_own, b_peer, table, tail, head, total):
@@ -403,19 +400,25 @@
     whole = cols == 2 and bucket == atoms
     common = dict(slots=slots, atoms=atoms, half=half)
     if whole:
-        at = (0, 0, 1 - me, inner[0], 0, 0)
-        sent = lax.dynamic_slice(a_rows, at, (1, 1, 1, len(inner)) + a_rows.shape[4:])
-        sent = sent.reshape(-1, tile)
-        b_offsets = after(b_offsets, sent)
+        all_rows = a_tiles.reshape(a_tiles.shape[:3] + (-1, tile))
+        p0, count = inner[0] * half * tile, len(inner) * half * tile
+        cut_at = (count + tile) // 2
+
+        def part(at, n):
+            rows = lax.dynamic_slice(all_rows, (0, 0, 1 - me, at, 0), (1, 1, 1, n, tile))
+            return rows.reshape(n, tile)
+
+        sent = part(p0, cut_at), part(p0 + cut_at, count - cut_at)
+        b_offsets = after(b_offsets, *sent)
         b_peer = across(b_tiles)
         own_rows = lax.dynamic_slice_in_dim(b_offsets, start, atoms, 0)
-        far = swap(sent)
+        far = [swap(x) for x in sent]
         table, tail, head = band_sums(own_rows, block_sizes, place, offsets, b_tiles, b_peer)
         rest = cut(a_rows, outer, tail)
         tail, head = onward(tail), back(head)
         rest = swap(rest)
         split = (len(inner) * half // 2 + 1) * tile
-        far = choose(atom_owner, a_rows, offsets, after(far, table), inner, split)
+        far = choose(atom_owner, a_rows, offsets, [after(f, table) for f in far], inner, split)
         far = [(f, across(f)) for f in far]
         tail, head = (tail, across(tail)), (head, across(head))
         plan = make_plan(atom_owner, block_sizes, place, c_offsets, half, far[-1], head, tail)

time: 46.2 us -> 46 us (level)
  waiting for transfers between devices: 18.4 us -> 16.9 us
  local copies, waits for them, and re-layouts: 4.84 us -> 5.56 us
  starting transfers between devices: 8.52 us -> 8.99 us
    reshape x0 -> x2, local copies, waits for them, and re-layouts: none -> 1.99 us  [part(): return rows.reshape(n, tile)]
    ppermute x2 -> x3, waiting for transfers between devices: 11.4 us -> 9.9 us  [swap(): return lax.ppermute(x, 'col', [(0, 1), (1, 0)])]
    dynamic_slice x1 -> x0, local copies, waits for them, and re-layouts: 1.28 us -> none  [local(): lax.dynamic_slice(a_rows, at, (1, 1, 1, len(inner)) + a_rows.shape[4:])]
    ppermute x2 -> x3, starting transfers between devices: 2.63 us -> 2.84 us  [swap(): return lax.ppermute(x, 'col', [(0, 1), (1, 0)])]
  transfers between devices with their start and end apart: 11 -> 12, of which waited for: 6 -> 6; matrix products, arithmetic and copies ran while one was open for 5% -> 6% of each run, Pallas kernels for 26% -> 26%
where the time goes in v6:
time: 46 us; the launch traced here: 45.7 us
  waiting for transfers between devices  16.9 us (37%)
  Pallas kernels  14 us (30%)
  starting transfers between devices  8.99 us (20%)
  local copies, waits for them, and re-layouts  5.56 us (12%)
    ppermute x3, waiting for transfers between devices, swap(): return lax.ppermute(x, 'col', [(0, 1), (1, 0)])  9.9 us
    pallas_call x3, Pallas kernels, products(): pl.pallas_call(functools.partial(product_kernel, cfg), out_shape=out_shap...  6 us
    ppermute x1, waiting for transfers between devices, onward(): lax.ppermute(x, ('row', 'col'), [(i, (i + 1) % cycle) for i in range(cycl...  5.64 us
    ppermute x1, starting transfers between devices, back(): lax.ppermute(x, ('row', 'col'), [((i + 1) % cycle, i) for i in range(cycl...  3.11 us
    pallas_call x1, Pallas kernels, band_sums(): pl.pallas_call(band_kernel, out_shape=(shape(2 * (atoms * WIDTH + 1) * ti...  2.98 us
    ppermute x3, starting transfers between devices, swap(): return lax.ppermute(x, 'col', [(0, 1), (1, 0)])  2.84 us
    unnamed x16, local copies, waits for them, and re-layouts  2.78 us
    pallas_call x1, Pallas kernels, make_plan(): pl.pallas_call(functools.partial(plan_kernel, half, len(pairs)), out_shap...  2.11 us
  transfers between devices with their start and end apart: 12, of which 6 were waited for; matrix products, arithmetic and copies ran while one was open for 6% of the time, Pallas kernels for 26%

profile of v6, /device:TPU:0, one launch (start us, length us, event | category | flops | bytes accessed | tf_op | source)
XLA Modules:
  0.0 45.7 jit_solution(8771177197327787104)
XLA Ops:
  0.0 0.5 collective-permute-start.1
  0.5 1.0 %dynamic-slice_bitcast_fusion.1 = bf16[1216,128]{1,0:T(8,128)(2,1)S(1)} fusion(bf16[1,1,2,4096,128]{4,3,2,1,0:T(8,128)(2,1)} %bitcast.10, s32[]{:T(128)S(6)} %select_n.7), kind=kLoop, calls=%fused_computation.1 | loop fusion | bytes 622596 | tf_op jit(solution)/shard_map/reshape | solution.py:409
  1.4 0.0 copy-start
  1.5 2.6 %collective-permute-start.2 = (bf16[1216,128]{1,0:T(8,128)(2,1)S(1)}, bf16[1216,128]{1,0:T(8,128)(2,1)S(1)}, u32[]{:S(2)}, u32[]{:S(2)}) collective-permute-start(bf16[1216,128]{1,0:T(8,128)(2,1)S(1)} %dynamic-slice_bitcast_fusion.1), channel_id=1, source_target_pairs={{0,2},{2,0},{1,3},{3,1},{4,6},{6,4},{5,7},{7,5},{8,10},{10,8},{9,1... | collective-permute-start | bytes 933896 | tf_op jit(solution)/shard_map/ppermute | solution.py:387
  4.0 1.0 %dynamic-slice_bitcast_fusion = bf16[1344,128]{1,0:T(8,128)(2,1)S(1)} fusion(bf16[1,1,2,4096,128]{4,3,2,1,0:T(8,128)(2,1)} %bitcast.11, s32[]{:T(128)S(6)} %select_n.7), kind=kLoop, calls=%fused_computation | loop fusion | bytes 688132 | tf_op jit(solution)/shard_map/reshape | solution.py:409
  5.0 0.2 collective-permute-start
  5.2 0.8 %copy.9 = s32[64,12]{1,0:T(8,128)S(1)} copy(s32[64,12]{0,1:T(8,128)} %param.11) | data formatting | bytes 6144 | tf_op jit(solution)/shard_map/optimization_barrier | solution.py:368
  6.0 0.1 pad_add_fusion.place
  6.1 1.4 %copy-done.1 = bf16[8,6,128,128]{3,2,1,0:T(8,128)(2,1)S(1)} copy-done((bf16[8,6,128,128]{3,2,1,0:T(8,128)(2,1)S(1)}, bf16[8,6,128,128]{3,2,1,0:T(8,128)(2,1)}, u32[]{:S(2)}) %copy-start.1) | copy-done | bytes 1572888
  7.5 0.7 %copy-done.2 = s32[1,1,2,8,4]{3,4,2,1,0:T(4,128)S(1)} copy-done((s32[1,1,2,8,4]{3,4,2,1,0:T(4,128)S(1)}, s32[1,1,2,8,4]{3,4,2,1,0:T(4,128)}, u32[]{:S(2)}) %copy-start.2) | copy-done | bytes 280
  8.2 0.7 %copy-done.6 = s32[64]{0:T(128)S(1)} copy-done((s32[64]{0:T(128)S(1)}, s32[64]{0:T(128)}, u32[]{:S(2)}) %copy-start.6) | copy-done | bytes 280
  8.9 3.0 %band_sums.1 = (bf16[10496,128]{1,0:T(8,128)(2,1)S(1)}, bf16[1296,128]{1,0:T(8,128)(2,1)S(1)}, bf16[1296,128]{1,0:T(8,128)(2,1)S(1)}) custom-call(s32[8,12]{1,0:T(8,128)S(1)} %constant_dynamic-slice_fusion.b_offsets.refs_0_, s32[64]{0:T(128)S(1)} %copy-done.6, s32[3]{0:T(128)S(1)} %pad_add_fusion.place, s32[1,1,2,4,8]{4,3,2,1,0:T(4,128)S(1)} %bitcast.15, ...), custom_call_target="tpu_custom_call" | custom-call | flops 1 | bytes 1 | tf_op jit(solution)/shard_map/band_sums/pallas_call | solution.py:154
  11.9 1.9 %collective-permute-start.6 = (bf16[1296,128]{1,0:T(8,128)(2,1)S(1)}, bf16[1296,128]{1,0:T(8,128)(2,1)S(1)}, u32[]{:S(2)}, u32[]{:S(2)}) collective-permute-start(bf16[1296,128]{1,0:T(8,128)(2,1)S(1)} %get-tuple-element.20.refs_0_), channel_id=1, source_target_pairs={{0,2},{2,4},{4,6},{6,8},{8,10},{10,12},{12,14},{14,0},{1,3},{3,5},... | collective-permute-start | bytes 995336 | tf_op jit(solution)/shard_map/ppermute | solution.py:390
  13.8 3.1 %collective-permute-start.4 = (bf16[1296,128]{1,0:T(8,128)(2,1)S(1)}, bf16[1296,128]{1,0:T(8,128)(2,1)S(1)}, u32[]{:S(2)}, u32[]{:S(2)}) collective-permute-start(bf16[1296,128]{1,0:T(8,128)(2,1)S(1)} %get-tuple-element.19), channel_id=1, source_target_pairs={{2,0},{4,2},{6,4},{8,6},{10,8},{12,10},{14,12},{0,14},{3,1},{5,3},... | collective-permute-start | bytes 995336 | tf_op jit(solution)/shard_map/ppermute | solution.py:393
  16.9 0.7 %cut.3 = bf16[1536,128]{1,0:T(8,128)(2,1)S(1)} custom-call(bf16[1,1,2,8,512,128]{5,4,3,2,1,0:T(8,128)(2,1)S(1)} %bitcast.12, bf16[1296,128]{1,0:T(8,128)(2,1)S(1)} %get-tuple-element.20.refs_0_), custom_call_target="tpu_custom_call" | custom-call | flops 1 | bytes 1 | tf_op jit(solution)/shard_map/cut/pallas_call | solution.py:46
  17.6 0.1 collective-permute-start.9
  17.7 9.0 %collective-permute-done.far_first = bf16[1344,128]{1,0:T(8,128)(2,1)S(1)} collective-permute-done((bf16[1344,128]{1,0:T(8,128)(2,1)S(1)}, bf16[1344,128]{1,0:T(8,128)(2,1)S(1)}, u32[]{:S(2)}, u32[]{:S(2)}) %collective-permute-start) | collective-permute-done | bytes 344096 | tf_op jit(solution)/shard_map/ppermute | solution.py:387
  26.7 0.8 %choose.1 = (bf16[1408,128]{1,0:T(8,128)(2,1)S(1)}, bf16[1168,128]{1,0:T(8,128)(2,1)S(1)}) custom-call(s32[8]{0:T(128)S(1)} %copy-done.5, bf16[1,1,2,8,512,128]{5,4,3,2,1,0:T(8,128)(2,1)S(1)} %bitcast.13, s32[1,1,2,4,8]{4,3,2,1,0:T(4,128)S(1)} %bitcast.16, bf16[1344,128]{1,0:T(8,128)(2,1)S(1)} %collective-permute-done.far_first, ...), custom_call_target="tpu_custom_call" | custom-call | flops 1 | bytes 1 | tf_op jit(solution)/shard_map/choose/pallas_call | solution.py:100
  27.6 0.1 collective-permute-start.10
  27.6 5.6 %collective-permute-done.6.refs_4_.tail = bf16[1296,128]{1,0:T(8,128)(2,1)S(1)} collective-permute-done((bf16[1296,128]{1,0:T(8,128)(2,1)S(1)}, bf16[1296,128]{1,0:T(8,128)(2,1)S(1)}, u32[]{:S(2)}, u32[]{:S(2)}) %collective-permute-start.6) | collective-permute-done | bytes 331808 | tf_op jit(solution)/shard_map/ppermute | solution.py:390
  33.3 0.5 %collective-permute-done.4.refs_2_.head = bf16[1296,128]{1,0:T(8,128)(2,1)S(1)} collective-permute-done((bf16[1296,128]{1,0:T(8,128)(2,1)S(1)}, bf16[1296,128]{1,0:T(8,128)(2,1)S(1)}, u32[]{:S(2)}, u32[]{:S(2)}) %collective-permute-start.4) | collective-permute-done | bytes 331808 | tf_op jit(solution)/shard_map/ppermute | solution.py:393
  33.8 0.5 %collective-permute-start.3 = (bf16[1168,128]{1,0:T(8,128)(2,1)S(1)}, bf16[1168,128]{1,0:T(8,128)(2,1)S(1)}, u32[]{:S(2)}, u32[]{:S(2)}) collective-permute-start(bf16[1168,128]{1,0:T(8,128)(2,1)S(1)} %get-tuple-element.18.refs_0_.refs_2_), channel_id=1, source_target_pairs={{0,1},{1,0},{2,3},{3,2},{4,5},{5,4},{6,7},{7,6},{8,9},{9,8},{10,11... | collective-permute-start | bytes 897032 | tf_op jit(solution)/shard_map/ppermute | solution.py:384
  34.3 0.7 %cut.2.refs_0_ = bf16[1536,128]{1,0:T(8,128)(2,1)S(1)} custom-call(bf16[1,1,2,8,512,128]{5,4,3,2,1,0:T(8,128)(2,1)S(1)} %bitcast.14, s32[8,12]{1,0:T(8,128)S(1)} %constant_dynamic-slice_fusion.b_offsets.refs_0_), custom_call_target="tpu_custom_call" | custom-call | flops 1 | bytes 1 | tf_op jit(solution)/shard_map/cut/pallas_call | solution.py:46
  35.1 0.1 collective-permute-start.8
  35.1 0.3 collective-permute-done.5.refs_3_.other_head
  35.5 0.6 %join.1.refs_4_.refs_2_ = bf16[15616,128]{1,0:T(8,128)(2,1)S(1)} custom-call(bf16[10496,128]{1,0:T(8,128)(2,1)S(1)} %get-tuple-element.15.table, bf16[1296,128]{1,0:T(8,128)(2,1)S(1)} %collective-permute-done.6.refs_4_.tail, bf16[1296,128]{1,0:T(8,128)(2,1)S(1)} %collective-permute-done.7.refs_5_.other_tail, ...), custom_call_target="tpu_custom_call" | custom-call | flops 1 | bytes 1 | tf_op jit(solution)/shard_map/join/pallas_call | solution.py:192
  36.1 2.1 %plan.1 = s32[8,128]{1,0:T(8,128)S(1)} custom-call(s32[8]{0:T(128)S(1)} %copy-done.5, s32[64]{0:T(128)S(1)} %copy-done.7, s32[3]{0:T(128)S(1)} %pad_add_fusion.place, s32[8,8]{1,0:T(8,128)S(1)} %copy-done.4, bf16[1168,128]{1,0:T(8,128)(2,1)S(1)} %get-tuple-element.18.refs_0_.refs_2_, bf16[1168,128]{1,0:T(8,128)(2,1)S(1)} %collective-permute-done.3.refs_1_.refs_3_, ...), custom_call_target="tpu_custom_call" | custom-call | flops 1 | bytes 1 | tf_op jit(solution)/shard_map/plan/pallas_call | solution.py:250
  38.3 2.9 %products.3.refs_4_ = bf16[8,4,128,128]{3,2,1,0:T(8,128)(2,1)} custom-call(s32[8,128]{1,0:T(8,128)S(1)} %plan.1, bf16[1408,128]{1,0:T(8,128)(2,1)S(1)} %get-tuple-element.21.refs_0_, bf16[1408,128]{1,0:T(8,128)(2,1)S(1)} %collective-permute-done.10.refs_1_, bf16[1168,128]{1,0:T(8,128)(2,1)S(1)} %get-tuple-element.18.refs_0_.refs_2_, ...), custom_call_target="tpu_custom_call" | custom-call | flops 1 | bytes 1 | tf_op jit(solution)/shard_map/products/pallas_call | solution.py:350
  41.2 0.9 %collective-permute-done.9.refs_1_ = bf16[1536,128]{1,0:T(8,128)(2,1)S(1)} collective-permute-done((bf16[1536,128]{1,0:T(8,128)(2,1)S(1)}, bf16[1536,128]{1,0:T(8,128)(2,1)S(1)}, u32[]{:S(2)}, u32[]{:S(2)}) %collective-permute-start.9) | collective-permute-done | bytes 393248 | tf_op jit(solution)/shard_map/ppermute | solution.py:387
  42.1 1.2 %products.4.refs_3_ = f32[3,2,128,256]{3,2,1,0:T(8,128)S(1)} custom-call(s32[8,128]{1,0:T(8,128)S(1)} %plan.1, bf16[1536,128]{1,0:T(8,128)(2,1)S(1)} %cut.2.refs_0_, bf16[1536,128]{1,0:T(8,128)(2,1)S(1)} %collective-permute-done.9.refs_1_, bf16[15616,128]{1,0:T(8,128)(2,1)S(1)} %join.1.refs_4_.refs_2_), custom_call_target="tpu_custom_call" | custom-call | flops 1 | bytes 1 | tf_op jit(solution)/shard_map/products/pallas_call | solution.py:350
  43.3 0.5 %collective-permute-done.11.refs_1_ = bf16[1536,128]{1,0:T(8,128)(2,1)S(1)} collective-permute-done((bf16[1536,128]{1,0:T(8,128)(2,1)S(1)}, bf16[1536,128]{1,0:T(8,128)(2,1)S(1)}, u32[]{:S(2)}, u32[]{:S(2)}) %collective-permute-start.11) | collective-permute-done | bytes 393248 | tf_op jit(solution)/shard_map/ppermute | solution.py:384
  43.8 1.9 %products.5 = bf16[8,4,128,128]{3,2,1,0:T(8,128)(2,1)} custom-call(s32[8,128]{1,0:T(8,128)S(1)} %plan.1, bf16[1536,128]{1,0:T(8,128)(2,1)S(1)} %collective-permute-done.8.refs_0_, bf16[1536,128]{1,0:T(8,128)(2,1)S(1)} %collective-permute-done.11.refs_1_, bf16[15616,128]{1,0:T(8,128)(2,1)S(1)} %join.1.refs_4_.refs_2_, ...), custom_call_target="tpu_custom_call", output_to_operand_aliasing={{}: (5, {})} | custom-call | flops 1 | bytes 1 | tf_op jit(solution)/shard_map/products/pallas_call | solution.py:350
  (22 shorter events, 0.1 us)
Async XLA Ops:
  0.0 6.1 %collective-permute-start.1 = (bf16[8,6,128,128]{3,2,1,0:T(8,128)(2,1)}, bf16[8,6,128,128]{3,2,1,0:T(8,128)(2,1)}, u32[]{:S(2)}, u32[]{:S(2)}) collective-permute-start(bf16[8,6,128,128]{3,2,1,0:T(8,128)(2,1)} %b_own.1), channel_id=1, source_target_pairs={{0,1},{1,0},{2,3},{3,2},{4,5},{5,4},{6,7},{7,6},{8,9},{9,8},{10,11... | collective-permute-start | bytes 4718600 | tf_op jit(solution)/shard_map/ppermute | solution.py:384
  1.4 15.5 %copy-start = (bf16[1,1,2,8,4,128,128]{6,5,4,3,2,1,0:T(8,128)(2,1)S(1)}, bf16[1,1,2,8,4,128,128]{6,5,4,3,2,1,0:T(8,128)(2,1)}, u32[]{:S(2)}) copy-start(bf16[1,1,2,8,4,128,128]{6,5,4,3,2,1,0:T(8,128)(2,1)} %param.7) | copy-start | bytes 6291460
  1.5 16.2 %collective-permute-start.2 = (bf16[1216,128]{1,0:T(8,128)(2,1)S(1)}, bf16[1216,128]{1,0:T(8,128)(2,1)S(1)}, u32[]{:S(2)}, u32[]{:S(2)}) collective-permute-start(bf16[1216,128]{1,0:T(8,128)(2,1)S(1)} %dynamic-slice_bitcast_fusion.1), channel_id=1, source_target_pairs={{0,2},{2,0},{1,3},{3,1},{4,6},{6,4},{5,7},{7,5},{8,10},{10,8},{9,1... | collective-permute-start | bytes 933896 | tf_op jit(solution)/shard_map/ppermute | solution.py:387
  5.0 21.7 %collective-permute-start = (bf16[1344,128]{1,0:T(8,128)(2,1)S(1)}, bf16[1344,128]{1,0:T(8,128)(2,1)S(1)}, u32[]{:S(2)}, u32[]{:S(2)}) collective-permute-start(bf16[1344,128]{1,0:T(8,128)(2,1)S(1)} %dynamic-slice_bitcast_fusion), channel_id=1, source_target_pairs={{0,2},{2,0},{1,3},{3,1},{4,6},{6,4},{5,7},{7,5},{8,10},{10,8},{9,1... | collective-permute-start | bytes 1032200 | tf_op jit(solution)/shard_map/ppermute | solution.py:387
  6.1 1.4 %copy-start.1 = (bf16[8,6,128,128]{3,2,1,0:T(8,128)(2,1)S(1)}, bf16[8,6,128,128]{3,2,1,0:T(8,128)(2,1)}, u32[]{:S(2)}) copy-start(bf16[8,6,128,128]{3,2,1,0:T(8,128)(2,1)} %b_own.1) | copy-start | bytes 4718596
  7.5 0.7 %copy-start.2 = (s32[1,1,2,8,4]{3,4,2,1,0:T(4,128)S(1)}, s32[1,1,2,8,4]{3,4,2,1,0:T(4,128)}, u32[]{:S(2)}) copy-start(s32[1,1,2,8,4]{3,4,2,1,0:T(4,128)} %param.8) | copy-start | bytes 772
  8.2 0.7 %copy-start.6 = (s32[64]{0:T(128)S(1)}, s32[64]{0:T(128)}, u32[]{:S(2)}) copy-start(s32[64]{0:T(128)} %sizes.3) | copy-start | bytes 772
  11.8 14.9 %copy-start.3 = (s32[1,1,2,8,4]{3,4,2,1,0:T(4,128)S(1)}, s32[1,1,2,8,4]{3,4,2,1,0:T(4,128)}, u32[]{:S(2)}) copy-start(s32[1,1,2,8,4]{3,4,2,1,0:T(4,128)} %param.8) | copy-start | bytes 772
  11.9 14.9 %copy-start.5 = (s32[8]{0:T(128)S(1)}, s32[8]{0:T(128)}, u32[]{:S(2)}) copy-start(s32[8]{0:T(128)} %owner.3) | copy-start | bytes 100
  11.9 21.4 %collective-permute-start.6 = (bf16[1296,128]{1,0:T(8,128)(2,1)S(1)}, bf16[1296,128]{1,0:T(8,128)(2,1)S(1)}, u32[]{:S(2)}, u32[]{:S(2)}) collective-permute-start(bf16[1296,128]{1,0:T(8,128)(2,1)S(1)} %get-tuple-element.20.refs_0_), channel_id=1, source_target_pairs={{0,2},{2,4},{4,6},{6,8},{8,10},{10,12},{12,14},{14,0},{1,3},{3,5},... | collective-permute-start | bytes 995336 | tf_op jit(solution)/shard_map/ppermute | solution.py:390
  13.8 20.0 %collective-permute-start.4 = (bf16[1296,128]{1,0:T(8,128)(2,1)S(1)}, bf16[1296,128]{1,0:T(8,128)(2,1)S(1)}, u32[]{:S(2)}, u32[]{:S(2)}) collective-permute-start(bf16[1296,128]{1,0:T(8,128)(2,1)S(1)} %get-tuple-element.19), channel_id=1, source_target_pairs={{2,0},{4,2},{6,4},{8,6},{10,8},{12,10},{14,12},{0,14},{3,1},{5,3},... | collective-permute-start | bytes 995336 | tf_op jit(solution)/shard_map/ppermute | solution.py:393
  17.6 24.4 %collective-permute-start.9 = (bf16[1536,128]{1,0:T(8,128)(2,1)S(1)}, bf16[1536,128]{1,0:T(8,128)(2,1)S(1)}, u32[]{:S(2)}, u32[]{:S(2)}) collective-permute-start(bf16[1536,128]{1,0:T(8,128)(2,1)S(1)} %cut.3), channel_id=1, source_target_pairs={{0,2},{2,0},{1,3},{3,1},{4,6},{6,4},{5,7},{7,5},{8,10},{10,8},{9,1... | collective-permute-start | bytes 1179656 | tf_op jit(solution)/shard_map/ppermute | solution.py:387
  27.6 10.7 %collective-permute-start.10 = (bf16[1408,128]{1,0:T(8,128)(2,1)S(1)}, bf16[1408,128]{1,0:T(8,128)(2,1)S(1)}, u32[]{:S(2)}, u32[]{:S(2)}) collective-permute-start(bf16[1408,128]{1,0:T(8,128)(2,1)S(1)} %get-tuple-element.21.refs_0_), channel_id=1, source_target_pairs={{0,1},{1,0},{2,3},{3,2},{4,5},{5,4},{6,7},{7,6},{8,9},{9,8},{10,11... | collective-permute-start | bytes 1081352 | tf_op jit(solution)/shard_map/ppermute | solution.py:384
  33.3 1.8 %collective-permute-start.7 = (bf16[1296,128]{1,0:T(8,128)(2,1)S(1)}, bf16[1296,128]{1,0:T(8,128)(2,1)S(1)}, u32[]{:S(2)}, u32[]{:S(2)}) collective-permute-start(bf16[1296,128]{1,0:T(8,128)(2,1)S(1)} %collective-permute-done.6.refs_4_.tail), channel_id=1, source_target_pairs={{0,1},{1,0},{2,3},{3,2},{4,5},{5,4},{6,7},{7,6},{8,9},{9,8},{10,11... | collective-permute-start | bytes 995336 | tf_op jit(solution)/shard_map/ppermute | solution.py:384
  33.8 1.6 %collective-permute-start.5 = (bf16[1296,128]{1,0:T(8,128)(2,1)S(1)}, bf16[1296,128]{1,0:T(8,128)(2,1)S(1)}, u32[]{:S(2)}, u32[]{:S(2)}) collective-permute-start(bf16[1296,128]{1,0:T(8,128)(2,1)S(1)} %collective-permute-done.4.refs_2_.head), channel_id=1, source_target_pairs={{0,1},{1,0},{2,3},{3,2},{4,5},{5,4},{6,7},{7,6},{8,9},{9,8},{10,11... | collective-permute-start | bytes 995336 | tf_op jit(solution)/shard_map/ppermute | solution.py:384
  33.8 2.3 %collective-permute-start.3 = (bf16[1168,128]{1,0:T(8,128)(2,1)S(1)}, bf16[1168,128]{1,0:T(8,128)(2,1)S(1)}, u32[]{:S(2)}, u32[]{:S(2)}) collective-permute-start(bf16[1168,128]{1,0:T(8,128)(2,1)S(1)} %get-tuple-element.18.refs_0_.refs_2_), channel_id=1, source_target_pairs={{0,1},{1,0},{2,3},{3,2},{4,5},{5,4},{6,7},{7,6},{8,9},{9,8},{10,11... | collective-permute-start | bytes 897032 | tf_op jit(solution)/shard_map/ppermute | solution.py:384
  35.0 1.1 %copy-start.4 = (s32[8,8]{1,0:T(8,128)S(1)}, s32[8,8]{1,0:T(8,128)}, u32[]{:S(2)}) copy-start(s32[8,8]{1,0:T(8,128)} %c_offsets.1) | copy-start | bytes 772
  35.0 1.1 %copy-start.7 = (s32[64]{0:T(128)S(1)}, s32[64]{0:T(128)}, u32[]{:S(2)}) copy-start(s32[64]{0:T(128)} %sizes.3) | copy-start | bytes 772
  35.1 8.2 %collective-permute-start.8 = (bf16[1536,128]{1,0:T(8,128)(2,1)S(1)}, bf16[1536,128]{1,0:T(8,128)(2,1)S(1)}, u32[]{:S(2)}, u32[]{:S(2)}) collective-permute-start(bf16[1536,128]{1,0:T(8,128)(2,1)S(1)} %cut.2.refs_0_), channel_id=1, source_target_pairs={{0,1},{1,0},{2,3},{3,2},{4,5},{5,4},{6,7},{7,6},{8,9},{9,8},{10,11... | collective-permute-start | bytes 1179656 | tf_op jit(solution)/shard_map/ppermute | solution.py:384
  42.1 1.7 %collective-permute-start.11 = (bf16[1536,128]{1,0:T(8,128)(2,1)S(1)}, bf16[1536,128]{1,0:T(8,128)(2,1)S(1)}, u32[]{:S(2)}, u32[]{:S(2)}) collective-permute-start(bf16[1536,128]{1,0:T(8,128)(2,1)S(1)} %collective-permute-done.9.refs_1_), channel_id=1, source_target_pairs={{0,1},{1,0},{2,3},{3,2},{4,5},{5,4},{6,7},{7,6},{8,9},{9,8},{10,11... | collective-permute-start | bytes 1179656 | tf_op jit(solution)/shard_map/ppermute | solution.py:384

commit v7 on v6

--- a/solution.py
+++ b/solution.py
@@ -111,7 +111,7 @@
     )(owner, a_rows, offsets, *far)
 
 
-def band_kernel(b_offsets, sizes, place, offsets, b_own, b_peer, table, tail, head, total):
+def band_kernel(pairwise, b_offsets, sizes, place, offsets, b_own, b_peer, table, first, second, total):
     atoms, half, tile, _ = b_own.shape
     blocks = sizes.shape[0]
     start, layer = place[0], place[1]
@@ -142,17 +142,20 @@
     there = 1 - place[2] if offsets.shape[2] == 2 else 0
     values = offsets[0, 0, pl.ds(there, 1)].reshape(places).astype(jnp.float32)
     values = jnp.pad(values, ((0, 16 - places[0]), (0, tile - places[1]))).astype(jnp.bfloat16)
-    for out, row in ((tail, atoms - BAND + layer), (head, layer)):
+    rows = atoms - BAND + layer, layer
+    if pairwise:
+        rows = [jnp.where(place[2] == 0, rows[i], rows[1 - i]) for i in range(2)]
+    for out, row in zip((first, second), rows, strict=True):
         out[pl.ds(0, height)] = table[pl.ds(row * height, height)]
         out[pl.ds(height, 16)] = values
 
 
-def band_sums(b_offsets, sizes, place, offsets, b_own, b_peer):
+def band_sums(b_offsets, sizes, place, offsets, b_own, b_peer, pairwise):
     atoms, half, tile, _ = b_own.shape
     shape = lambda *dims: jax.ShapeDtypeStruct(dims + (tile,), jnp.bfloat16)
     row = shape(2 * WIDTH * tile + 16)
     return pl.pallas_call(
-        band_kernel,
+        functools.partial(band_kernel, pairwise),
         out_shape=(shape(2 * (atoms * WIDTH + 1) * tile), row, row),
         in_specs=[SMEM, SMEM, SMEM, VMEM, VMEM, VMEM],
         out_specs=(VMEM, VMEM, VMEM),
@@ -162,17 +165,21 @@
     )(b_offsets, sizes, place, offsets, b_own, b_peer)
 
 
-def join_kernel(table, tail, other_tail, head, other_head, out, sem):
+def join_kernel(pairwise, table, first, other_first, second, other_second, out, sem):
     layer = lax.axis_index("layer")
     tile = table.shape[-1]
     height = 2 * WIDTH * tile
     rows = table.shape[0] // height
+    at = 0, BAND + rows
+    if pairwise:
+        me = lax.axis_index("col")
+        at = [jnp.where(me == 0, at[1 - i], at[i]) for i in range(2)]
     parts = (
         (table, BAND, rows),
-        (tail, layer, 1),
-        (other_tail, 1 - layer, 1),
-        (head, BAND + rows + layer, 1),
-        (other_head, BAND + rows + 1 - layer, 1),
+        (first, at[0] + layer, 1),
+        (other_first, at[0] + 1 - layer, 1),
+        (second, at[1] + layer, 1),
+        (other_second, at[1] + 1 - layer, 1),
     )
     moves = [
         pltpu.make_async_copy(
@@ -187,17 +194,17 @@
         move.wait()
 
 
-def join(table, tail, head):
+def join(table, first, second, pairwise):
     more = 2 * BAND * 2 * WIDTH * table.shape[1]
     return pl.pallas_call(
-        join_kernel,
+        functools.partial(join_kernel, pairwise),
         out_shape=jax.ShapeDtypeStruct((table.shape[0] + more, table.shape[1]), table.dtype),
         in_specs=[ANY] * 5,
         out_specs=VMEM,
         scratch_shapes=[pltpu.SemaphoreType.DMA((5,))],
         name="join",
         **settings(12),
-    )(table, *tail, *head)
+    )(table, *first, *second)
 
 
 def plan_kernel(half, n_src, owner, sizes, place, c_offsets, *refs):
@@ -219,8 +226,7 @@
     else:
         mine = owner[0] == place[2]
         pl.when(mine)(lambda: load(pairs[0]))
-        pl.when(jnp.logical_not(mine) & (place[2] == 0))(lambda: load(pairs[1]))
-        pl.when(jnp.logical_not(mine) & (place[2] != 0))(lambda: load(pairs[2]))
+        pl.when(jnp.logical_not(mine))(lambda: load(pairs[1]))
     atoms = c_offsets.shape[0]
     slots = c_offsets.shape[1] // 2
     start, layer, me = place[0], place[1], place[2]
@@ -392,6 +398,10 @@
     def back(x):
         return lax.ppermute(x, ("row", "col"), [((i + 1) % cycle, i) for i in range(cycle)])
 
+    def diagonal(x):
+        there = [(i, (i + 1) % cycle) for i in range(1, cycle, 2)]
+        return lax.ppermute(x, ("row", "col"), there + [(j, i) for i, j in there])
+
     half, tile = a_tiles.shape[4:6]
     inner = tuple(range(1, atoms - BAND))
     outer = (0,) + tuple(range(atoms - BAND, atoms))
@@ -402,7 +412,7 @@
     if whole:
         all_rows = a_tiles.reshape(a_tiles.shape[:3] + (-1, tile))
         p0, count = inner[0] * half * tile, len(inner) * half * tile
-        cut_at = (count + tile) // 2
+        cut_at = (count - tile) // 2
 
         def part(at, n):
             rows = lax.dynamic_slice(all_rows, (0, 0, 1 - me, at, 0), (1, 1, 1, n, tile))
@@ -410,19 +420,21 @@
 
         sent = part(p0, cut_at), part(p0 + cut_at, count - cut_at)
         b_offsets = after(b_offsets, *sent)
-        b_peer = across(b_tiles)
+        b_peer = across(after(b_tiles, sent[1]))
         own_rows = lax.dynamic_slice_in_dim(b_offsets, start, atoms, 0)
         far = [swap(x) for x in sent]
-        table, tail, head = band_sums(own_rows, block_sizes, place, offsets, b_tiles, b_peer)
-        rest = cut(a_rows, outer, tail)
-        tail, head = onward(tail), back(head)
+        table, first, second = band_sums(
+            own_rows, block_sizes, place, offsets, b_tiles, b_peer, True
+        )
+        rest = cut(a_rows, outer, first)
+        first, second = swap(first), diagonal(second)
         rest = swap(rest)
         split = (len(inner) * half // 2 + 1) * tile
         far = choose(atom_owner, a_rows, offsets, [after(f, table) for f in far], inner, split)
         far = [(f, across(f)) for f in far]
-        tail, head = (tail, across(tail)), (head, across(head))
-        plan = make_plan(atom_owner, block_sizes, place, c_offsets, half, far[-1], head, tail)
-        table = join(table, tail, head)
+        first, second = (first, across(first)), (second, across(second))
+        plan = make_plan(atom_owner, block_sizes, place, c_offsets, half, far[-1], first)
+        table = join(table, first, second, True)
         c = products(plan, far, table, inner, **common)
         near = cut(a_rows, outer, own_rows, away=False)
         near = (near, across(near))
@@ -434,7 +446,7 @@
         return products(plan, [rest[1:]], near=near[1:], halves=(1,), **common)
     b_peer = across(b_tiles)
     own_rows = lax.dynamic_slice_in_dim(b_offsets, start, atoms, 0)
-    table, tail, head = band_sums(own_rows, block_sizes, place, offsets, b_tiles, b_peer)
+    table, tail, head = band_sums(own_rows, block_sizes, place, offsets, b_tiles, b_peer, False)
     tail, head = onward(tail), back(head)
     received = lax.all_to_all(a_tiles, "col", split_axis=2, concat_axis=1, tiled=True)
     moved = lax.all_to_all(a_offsets, "col", split_axis=2, concat_axis=1, tiled=True)
@@ -449,7 +461,7 @@
     rows = jnp.concatenate([rows, jnp.pad(shift, ((0, 16 - half), (0, tile - atoms)))], axis=0)
     other = across(rows)
     plan = make_plan(atom_owner, block_sizes, place, c_offsets, half, (rows, other))
-    table = join(table, (tail, across(tail)), (head, across(head)))
+    table = join(table, (tail, across(tail)), (head, across(head)), False)
     return products(plan, [(rows, other)], table, tuple(range(atoms)), **common)
 
 

time: 46 us -> 46 us (level)
  starting transfers between devices: 8.99 us -> 11.5 us
  waiting for transfers between devices: 16.9 us -> 14.4 us
    ppermute x2 -> x1, waiting for transfers between devices: 6.18 us -> 0.01 us  [diagonal(): return lax.ppermute(x, ('row', 'col'), there + [(j, i) for i, j in there])]
    ppermute x3 -> x4, waiting for transfers between devices: 9.9 us -> 13.6 us  [swap(): return lax.ppermute(x, 'col', [(0, 1), (1, 0)])]
    ppermute x3 -> x4, starting transfers between devices: 2.84 us -> 4.85 us  [swap(): return lax.ppermute(x, 'col', [(0, 1), (1, 0)])]
    ppermute x7, starting transfers between devices: 1.12 us -> 1.67 us  [across(): return lax.ppermute(x, 'layer', [(0, 1), (1, 0)])]
    ppermute x2 -> x1, starting transfers between devices: 5.03 us -> 4.99 us  [diagonal(): return lax.ppermute(x, ('row', 'col'), there + [(j, i) for i, j in there])]
    unnamed x16 -> x14, local copies, waits for them, and re-layouts: 2.78 us -> 2.78 us
  transfers between devices with their start and end apart: 12 -> 12, of which waited for: 6 -> 5; matrix products, arithmetic and copies ran while one was open for 6% -> 4% of each run, Pallas kernels for 26% -> 26%
where the time goes in v7:
time: 46 us; the launch traced here: 45.7 us
  waiting for transfers between devices  14.4 us (31%)
  Pallas kernels  14 us (30%)
  starting transfers between devices  11.5 us (25%)
  local copies, waits for them, and re-layouts  5.55 us (12%)
    ppermute x4, waiting for transfers between devices, swap(): return lax.ppermute(x, 'col', [(0, 1), (1, 0)])  13.6 us
    pallas_call x3, Pallas kernels, products(): pl.pallas_call(functools.partial(product_kernel, cfg), out_shape=out_shap...  6.01 us
    ppermute x1, starting transfers between devices, diagonal(): return lax.ppermute(x, ('row', 'col'), there + [(j, i) for i, j in there])  4.99 us
    ppermute x4, starting transfers between devices, swap(): return lax.ppermute(x, 'col', [(0, 1), (1, 0)])  4.85 us
    pallas_call x1, Pallas kernels, band_sums(): pl.pallas_call(functools.partial(band_kernel, pairwise), out_shape=(shape...  2.98 us
    unnamed x14, local copies, waits for them, and re-layouts  2.78 us
    pallas_call x1, Pallas kernels, make_plan(): pl.pallas_call(functools.partial(plan_kernel, half, len(pairs)), out_shap...  2.09 us
    reshape x2, local copies, waits for them, and re-layouts, part(): return rows.reshape(n, tile)  1.99 us
  transfers between devices with their start and end apart: 12, of which 5 were waited for; matrix products, arithmetic and copies ran while one was open for 4% of the time, Pallas kernels for 26%

profile of v7, /device:TPU:0, one launch (start us, length us, event | category | flops | bytes accessed | tf_op | source)
XLA Modules:
  0.0 45.7 jit_solution(5106291996568445651)
XLA Ops:
  0.0 1.0 %dynamic-slice_bitcast_fusion = bf16[1344,128]{1,0:T(8,128)(2,1)S(1)} fusion(bf16[1,1,2,4096,128]{4,3,2,1,0:T(8,128)(2,1)} %bitcast.10, s32[]{:T(128)S(6)} %select_n.7), kind=kLoop, calls=%fused_computation | loop fusion | bytes 688132 | tf_op jit(solution)/shard_map/reshape | solution.py:419
  1.0 0.0 copy-start
  1.0 0.5 %collective-permute-start.1 = (bf16[8,6,128,128]{3,2,1,0:T(8,128)(2,1)}, bf16[8,6,128,128]{3,2,1,0:T(8,128)(2,1)}, u32[]{:S(2)}, u32[]{:S(2)}) collective-permute-start(bf16[8,6,128,128]{3,2,1,0:T(8,128)(2,1)} %b_own.1), channel_id=1, source_target_pairs={{0,1},{1,0},{2,3},{3,2},{4,5},{5,4},{6,7},{7,6},{8,9},{9,8},{10,11... | collective-permute-start | bytes 4718600 | tf_op jit(solution)/shard_map/ppermute | solution.py:390
  1.5 2.6 %collective-permute-start.2 = (bf16[1344,128]{1,0:T(8,128)(2,1)S(1)}, bf16[1344,128]{1,0:T(8,128)(2,1)S(1)}, u32[]{:S(2)}, u32[]{:S(2)}) collective-permute-start(bf16[1344,128]{1,0:T(8,128)(2,1)S(1)} %dynamic-slice_bitcast_fusion), channel_id=1, source_target_pairs={{0,2},{2,0},{1,3},{3,1},{4,6},{6,4},{5,7},{7,5},{8,10},{10,8},{9,1... | collective-permute-start | bytes 1032200 | tf_op jit(solution)/shard_map/ppermute | solution.py:393
  4.1 1.0 %dynamic-slice_bitcast_fusion.1 = bf16[1216,128]{1,0:T(8,128)(2,1)S(1)} fusion(bf16[1,1,2,4096,128]{4,3,2,1,0:T(8,128)(2,1)} %bitcast.11, s32[]{:T(128)S(6)} %select_n.7), kind=kLoop, calls=%fused_computation.1 | loop fusion | bytes 622596 | tf_op jit(solution)/shard_map/reshape | solution.py:419
  5.1 0.2 collective-permute-start
  5.3 0.8 %copy.9 = s32[64,12]{1,0:T(8,128)S(1)} copy(s32[64,12]{0,1:T(8,128)} %param.11) | data formatting | bytes 6144 | tf_op jit(solution)/shard_map/optimization_barrier | solution.py:374
  6.1 0.1 pad_add_fusion.place
  6.2 1.4 %copy-done.1 = bf16[8,6,128,128]{3,2,1,0:T(8,128)(2,1)S(1)} copy-done((bf16[8,6,128,128]{3,2,1,0:T(8,128)(2,1)S(1)}, bf16[8,6,128,128]{3,2,1,0:T(8,128)(2,1)}, u32[]{:S(2)}) %copy-start.1) | copy-done | bytes 1572888
  7.6 0.7 %copy-done.2 = s32[1,1,2,8,4]{3,4,2,1,0:T(4,128)S(1)} copy-done((s32[1,1,2,8,4]{3,4,2,1,0:T(4,128)S(1)}, s32[1,1,2,8,4]{3,4,2,1,0:T(4,128)}, u32[]{:S(2)}) %copy-start.2) | copy-done | bytes 280
  8.3 0.7 %copy-done.5 = s32[64]{0:T(128)S(1)} copy-done((s32[64]{0:T(128)S(1)}, s32[64]{0:T(128)}, u32[]{:S(2)}) %copy-start.5) | copy-done | bytes 280
  8.9 3.0 %band_sums.1 = (bf16[10496,128]{1,0:T(8,128)(2,1)S(1)}, bf16[1296,128]{1,0:T(8,128)(2,1)S(1)}, bf16[1296,128]{1,0:T(8,128)(2,1)S(1)}) custom-call(s32[8,12]{1,0:T(8,128)S(1)} %constant_dynamic-slice_fusion.b_offsets.refs_0_, s32[64]{0:T(128)S(1)} %copy-done.5, s32[3]{0:T(128)S(1)} %pad_add_fusion.place, s32[1,1,2,4,8]{4,3,2,1,0:T(4,128)S(1)} %bitcast.15, ...), custom_call_target="tpu_custom_call" | custom-call | flops 1 | bytes 1 | tf_op jit(solution)/shard_map/band_sums/pallas_call | solution.py:157
  11.9 0.0 copy-start.4
  11.9 5.0 %collective-permute-start.9 = (bf16[1296,128]{1,0:T(8,128)(2,1)S(1)}, bf16[1296,128]{1,0:T(8,128)(2,1)S(1)}, u32[]{:S(2)}, u32[]{:S(2)}) collective-permute-start(bf16[1296,128]{1,0:T(8,128)(2,1)S(1)} %get-tuple-element.23), channel_id=1, source_target_pairs={{2,4},{6,8},{10,12},{14,0},{4,2},{8,6},{12,10},{0,14},{3,5},{7,9},... | collective-permute-start | bytes 995336 | tf_op jit(solution)/shard_map/ppermute | solution.py:403
  16.9 0.7 %cut.3 = bf16[1536,128]{1,0:T(8,128)(2,1)S(1)} custom-call(bf16[1,1,2,8,512,128]{5,4,3,2,1,0:T(8,128)(2,1)S(1)} %bitcast.12, bf16[1296,128]{1,0:T(8,128)(2,1)S(1)} %get-tuple-element.21.refs_0_), custom_call_target="tpu_custom_call" | custom-call | flops 1 | bytes 1 | tf_op jit(solution)/shard_map/cut/pallas_call | solution.py:46
  17.6 2.1 %collective-permute-start.7 = (bf16[1536,128]{1,0:T(8,128)(2,1)S(1)}, bf16[1536,128]{1,0:T(8,128)(2,1)S(1)}, u32[]{:S(2)}, u32[]{:S(2)}) collective-permute-start(bf16[1536,128]{1,0:T(8,128)(2,1)S(1)} %cut.3), channel_id=1, source_target_pairs={{0,2},{2,0},{1,3},{3,1},{4,6},{6,4},{5,7},{7,5},{8,10},{10,8},{9,1... | collective-permute-start | bytes 1179656 | tf_op jit(solution)/shard_map/ppermute | solution.py:393
  19.7 7.1 %collective-permute-done.far_first = bf16[1216,128]{1,0:T(8,128)(2,1)S(1)} collective-permute-done((bf16[1216,128]{1,0:T(8,128)(2,1)S(1)}, bf16[1216,128]{1,0:T(8,128)(2,1)S(1)}, u32[]{:S(2)}, u32[]{:S(2)}) %collective-permute-start) | collective-permute-done | bytes 311328 | tf_op jit(solution)/shard_map/ppermute | solution.py:393
  26.8 0.8 %choose.1 = (bf16[1408,128]{1,0:T(8,128)(2,1)S(1)}, bf16[1168,128]{1,0:T(8,128)(2,1)S(1)}) custom-call(s32[8]{0:T(128)S(1)} %copy-done.4, bf16[1,1,2,8,512,128]{5,4,3,2,1,0:T(8,128)(2,1)S(1)} %bitcast.13, s32[1,1,2,4,8]{4,3,2,1,0:T(4,128)S(1)} %bitcast.16, bf16[1216,128]{1,0:T(8,128)(2,1)S(1)} %collective-permute-done.far_first, ...), custom_call_target="tpu_custom_call" | custom-call | flops 1 | bytes 1 | tf_op jit(solution)/shard_map/choose/pallas_call | solution.py:100
  27.6 0.1 collective-permute-start.8
  27.7 0.5 %collective-permute-start.10 = (bf16[1296,128]{1,0:T(8,128)(2,1)S(1)}, bf16[1296,128]{1,0:T(8,128)(2,1)S(1)}, u32[]{:S(2)}, u32[]{:S(2)}) collective-permute-start(bf16[1296,128]{1,0:T(8,128)(2,1)S(1)} %collective-permute-done.9.second), channel_id=1, source_target_pairs={{0,1},{1,0},{2,3},{3,2},{4,5},{5,4},{6,7},{7,6},{8,9},{9,8},{10,11... | collective-permute-start | bytes 995336 | tf_op jit(solution)/shard_map/ppermute | solution.py:390
  28.2 5.7 %collective-permute-done.4.refs_2_.first = bf16[1296,128]{1,0:T(8,128)(2,1)S(1)} collective-permute-done((bf16[1296,128]{1,0:T(8,128)(2,1)S(1)}, bf16[1296,128]{1,0:T(8,128)(2,1)S(1)}, u32[]{:S(2)}, u32[]{:S(2)}) %collective-permute-start.4) | collective-permute-done | bytes 331808 | tf_op jit(solution)/shard_map/ppermute | solution.py:393
  33.9 0.5 %collective-permute-start.3 = (bf16[1168,128]{1,0:T(8,128)(2,1)S(1)}, bf16[1168,128]{1,0:T(8,128)(2,1)S(1)}, u32[]{:S(2)}, u32[]{:S(2)}) collective-permute-start(bf16[1168,128]{1,0:T(8,128)(2,1)S(1)} %get-tuple-element.20.refs_0_.refs_2_), channel_id=1, source_target_pairs={{0,1},{1,0},{2,3},{3,2},{4,5},{5,4},{6,7},{7,6},{8,9},{9,8},{10,11... | collective-permute-start | bytes 897032 | tf_op jit(solution)/shard_map/ppermute | solution.py:390
  34.4 0.7 %cut.2.refs_0_ = bf16[1536,128]{1,0:T(8,128)(2,1)S(1)} custom-call(bf16[1,1,2,8,512,128]{5,4,3,2,1,0:T(8,128)(2,1)S(1)} %bitcast.14, s32[8,12]{1,0:T(8,128)S(1)} %constant_dynamic-slice_fusion.b_offsets.refs_0_), custom_call_target="tpu_custom_call" | custom-call | flops 1 | bytes 1 | tf_op jit(solution)/shard_map/cut/pallas_call | solution.py:46
  35.2 0.1 collective-permute-start.6
  35.2 0.3 collective-permute-done.5.refs_3_.other_first
  35.5 0.6 %join.1.refs_4_.refs_2_ = bf16[15616,128]{1,0:T(8,128)(2,1)S(1)} custom-call(bf16[10496,128]{1,0:T(8,128)(2,1)S(1)} %get-tuple-element.17.table, bf16[1296,128]{1,0:T(8,128)(2,1)S(1)} %collective-permute-done.4.refs_2_.first, bf16[1296,128]{1,0:T(8,128)(2,1)S(1)} %collective-permute-done.5.refs_3_.other_first, ...), custom_call_target="tpu_custom_call" | custom-call | flops 1 | bytes 1 | tf_op jit(solution)/shard_map/join/pallas_call | solution.py:199
  36.2 2.1 %plan.1 = s32[8,128]{1,0:T(8,128)S(1)} custom-call(s32[8]{0:T(128)S(1)} %copy-done.4, s32[64]{0:T(128)S(1)} %copy-done.6, s32[3]{0:T(128)S(1)} %pad_add_fusion.place, s32[8,8]{1,0:T(8,128)S(1)} %copy-done.3, bf16[1168,128]{1,0:T(8,128)(2,1)S(1)} %get-tuple-element.20.refs_0_.refs_2_, bf16[1168,128]{1,0:T(8,128)(2,1)S(1)} %collective-permute-done.3.refs_1_.refs_3_, ...), custom_call_target="tpu_custom_call" | custom-call | flops 1 | bytes 1 | tf_op jit(solution)/shard_map/plan/pallas_call | solution.py:256
  38.3 2.9 %products.3.refs_4_ = bf16[8,4,128,128]{3,2,1,0:T(8,128)(2,1)} custom-call(s32[8,128]{1,0:T(8,128)S(1)} %plan.1, bf16[1408,128]{1,0:T(8,128)(2,1)S(1)} %get-tuple-element.22.refs_0_, bf16[1408,128]{1,0:T(8,128)(2,1)S(1)} %collective-permute-done.8.refs_1_, bf16[1168,128]{1,0:T(8,128)(2,1)S(1)} %get-tuple-element.20.refs_0_.refs_2_, ...), custom_call_target="tpu_custom_call" | custom-call | flops 1 | bytes 1 | tf_op jit(solution)/shard_map/products/pallas_call | solution.py:356
  41.2 0.8 %collective-permute-done.7.refs_1_ = bf16[1536,128]{1,0:T(8,128)(2,1)S(1)} collective-permute-done((bf16[1536,128]{1,0:T(8,128)(2,1)S(1)}, bf16[1536,128]{1,0:T(8,128)(2,1)S(1)}, u32[]{:S(2)}, u32[]{:S(2)}) %collective-permute-start.7) | collective-permute-done | bytes 393248 | tf_op jit(solution)/shard_map/ppermute | solution.py:393
  42.1 1.2 %products.4.refs_3_ = f32[3,2,128,256]{3,2,1,0:T(8,128)S(1)} custom-call(s32[8,128]{1,0:T(8,128)S(1)} %plan.1, bf16[1536,128]{1,0:T(8,128)(2,1)S(1)} %cut.2.refs_0_, bf16[1536,128]{1,0:T(8,128)(2,1)S(1)} %collective-permute-done.7.refs_1_, bf16[15616,128]{1,0:T(8,128)(2,1)S(1)} %join.1.refs_4_.refs_2_), custom_call_target="tpu_custom_call" | custom-call | flops 1 | bytes 1 | tf_op jit(solution)/shard_map/products/pallas_call | solution.py:356
  43.3 0.5 %collective-permute-done.11.refs_1_ = bf16[1536,128]{1,0:T(8,128)(2,1)S(1)} collective-permute-done((bf16[1536,128]{1,0:T(8,128)(2,1)S(1)}, bf16[1536,128]{1,0:T(8,128)(2,1)S(1)}, u32[]{:S(2)}, u32[]{:S(2)}) %collective-permute-start.11) | collective-permute-done | bytes 393248 | tf_op jit(solution)/shard_map/ppermute | solution.py:390
  43.8 1.9 %products.5 = bf16[8,4,128,128]{3,2,1,0:T(8,128)(2,1)} custom-call(s32[8,128]{1,0:T(8,128)S(1)} %plan.1, bf16[1536,128]{1,0:T(8,128)(2,1)S(1)} %collective-permute-done.6.refs_0_, bf16[1536,128]{1,0:T(8,128)(2,1)S(1)} %collective-permute-done.11.refs_1_, bf16[15616,128]{1,0:T(8,128)(2,1)S(1)} %join.1.refs_4_.refs_2_, ...), custom_call_target="tpu_custom_call", output_to_operand_aliasing={{}: (5, {})} | custom-call | flops 1 | bytes 1 | tf_op jit(solution)/shard_map/products/pallas_call | solution.py:356
  (20 shorter events, 0.0 us)
Async XLA Ops:
  1.0 15.9 %copy-start = (bf16[1,1,2,8,4,128,128]{6,5,4,3,2,1,0:T(8,128)(2,1)S(1)}, bf16[1,1,2,8,4,128,128]{6,5,4,3,2,1,0:T(8,128)(2,1)}, u32[]{:S(2)}) copy-start(bf16[1,1,2,8,4,128,128]{6,5,4,3,2,1,0:T(8,128)(2,1)} %param.7) | copy-start | bytes 6291460
  1.0 5.1 %collective-permute-start.1 = (bf16[8,6,128,128]{3,2,1,0:T(8,128)(2,1)}, bf16[8,6,128,128]{3,2,1,0:T(8,128)(2,1)}, u32[]{:S(2)}, u32[]{:S(2)}) collective-permute-start(bf16[8,6,128,128]{3,2,1,0:T(8,128)(2,1)} %b_own.1), channel_id=1, source_target_pairs={{0,1},{1,0},{2,3},{3,2},{4,5},{5,4},{6,7},{7,6},{8,9},{9,8},{10,11... | collective-permute-start | bytes 4718600 | tf_op jit(solution)/shard_map/ppermute | solution.py:390
  1.5 18.2 %collective-permute-start.2 = (bf16[1344,128]{1,0:T(8,128)(2,1)S(1)}, bf16[1344,128]{1,0:T(8,128)(2,1)S(1)}, u32[]{:S(2)}, u32[]{:S(2)}) collective-permute-start(bf16[1344,128]{1,0:T(8,128)(2,1)S(1)} %dynamic-slice_bitcast_fusion), channel_id=1, source_target_pairs={{0,2},{2,0},{1,3},{3,1},{4,6},{6,4},{5,7},{7,5},{8,10},{10,8},{9,1... | collective-permute-start | bytes 1032200 | tf_op jit(solution)/shard_map/ppermute | solution.py:393
  5.1 21.7 %collective-permute-start = (bf16[1216,128]{1,0:T(8,128)(2,1)S(1)}, bf16[1216,128]{1,0:T(8,128)(2,1)S(1)}, u32[]{:S(2)}, u32[]{:S(2)}) collective-permute-start(bf16[1216,128]{1,0:T(8,128)(2,1)S(1)} %dynamic-slice_bitcast_fusion.1), channel_id=1, source_target_pairs={{0,2},{2,0},{1,3},{3,1},{4,6},{6,4},{5,7},{7,5},{8,10},{10,8},{9,1... | collective-permute-start | bytes 933896 | tf_op jit(solution)/shard_map/ppermute | solution.py:393
  6.2 1.4 %copy-start.1 = (bf16[8,6,128,128]{3,2,1,0:T(8,128)(2,1)S(1)}, bf16[8,6,128,128]{3,2,1,0:T(8,128)(2,1)}, u32[]{:S(2)}) copy-start(bf16[8,6,128,128]{3,2,1,0:T(8,128)(2,1)} %b_own.1) | copy-start | bytes 4718596
  7.6 0.7 %copy-start.2 = (s32[1,1,2,8,4]{3,4,2,1,0:T(4,128)S(1)}, s32[1,1,2,8,4]{3,4,2,1,0:T(4,128)}, u32[]{:S(2)}) copy-start(s32[1,1,2,8,4]{3,4,2,1,0:T(4,128)} %param.8) | copy-start | bytes 772
  8.3 0.7 %copy-start.5 = (s32[64]{0:T(128)S(1)}, s32[64]{0:T(128)}, u32[]{:S(2)}) copy-start(s32[64]{0:T(128)} %sizes.3) | copy-start | bytes 772
  11.9 14.9 %copy-start.4 = (s32[8]{0:T(128)S(1)}, s32[8]{0:T(128)}, u32[]{:S(2)}) copy-start(s32[8]{0:T(128)} %owner.3) | copy-start | bytes 100
  11.9 15.8 %collective-permute-start.9 = (bf16[1296,128]{1,0:T(8,128)(2,1)S(1)}, bf16[1296,128]{1,0:T(8,128)(2,1)S(1)}, u32[]{:S(2)}, u32[]{:S(2)}) collective-permute-start(bf16[1296,128]{1,0:T(8,128)(2,1)S(1)} %get-tuple-element.23), channel_id=1, source_target_pairs={{2,4},{6,8},{10,12},{14,0},{4,2},{8,6},{12,10},{0,14},{3,5},{7,9},... | collective-permute-start | bytes 995336 | tf_op jit(solution)/shard_map/ppermute | solution.py:403
  16.9 17.0 %collective-permute-start.4 = (bf16[1296,128]{1,0:T(8,128)(2,1)S(1)}, bf16[1296,128]{1,0:T(8,128)(2,1)S(1)}, u32[]{:S(2)}, u32[]{:S(2)}) collective-permute-start(bf16[1296,128]{1,0:T(8,128)(2,1)S(1)} %get-tuple-element.21.refs_0_), channel_id=1, source_target_pairs={{0,2},{2,0},{1,3},{3,1},{4,6},{6,4},{5,7},{7,5},{8,10},{10,8},{9,1... | collective-permute-start | bytes 995336 | tf_op jit(solution)/shard_map/ppermute | solution.py:393
  17.6 24.4 %collective-permute-start.7 = (bf16[1536,128]{1,0:T(8,128)(2,1)S(1)}, bf16[1536,128]{1,0:T(8,128)(2,1)S(1)}, u32[]{:S(2)}, u32[]{:S(2)}) collective-permute-start(bf16[1536,128]{1,0:T(8,128)(2,1)S(1)} %cut.3), channel_id=1, source_target_pairs={{0,2},{2,0},{1,3},{3,1},{4,6},{6,4},{5,7},{7,5},{8,10},{10,8},{9,1... | collective-permute-start | bytes 1179656 | tf_op jit(solution)/shard_map/ppermute | solution.py:393
  27.6 10.7 %collective-permute-start.8 = (bf16[1408,128]{1,0:T(8,128)(2,1)S(1)}, bf16[1408,128]{1,0:T(8,128)(2,1)S(1)}, u32[]{:S(2)}, u32[]{:S(2)}) collective-permute-start(bf16[1408,128]{1,0:T(8,128)(2,1)S(1)} %get-tuple-element.22.refs_0_), channel_id=1, source_target_pairs={{0,1},{1,0},{2,3},{3,2},{4,5},{5,4},{6,7},{7,6},{8,9},{9,8},{10,11... | collective-permute-start | bytes 1081352 | tf_op jit(solution)/shard_map/ppermute | solution.py:390
  27.7 7.4 %collective-permute-start.10 = (bf16[1296,128]{1,0:T(8,128)(2,1)S(1)}, bf16[1296,128]{1,0:T(8,128)(2,1)S(1)}, u32[]{:S(2)}, u32[]{:S(2)}) collective-permute-start(bf16[1296,128]{1,0:T(8,128)(2,1)S(1)} %collective-permute-done.9.second), channel_id=1, source_target_pairs={{0,1},{1,0},{2,3},{3,2},{4,5},{5,4},{6,7},{7,6},{8,9},{9,8},{10,11... | collective-permute-start | bytes 995336 | tf_op jit(solution)/shard_map/ppermute | solution.py:390
  33.9 1.6 %collective-permute-start.5 = (bf16[1296,128]{1,0:T(8,128)(2,1)S(1)}, bf16[1296,128]{1,0:T(8,128)(2,1)S(1)}, u32[]{:S(2)}, u32[]{:S(2)}) collective-permute-start(bf16[1296,128]{1,0:T(8,128)(2,1)S(1)} %collective-permute-done.4.refs_2_.first), channel_id=1, source_target_pairs={{0,1},{1,0},{2,3},{3,2},{4,5},{5,4},{6,7},{7,6},{8,9},{9,8},{10,11... | collective-permute-start | bytes 995336 | tf_op jit(solution)/shard_map/ppermute | solution.py:390
  33.9 2.3 %collective-permute-start.3 = (bf16[1168,128]{1,0:T(8,128)(2,1)S(1)}, bf16[1168,128]{1,0:T(8,128)(2,1)S(1)}, u32[]{:S(2)}, u32[]{:S(2)}) collective-permute-start(bf16[1168,128]{1,0:T(8,128)(2,1)S(1)} %get-tuple-element.20.refs_0_.refs_2_), channel_id=1, source_target_pairs={{0,1},{1,0},{2,3},{3,2},{4,5},{5,4},{6,7},{7,6},{8,9},{9,8},{10,11... | collective-permute-start | bytes 897032 | tf_op jit(solution)/shard_map/ppermute | solution.py:390
  35.1 1.1 %copy-start.3 = (s32[8,8]{1,0:T(8,128)S(1)}, s32[8,8]{1,0:T(8,128)}, u32[]{:S(2)}) copy-start(s32[8,8]{1,0:T(8,128)} %c_offsets.1) | copy-start | bytes 772
  35.1 1.1 %copy-start.6 = (s32[64]{0:T(128)S(1)}, s32[64]{0:T(128)}, u32[]{:S(2)}) copy-start(s32[64]{0:T(128)} %sizes.3) | copy-start | bytes 772
  35.2 8.1 %collective-permute-start.6 = (bf16[1536,128]{1,0:T(8,128)(2,1)S(1)}, bf16[1536,128]{1,0:T(8,128)(2,1)S(1)}, u32[]{:S(2)}, u32[]{:S(2)}) collective-permute-start(bf16[1536,128]{1,0:T(8,128)(2,1)S(1)} %cut.2.refs_0_), channel_id=1, source_target_pairs={{0,1},{1,0},{2,3},{3,2},{4,5},{5,4},{6,7},{7,6},{8,9},{9,8},{10,11... | collective-permute-start | bytes 1179656 | tf_op jit(solution)/shard_map/ppermute | solution.py:390
  42.1 1.7 %collective-permute-start.11 = (bf16[1536,128]{1,0:T(8,128)(2,1)S(1)}, bf16[1536,128]{1,0:T(8,128)(2,1)S(1)}, u32[]{:S(2)}, u32[]{:S(2)}) collective-permute-start(bf16[1536,128]{1,0:T(8,128)(2,1)S(1)} %collective-permute-done.7.refs_1_), channel_id=1, source_target_pairs={{0,1},{1,0},{2,3},{3,2},{4,5},{5,4},{6,7},{7,6},{8,9},{9,8},{10,11... | collective-permute-start | bytes 1179656 | tf_op jit(solution)/shard_map/ppermute | solution.py:390
